TPU v7x, 256 devices: a whole 4x4x8 slice. The times are simulated.
256 devices in a mesh: feat: 32 (over z, y), node: 8 (over x, core).
Axes of the slice: x: 4, y: 4, z: 8, core: 2. Of those that a mesh axis runs over, the one named last changes fastest.
Arguments:
- features: bfloat16 [1280, 8, 24576], P('feat', 'node'), may hold values from -6 to 6
- first_neighbours: int32 [10, 8, 6144], P(None, 'node'), may hold values from 0 to 24575
- first_mask: int32 [10, 8, 6144], P(None, 'node'), may hold values 0 or 1
- second_neighbours: int32 [10, 8, 4096], P(None, 'node', 'feat'), may hold values from 0 to 6143, as said below
- second_mask: int32 [10, 8, 4096], P(None, 'node', 'feat'), may hold values 0 or 1
- target_index: int32 [8, 4096], P('node', 'feat'), may hold values from 0 to 6143
- labels: int32 [8, 4096], P('node', 'feat'), may hold values from 0 to 10239
- first_weight: bfloat16 [2, 1280, 256], P(None, 'feat'), may hold values from -0.15625 to 0.15625
- first_bias: float32 [256], replicated, may hold values from -3 to 3
- class_weight: bfloat16 [512, 10240], P(None, 'node'), may hold values from -2.5 to 2.5
Outputs:
- hidden: bfloat16 [8, 6144, 256], P('node', 'feat')
- loss: float32 [8, 4096], P('node', 'feat')
Inputs may be any that keep to these rules, and one draw needn't show every extreme that they name: In every group, the 128 targets of each aligned block of target positions name, through second_neighbours (masked slots included) and target_index together, exactly 24 distinct first-layer nodes among the 192 nodes o * 192 to (o + 1) * 192 - 1, for every o.
All inputs are finite; a program needn't handle non-finite values. No bound on the sum of `first_mask` or of `second_mask` on one device may be relied on, other than what follows from the above.
Results may differ from a plain program's by a relative error of at most 0.0027.
Values may be sent and summed in bfloat16 or wider, within the bound.
No kernel may reach another device: no remote copies, remote signals or barrier semaphores. Data moves between devices by JAX's collectives and lax.ppermute only.
A program may use at most 128 MiB of HBM per device.

v0:
```python
import jax
import jax.numpy as jnp
from jax import lax
from jax.sharding import PartitionSpec as P


def average_rows(table, lists, mask):
    total = jnp.zeros((lists.shape[1], table.shape[1]), jnp.float32)
    count = jnp.zeros((lists.shape[1],), jnp.float32)
    for slot in range(lists.shape[0]):
        weight = mask[slot].astype(jnp.float32)
        total = total + table[lists[slot]].astype(jnp.float32) * weight[:, None]
        count = count + weight
    return (total / jnp.maximum(count, 1.0)[:, None]).astype(jnp.bfloat16)


def project_rows(stacked, weights):
    return lax.dot_general(
        stacked, weights, (((0, 2), (0, 1)), ((), ())), preferred_element_type=jnp.float32
    )


def pick_label(logits, wanted):
    classes = lax.broadcasted_iota(jnp.int32, logits.shape, 1)
    return jnp.sum(jnp.where(classes == wanted[:, None], logits, 0.0), axis=1)


def body(
    features,
    first_neighbours,
    first_mask,
    second_neighbours,
    second_mask,
    target_index,
    labels,
    first_weight,
    first_bias,
    class_weight,
):
    row_major = features[:, 0, :].T
    first_rows = first_neighbours.shape[2]
    agg_one = average_rows(row_major, first_neighbours[:, 0, :], first_mask[:, 0, :])
    stacked = jnp.stack([row_major[:first_rows], agg_one])
    pre_one = lax.psum_scatter(
        project_rows(stacked, first_weight), "feat", scatter_dimension=0, tiled=True
    )
    hidden_own = jax.nn.relu(pre_one + first_bias[None, :]).astype(jnp.bfloat16)
    neighbour_lists = second_neighbours[:, 0, :]
    self_rows = target_index[0]
    row_table = lax.all_gather(hidden_own, "feat", axis=0, tiled=True)
    agg_two = average_rows(row_table, neighbour_lists, second_mask[:, 0, :])
    inputs = jnp.concatenate([row_table[self_rows], agg_two], axis=1)
    logits = jnp.dot(
        inputs,
        lax.all_gather(class_weight, "node", axis=1, tiled=True),
        preferred_element_type=jnp.float32,
    )
    largest = jnp.max(logits, axis=1)
    summed = jnp.sum(jnp.exp(logits - largest[:, None]), axis=1)
    picked = pick_label(logits, labels[0])
    loss_rows = largest + jnp.log(summed) - picked
    return (hidden_own[None], loss_rows[None])


def solution(mesh):
    placed = (
        P("feat", "node", None),
        P(None, "node", None),
        P(None, "node", None),
        P(None, "node", "feat"),
        P(None, "node", "feat"),
        P("node", "feat"),
        P("node", "feat"),
        P(None, "feat", None),
        P(),
        P(None, "node"),
    )
    return jax.shard_map(
        body,
        mesh=mesh,
        in_specs=placed,
        out_specs=(P("node", "feat", None), P("node", "feat")),
        check_vma=False,
    )
```

profile of v0, /device:TPU:1, one launch (start us, length us, event | category | flops | bytes accessed | tf_op | source)
XLA Modules:
  0.0 619.7 jit_solution(6292568670576730414)
XLA Ops:
  7.2 6.4 %copy.32 = bf16[24576,40]{1,0:T(8,128)(2,1)} copy(bf16[24576,40]{0,1:T(8,128)(2,1)} %bitcast.168) | data formatting | bytes 3932160 | tf_op jit(solution)/shard_map/transpose | solution.py:40
  15.0 20.1 %gather_fusion.9 = bf16[6144,40]{1,0:T(8,128)(2,1)S(1)} fusion(bf16[24576,40]{1,0:T(8,128)(2,1)} %copy.32, s32[6144]{0:T(1024)S(1)} %broadcast_clamp_fusion), kind=kCustom, calls=%fused_computation.9 | custom fusion | bytes 1007616 | tf_op jit(solution)/shard_map/gather | solution.py:12
  35.8 20.1 %gather_fusion.8 = bf16[6144,40]{1,0:T(8,128)(2,1)S(1)} fusion(bf16[24576,40]{1,0:T(8,128)(2,1)} %copy.32, s32[6144]{0:T(1024)S(1)} %broadcast_clamp_fusion.1), kind=kCustom, calls=%fused_computation.8 | custom fusion | bytes 1007616 | tf_op jit(solution)/shard_map/gather | solution.py:12
  56.5 20.1 %gather_fusion.7 = bf16[6144,40]{1,0:T(8,128)(2,1)S(1)} fusion(bf16[24576,40]{1,0:T(8,128)(2,1)} %copy.32, s32[6144]{0:T(1024)S(1)} %broadcast_clamp_fusion.2), kind=kCustom, calls=%fused_computation.7 | custom fusion | bytes 1007616 | tf_op jit(solution)/shard_map/gather | solution.py:12
  77.9 20.1 %gather_fusion.6 = bf16[6144,40]{1,0:T(8,128)(2,1)S(1)} fusion(bf16[24576,40]{1,0:T(8,128)(2,1)} %copy.32, s32[6144]{0:T(1024)S(1)} %broadcast_clamp_fusion.3), kind=kCustom, calls=%fused_computation.6 | custom fusion | bytes 1007616 | tf_op jit(solution)/shard_map/gather | solution.py:12
  99.4 20.1 %gather_fusion.5 = bf16[6144,40]{1,0:T(8,128)(2,1)S(1)} fusion(bf16[24576,40]{1,0:T(8,128)(2,1)} %copy.32, s32[6144]{0:T(1024)S(1)} %broadcast_clamp_fusion.4), kind=kCustom, calls=%fused_computation.5 | custom fusion | bytes 1007616 | tf_op jit(solution)/shard_map/gather | solution.py:12
  120.8 20.1 %gather_fusion.4 = bf16[6144,40]{1,0:T(8,128)(2,1)S(1)} fusion(bf16[24576,40]{1,0:T(8,128)(2,1)} %copy.32, s32[6144]{0:T(1024)S(1)} %broadcast_clamp_fusion.5), kind=kCustom, calls=%fused_computation.4 | custom fusion | bytes 1007616 | tf_op jit(solution)/shard_map/gather | solution.py:12
  140.8 1.4 copy.41
  142.2 20.1 %gather_fusion.3 = bf16[6144,40]{1,0:T(8,128)(2,1)S(1)} fusion(bf16[24576,40]{1,0:T(8,128)(2,1)} %copy.32, s32[6144]{0:T(1024)S(1)} %broadcast_clamp_fusion.6), kind=kCustom, calls=%fused_computation.3 | custom fusion | bytes 1007616 | tf_op jit(solution)/shard_map/gather | solution.py:12
  162.3 1.4 copy.39
  163.6 20.0 %gather_fusion.2 = bf16[6144,40]{1,0:T(8,128)(2,1)S(1)} fusion(bf16[24576,40]{1,0:T(8,128)(2,1)} %copy.32, s32[6144]{0:T(1024)S(1)} %broadcast_clamp_fusion.7), kind=kCustom, calls=%fused_computation.2 | custom fusion | bytes 1007616 | tf_op jit(solution)/shard_map/gather | solution.py:12
  185.0 20.1 %gather_fusion.1 = bf16[6144,40]{1,0:T(8,128)(2,1)S(1)} fusion(bf16[24576,40]{1,0:T(8,128)(2,1)} %copy.32, s32[6144]{0:T(1024)S(1)} %broadcast_clamp_fusion.8), kind=kCustom, calls=%fused_computation.1 | custom fusion | bytes 1007616 | tf_op jit(solution)/shard_map/gather | solution.py:12
  205.1 1.5 copy.35
  206.6 20.1 %gather_fusion = bf16[6144,40]{1,0:T(8,128)(2,1)S(1)} fusion(bf16[24576,40]{1,0:T(8,128)(2,1)} %copy.32, s32[6144]{0:T(1024)S(1)} %broadcast_clamp_fusion.9), kind=kCustom, calls=%fused_computation | custom fusion | bytes 1007616 | tf_op jit(solution)/shard_map/gather | solution.py:12
  228.3 3.2 fusion.5
  231.4 3.7 convolution_bitcast_fusion
  235.2 225.2 %reduce-scatter.2.cloned.1.call-done = f32[192,256]{1,0:T(8,128)} async-done(((f32[6144,256]{1,0:T(8,128)}), f32[192,256]{1,0:T(8,128)}) %reduce-scatter.2.cloned.1.call-update) | async-done | bytes 196624 | tf_op jit(solution)/shard_map/reduce_scatter | solution.py:44
  460.5 1.7 maximum_convert_fusion
  464.7 76.3 %all-gather.3.cloned.1.call-done = bf16[6144,256]{1,0:T(8,128)(2,1)} async-done(((bf16[192,256]{1,0:T(8,128)(2,1)}), bf16[6144,256]{1,0:T(8,128)(2,1)}) %all-gather.3.cloned.1.call-update) | async-done | bytes 3145744 | tf_op jit(solution)/shard_map/all_gather | solution.py:50
  541.1 3.2 gather_fusion.20
  544.3 3.1 gather_fusion.19
  547.3 3.1 gather_fusion.18
  550.4 3.1 gather_fusion.17
  553.4 3.8 gather_fusion.16
  557.2 4.3 gather_fusion.15
  561.5 1.5 gather_fusion.14
  562.9 1.5 gather_fusion.13
  564.4 1.5 gather_fusion.12
  565.9 1.5 gather_fusion.11
  569.6 35.5 %all-gather.5.cloned.1.call-done = bf16[512,10240]{1,0:T(8,128)(2,1)} async-done(((bf16[512,1280]{1,0:T(8,128)(2,1)}), bf16[512,10240]{1,0:T(8,128)(2,1)}) %all-gather.5.cloned.1.call-update) | async-done | bytes 10485776 | tf_op jit(solution)/shard_map/all_gather | solution.py:55
  605.1 5.7 fusion.31
  610.8 1.9 exponential_reduce_fusion
  (61 shorter events, 15.0 us)
Async XLA Ops:
  7.2 224.3 %copy-start = (bf16[2,40,256]{2,1,0:T(8,128)(2,1)S(1)}, bf16[2,40,256]{2,1,0:T(8,128)(2,1)}, u32[]{:S(2)}) copy-start(bf16[2,40,256]{2,1,0:T(8,128)(2,1)} %param.17) | copy-start | bytes 122884
  7.2 453.3 %reduce-scatter.2.cloned.1.call-start = ((), (), s32[]{:S(2)}) async-start(), calls=%async_computation.1 | async-start | bytes 6488064 | tf_op jit(solution)/shard_map/reduce_scatter | solution.py:44
  7.2 7.5 %copy-start.3 = (s32[10,1,6144]{2,1,0:T(1,128)S(1)}, s32[10,1,6144]{2,1,0:T(1,128)}, u32[]{:S(2)}) copy-start(s32[10,1,6144]{2,1,0:T(1,128)} %param.11) | copy-start | bytes 737284
  226.7 1.4 copy-start.4
  235.1 225.4 %copy-start.7 = (f32[256]{0:T(256)S(1)}, f32[256]{0:T(256)}, u32[]{:S(2)}) copy-start(f32[256]{0:T(256)} %param.18) | copy-start | bytes 3076
  235.2 227.7 %copy-start.9 = (s32[1,128]{1,0:T(1,128)S(1)}, s32[1,128]{1,0:T(1,128)}, u32[]{:S(2)}) copy-start(s32[1,128]{1,0:T(1,128)} %param.15) | copy-start | bytes 1540
  235.2 227.8 %copy-start.6 = (s32[10,1,128]{2,1,0:T(1,128)S(1)}, s32[10,1,128]{2,1,0:T(1,128)}, u32[]{:S(2)}) copy-start(s32[10,1,128]{2,1,0:T(1,128)} %param.13) | copy-start | bytes 15364
  235.2 227.9 %copy-start.5 = (s32[10,1,128]{2,1,0:T(1,128)S(1)}, s32[10,1,128]{2,1,0:T(1,128)}, u32[]{:S(2)}) copy-start(s32[10,1,128]{2,1,0:T(1,128)} %param.14) | copy-start | bytes 15364
  235.2 305.9 %all-gather.3.cloned.1.call-start = ((), (), s32[]{:S(2)}) async-start(), calls=%async_computation.2 | async-start | bytes 3244032 | tf_op jit(solution)/shard_map/all_gather | solution.py:50
  460.5 3.6 copy-start.2
  462.2 142.9 %all-gather.5.cloned.1.call-start = ((), (), s32[]{:S(2)}) async-start(), calls=%async_computation.3 | async-start | bytes 11796480 | tf_op jit(solution)/shard_map/all_gather | solution.py:55
  541.1 20.4 %copy-start.1 = (bf16[6144,256]{1,0:T(8,128)(2,1)S(1)}, bf16[6144,256]{1,0:T(8,128)(2,1)}, u32[]{:S(2)}) copy-start(bf16[6144,256]{1,0:T(8,128)(2,1)} %all-gather.3.cloned.1.call-done) | copy-start | bytes 9437188
  569.5 41.3 %copy-start.8 = (s32[1,128]{1,0:T(1,128)S(1)}, s32[1,128]{1,0:T(1,128)}, u32[]{:S(2)}) copy-start(s32[1,128]{1,0:T(1,128)} %param.16) | copy-start | bytes 1540
Sparse Core Ops, SparseCore 0:
  235.3 225.1 reduce-scatter.1
  463.4 77.6 all-gather.2
  543.0 62.0 all-gather.4
where the time goes:
time: 621 us; the launch traced here: 620 us
  waiting for transfers between devices  338 us (54%)
  local copies, waits for them, and re-layouts  247 us (40%)
  between operations  14.1 us (2%)
  other arithmetic  10.8 us (2%)
  matrix products  9.4 us (2%)
    gather x30, local copies, waits for them, and re-layouts, average_rows(): total = total + table[lists[slot]].astype(jnp.float32) * weight[:, None]  239 us
    reduce_scatter x1, waiting for transfers between devices, body(): lax.psum_scatter(project_rows(stacked, first_weight), 'feat', scatter_dim...  225 us
    all_gather x1, waiting for transfers between devices, body(): row_table = lax.all_gather(hidden_own, 'feat', axis=0, tiled=True)  76.3 us
    all_gather x1, waiting for transfers between devices, body(): lax.all_gather(class_weight, 'node', axis=1, tiled=True)  35.5 us
  transfers between devices with their start and end apart: 3, of which 3 were waited for; matrix products, arithmetic and copies ran while one was open for 5% of the time, Pallas kernels for 0%

commit v1 on v0

v1 whole, which is shorter than its diff:
```python
import functools

import jax
import jax.numpy as jnp
from jax import lax
from jax.experimental import pallas as pl
from jax.experimental.pallas import tpu as pltpu
from jax.sharding import PartitionSpec as P

FEAT = 32
NODE = 8
WIDTH = 40
INPUTS = 24576
ROWS = 6144
OWN = 192
FAN = 10
TARGETS = 128
HIDDEN = 256
UNION = 24
SLAB = 256
UNROLL = 16
TABLE_STEP = 8
F32 = jnp.float32
BF16 = jnp.bfloat16


def iota(shape, dim):
    return lax.broadcasted_iota(jnp.int32, shape, dim)


def contract(a, b, dim_a, dim_b):
    return lax.dot_general(a, b, (((dim_a,), (dim_b,)), ((), ())), preferred_element_type=F32)


def earlier(size):
    return jnp.where(iota((size, size), 0) < iota((size, size), 1), 1.0, 0.0).astype(BF16)


def add_all(terms):
    while len(terms) > 1:
        paired = [terms[k] + terms[k + 1] for k in range(0, len(terms) - 1, 2)]
        terms = paired + terms[len(terms) - len(terms) % 2 :]
    return terms[0]


def gather_kernel(slots, features, second, send, place, table, sums, flags):
    def fill(step, carry):
        for part in range(TABLE_STEP):
            at = pl.multiple_of((step * TABLE_STEP + part) * 128, 128)
            block = jnp.concatenate(
                [features[:, pl.ds(at, 128)].astype(F32), jnp.ones((8, 128), F32)], axis=0
            )
            table[pl.ds(at, 128), pl.ds(0, WIDTH + 8)] = block.T
        return carry

    lax.fori_loop(0, INPUTS // 128 // TABLE_STEP, fill, 0)
    table[pl.ds(INPUTS, 8), :] = jnp.zeros((8, 128), F32)

    owners, lanes = [], []
    named = jnp.zeros((FEAT, SLAB), F32)
    for slot in range(FAN + 1):
        index = second[pl.ds(slot, 1), :]
        owner = ((index.astype(F32) + 0.5) * (1.0 / OWN)).astype(jnp.int32)
        row = index - owner * OWN
        owner_hot = jnp.where(iota((FEAT, TARGETS), 0) == owner, 1.0, 0.0).astype(BF16)
        row_hot = jnp.where(iota((SLAB, TARGETS), 0) == row, 1.0, 0.0)
        named = named + contract(owner_hot, row_hot.astype(BF16), 1, 1)
        owners.append((owner, owner_hot))
        lanes.append(row_hot)
    marked = jnp.where(named > 0.0, 1.0, 0.0)
    flags[...] = marked
    rank = contract(marked.astype(BF16), earlier(SLAB), 1, 0).astype(BF16)
    places = []
    for slot in range(FAN + 1):
        owner, owner_hot = owners[slot]
        mine = jnp.sum(contract(rank, owner_hot, 0, 0) * lanes[slot], axis=0, keepdims=True)
        places.append(owner * UNION + mine.astype(jnp.int32))
    place[...] = jnp.concatenate(places + [jnp.zeros((5, TARGETS), jnp.int32)], axis=0)

    def owner_step(owner, carry):
        first = pl.multiple_of(owner * OWN, 64)

        def block(step, inner):
            at = first + step * UNROLL
            lists = [slots.at[pl.ds(slot * ROWS + at, UNROLL)] for slot in range(FAN)]
            result = sums.at[pl.ds(pl.multiple_of(step * UNROLL, UNROLL), UNROLL), :]
            for row in range(UNROLL):
                result[pl.ds(row, 1), :] = add_all(
                    [table[pl.ds(lists[slot][row], 1), :] for slot in range(FAN)]
                )
            return inner

        lax.fori_loop(0, OWN // UNROLL, block, 0)
        own = table[pl.ds(first, 128), :].T
        head = sums[pl.ds(0, 128), :].T
        tail = jnp.concatenate(
            [table[pl.ds(first + 128, 64), :], sums[pl.ds(128, 64), :]], axis=0
        ).T
        marks = flags[pl.ds(owner, 1), :]
        send[owner] = jnp.concatenate(
            [
                own[:WIDTH],
                head[:WIDTH] / jnp.maximum(head[WIDTH : WIDTH + 1], 1.0),
                tail[:WIDTH] / jnp.maximum(tail[WIDTH : WIDTH + 1], 1.0),
                marks[:, :128],
                marks[:, 128:],
                jnp.zeros((6, 128), F32),
            ],
            axis=0,
        ).astype(BF16)
        return carry

    lax.fori_loop(0, FEAT, owner_step, 0)


def hidden_kernel(got, weights, bias, hidden, rows, head, tail, tail_weights, marks, chosen):
    for source in range(FEAT):
        block = got[source].astype(F32)
        head[pl.ds(source * 80, 80), :] = block[:80].astype(BF16)
        tail[pl.ds(source * 40, 40), :] = block[80:120].astype(BF16)
        marks[pl.ds(source, 1), pl.ds(0, 128)] = block[120:121]
        marks[pl.ds(source, 1), pl.ds(128, 128)] = block[121:122]
        pair = weights[pl.ds(source * 80, 80), :].astype(F32)
        tail_weights[pl.ds(source * 40, 40), pl.ds(0, HIDDEN)] = pair[:40].astype(BF16)
        tail_weights[pl.ds(source * 40, 40), pl.ds(HIDDEN, HIDDEN)] = pair[40:].astype(BF16)
    most = contract(head[...], weights[...], 0, 0)
    rest = contract(tail[...], tail_weights[...], 0, 0)
    rest = rest[:64, :HIDDEN] + rest[64:, HIDDEN:]
    pre = jnp.concatenate([most, rest], axis=0) + bias[...]
    result = jnp.maximum(pre, 0.0).astype(BF16)
    hidden[...] = result
    rank = contract(marks[...].astype(BF16), earlier(SLAB), 1, 0)
    for source in range(FEAT):
        hit = (iota((UNION, SLAB), 0).astype(F32) == rank[source : source + 1]) & (
            marks[pl.ds(source, 1), :] > 0.0
        )
        chosen[pl.ds(source * UNION, UNION), :] = jnp.where(hit, 1.0, 0.0)
    padded = jnp.concatenate([result, jnp.zeros((SLAB - OWN, HIDDEN), BF16)], axis=0)
    rows[...] = contract(chosen[...].astype(BF16), padded, 1, 0).astype(BF16)


def loss_kernel(rows, place, mask, labels, weights, loss, inputs, largest, summed, picked):
    step = pl.program_id(0)
    width = weights.shape[2]

    @pl.when(step == 0)
    def _():
        spots = iota((FEAT * UNION, TARGETS), 0)
        total = jnp.zeros((FEAT * UNION, TARGETS), F32)
        for slot in range(FAN):
            used = mask[pl.ds(slot, 1), :].astype(F32)
            total = total + jnp.where(spots == place[pl.ds(slot, 1), :], used, 0.0)
        total = total.astype(BF16)
        self_hot = jnp.where(spots == place[pl.ds(FAN, 1), :], 1.0, 0.0).astype(BF16)
        count = contract(total, jnp.ones((FEAT * UNION, 128), BF16), 0, 0)[:, :1]
        agg = contract(total, rows[...], 0, 0) / jnp.maximum(count, 1.0)
        inputs[:, pl.ds(0, HIDDEN)] = contract(self_hot, rows[...], 0, 0).astype(BF16)
        inputs[:, pl.ds(HIDDEN, HIDDEN)] = agg.astype(BF16)
        largest[...] = jnp.full((TARGETS, 1), -jnp.inf, F32)
        summed[...] = jnp.zeros((TARGETS, 1), F32)
        picked[...] = jnp.zeros((TARGETS, 1), F32)

    logits = contract(inputs[...], weights[0], 1, 0)
    before = largest[...]
    now = jnp.maximum(before, jnp.max(logits, axis=1, keepdims=True))
    part = jnp.sum(jnp.exp(logits - now), axis=1, keepdims=True)
    summed[...] = summed[...] * jnp.exp(before - now) + part
    largest[...] = now
    classes = iota((TARGETS, width), 1) + step * width
    picked[...] += jnp.sum(jnp.where(classes == labels[...], logits, 0.0), axis=1, keepdims=True)

    @pl.when(step == NODE - 1)
    def _():
        loss[...] = largest[...] + jnp.log(summed[...]) - picked[...]


VMEM = pl.BlockSpec(memory_space=pltpu.VMEM)
SMEM = pl.BlockSpec(memory_space=pltpu.SMEM)


def body(
    features,
    first_neighbours,
    first_mask,
    second_neighbours,
    second_mask,
    target_index,
    labels,
    first_weight,
    first_bias,
    class_weight,
):
    slots = jnp.where(first_mask[:, 0, :] > 0, first_neighbours[:, 0, :], INPUTS).reshape(-1)
    second = jnp.concatenate(
        [second_neighbours[:, 0, :], target_index, jnp.zeros((5, TARGETS), jnp.int32)], axis=0
    )
    all_first = lax.all_gather(first_weight, "feat", axis=0).reshape(FEAT * 2 * WIDTH, HIDDEN)
    all_class = lax.all_gather(class_weight, "node", axis=0)
    send, place = pl.pallas_call(
        gather_kernel,
        out_shape=(
            jax.ShapeDtypeStruct((FEAT, 128, 128), BF16),
            jax.ShapeDtypeStruct((16, TARGETS), jnp.int32),
        ),
        in_specs=[SMEM, VMEM, VMEM],
        out_specs=(VMEM, VMEM),
        scratch_shapes=[
            pltpu.VMEM((INPUTS + 8, 128), F32),
            pltpu.VMEM((OWN, 128), F32),
            pltpu.VMEM((FEAT, SLAB), F32),
        ],
        compiler_params=pltpu.CompilerParams(vmem_limit_bytes=40 * 2**20),
        cost_estimate=pl.CostEstimate(flops=10**9, bytes_accessed=150 * 10**6, transcendentals=0),
    )(slots, features[:, 0, :], second)
    got = lax.all_to_all(send, "feat", 0, 0)
    hidden, rows = pl.pallas_call(
        hidden_kernel,
        out_shape=(
            jax.ShapeDtypeStruct((OWN, HIDDEN), BF16),
            jax.ShapeDtypeStruct((FEAT * UNION, HIDDEN), BF16),
        ),
        in_specs=[VMEM] * 3,
        out_specs=(VMEM, VMEM),
        scratch_shapes=[
            pltpu.VMEM((FEAT * 80, 128), BF16),
            pltpu.VMEM((FEAT * 40, 128), BF16),
            pltpu.VMEM((FEAT * 40, 2 * HIDDEN), BF16),
            pltpu.VMEM((FEAT, SLAB), F32),
            pltpu.VMEM((FEAT * UNION, SLAB), F32),
        ],
        compiler_params=pltpu.CompilerParams(vmem_limit_bytes=40 * 2**20),
    )(got, all_first, first_bias[None, :])
    rows = lax.all_to_all(rows.reshape(FEAT, UNION, HIDDEN), "feat", 0, 0)
    rows = rows.reshape(FEAT * UNION, HIDDEN)
    width = class_weight.shape[1]
    whole = lambda *shape: pl.BlockSpec(shape, lambda i: (0,) * len(shape))
    loss = pl.pallas_call(
        loss_kernel,
        grid=(NODE,),
        out_shape=jax.ShapeDtypeStruct((TARGETS, 1), F32),
        in_specs=[
            whole(FEAT * UNION, HIDDEN),
            whole(16, TARGETS),
            whole(FAN, TARGETS),
            whole(TARGETS, 1),
            pl.BlockSpec((1, 2 * HIDDEN, width), lambda i: (i, 0, 0)),
        ],
        out_specs=whole(TARGETS, 1),
        scratch_shapes=[
            pltpu.VMEM((TARGETS, 2 * HIDDEN), BF16),
            pltpu.VMEM((TARGETS, 1), F32),
            pltpu.VMEM((TARGETS, 1), F32),
            pltpu.VMEM((TARGETS, 1), F32),
        ],
        compiler_params=pltpu.CompilerParams(vmem_limit_bytes=40 * 2**20),
    )(rows, place, second_mask[:, 0, :], labels.reshape(TARGETS, 1), all_class)
    return (hidden[None], loss.reshape(1, TARGETS))


def solution(mesh):
    placed = (
        P("feat", "node", None),
        P(None, "node", None),
        P(None, "node", None),
        P(None, "node", "feat"),
        P(None, "node", "feat"),
        P("node", "feat"),
        P("node", "feat"),
        P(None, "feat", None),
        P(),
        P(None, "node"),
    )
    return jax.shard_map(
        body,
        mesh=mesh,
        in_specs=placed,
        out_specs=(P("node", "feat", None), P("node", "feat")),
        check_vma=False,
    )
```

time: 621 us -> 175 us (0.28)
  waiting for transfers between devices: 338 us -> 42.4 us
  local copies, waits for them, and re-layouts: 247 us -> 6.35 us
  Pallas kernels: 0 us -> 61.7 us
  blocking collectives: 0 us -> 41.4 us
  matrix products: 9.4 us -> 0 us
  other arithmetic: 10.8 us -> 2.79 us
    gather x31 -> x0, local copies, waits for them, and re-layouts: 240 us -> none  [the longest x30 239 us: average_rows(): total = total + table[lists[slot]].astype(jnp.float32) * weight[:, None]]
    reduce_scatter x1 -> x0, waiting for transfers between devices: 225 us -> none  [body(): lax.psum_scatter(project_rows(stacked, first_weight), 'feat', scatter_dim...]
    all_gather x2, waiting for transfers between devices: 112 us -> 27.3 us  [the longest x1 27.3 us: body(): all_class = lax.all_gather(class_weight, 'node', axis=0)]
    pallas_call x0 -> x3, Pallas kernels: none -> 61.7 us  [the longest x1 53.1 us: body(): pl.pallas_call(gather_kernel, out_shape=(jax.ShapeDtypeStruct((FEAT, 128,...]
    all_to_all x0 -> x1, blocking collectives: none -> 41.4 us  [body(): got = lax.all_to_all(send, 'feat', 0, 0)]
    all_to_all x0 -> x1, waiting for transfers between devices: none -> 13.8 us  [body(): rows = lax.all_to_all(rows.reshape(FEAT, UNION, HIDDEN), 'feat', 0, 0)]
    dot_general x2 -> x0, matrix products: 9.4 us -> none  [the longest x1 5.73 us: body(): jnp.dot(inputs, lax.all_gather(class_weight, 'node', axis=1, tiled=True),...]
    convert_element_type x5 -> x0, other arithmetic: 6.87 us -> none  [the longest x2 4.53 us: average_rows(): return (total / jnp.maximum(count, 1.0)[:, None]).astype(jnp.bfloat16)]
  transfers between devices with their start and end apart: 3 -> 3, of which waited for: 3 -> 2; matrix products, arithmetic and copies ran while one was open for 5% -> 2% of each run, Pallas kernels for 0% -> 31%
where the time goes in v1:
time: 175 us; the launch traced here: 174 us
  Pallas kernels  61.7 us (35%)
  waiting for transfers between devices  42.4 us (24%)
  blocking collectives  41.4 us (24%)
  between operations  14.1 us (8%)
  local copies, waits for them, and re-layouts  6.35 us (4%)
  starting transfers between devices  5.64 us (3%)
  other arithmetic  2.79 us (2%)
    pallas_call x1, Pallas kernels, body(): pl.pallas_call(gather_kernel, out_shape=(jax.ShapeDtypeStruct((FEAT, 128,...  53.1 us
    all_to_all x1, blocking collectives, body(): got = lax.all_to_all(send, 'feat', 0, 0)  41.4 us
    all_gather x1, waiting for transfers between devices, body(): all_class = lax.all_gather(class_weight, 'node', axis=0)  27.3 us
    all_to_all x1, waiting for transfers between devices, body(): rows = lax.all_to_all(rows.reshape(FEAT, UNION, HIDDEN), 'feat', 0, 0)  13.8 us
    pallas_call x1, Pallas kernels, body(): pl.pallas_call(loss_kernel, grid=(NODE,), out_shape=jax.ShapeDtypeStruct(...  6.85 us
    unnamed x14, local copies, waits for them, and re-layouts  6.16 us
    all_to_all x1, starting transfers between devices, body(): rows = lax.all_to_all(rows.reshape(FEAT, UNION, HIDDEN), 'feat', 0, 0)  5.56 us
  transfers between devices with their start and end apart: 3, of which 2 were waited for; matrix products, arithmetic and copies ran while one was open for 2% of the time, Pallas kernels for 31%

profile of v1, /device:TPU:1, one launch (start us, length us, event | category | flops | bytes accessed | tf_op | source)
XLA Modules:
  0.0 174.4 jit_solution(12138314102601083364)
XLA Ops:
  7.2 0.0 copy-start.3
  7.2 0.0 all-gather.5.cloned.1.call-start
  7.2 0.7 all-gather.5.cloned.1.call-update
  7.9 0.0 all-gather.7.cloned.1.call-start
  8.0 0.7 all-gather.7.cloned.1.call-update
  8.7 0.7 copy.20
  9.4 0.1 pad.2.clone
  9.4 0.7 add_add_fusion.second
  10.2 1.4 compare_select_fusion
  11.6 0.0 copy-done.3
  11.6 53.1 %shard_map.113 = (bf16[32,128,128]{2,1,0:T(8,128)(2,1)S(1)}, s32[16,128]{1,0:T(8,128)S(1)}) custom-call(s32[61440]{0:T(1024)S(1)} %bitcast.19, bf16[40,24576]{1,0:T(8,128)(2,1)S(1)} %bitcast.22, s32[16,128]{1,0:T(8,128)S(1)} %add_add_fusion.second), custom_call_target="tpu_custom_call" | custom-call | flops 1000000000 | bytes 150000000 | tf_op jit(solution)/shard_map/pallas_call | solution.py:199
  64.7 0.0 copy-start.2
  64.7 0.0 copy-start.4
  64.7 41.4 %all_to_all.10.got = bf16[32,128,128]{2,1,0:T(8,128)(2,1)S(1)} all-to-all(bf16[32,128,128]{2,1,0:T(8,128)(2,1)S(1)} %get-tuple-element.6), channel_id=1, replica_groups=mesh['feat'=32,'node'=8] {'feat'}, dimensions={0} | all-to-all | bytes 2097152 | tf_op jit(solution)/shard_map/all_to_all | solution.py:215
  106.1 0.0 copy-start.5
  106.1 0.0 all-gather.5.cloned.1.call-done
  106.1 0.0 copy-done.2
  106.1 0.0 copy-start.1
  106.1 1.5 copy-done.1
  107.6 1.8 %shard_map.114 = (bf16[192,256]{1,0:T(8,128)(2,1)}, bf16[768,256]{1,0:T(8,128)(2,1)}) custom-call(bf16[32,128,128]{2,1,0:T(8,128)(2,1)S(1)} %all_to_all.10.got, bf16[2560,256]{1,0:T(8,128)(2,1)S(1)} %bitcast.18, f32[1,256]{1,0:T(1,128)S(1)} %bitcast.21), custom_call_target="tpu_custom_call" | custom-call | tf_op jit(solution)/shard_map/pallas_call | solution.py:216
  109.3 5.6 %all-to-all-start.1 = ((bf16[32,24,256]{2,1,0:T(8,128)(2,1)}), bf16[32,24,256]{2,1,0:T(8,128)(2,1)S(1)}, u32[]{:S(2)}, u32[]{:S(2)}) async-start(bf16[32,24,256]{2,1,0:T(8,128)(2,1)} %bitcast.5), calls=%async_computation.1 | async-start | bytes 786432 | tf_op jit(solution)/shard_map/all_to_all | solution.py:233
  114.9 0.0 copy-done.4
  114.9 0.0 copy-done.5
  114.9 0.1 copy.14.labels
  115.0 13.8 %all-to-all-done.1 = bf16[32,24,256]{2,1,0:T(8,128)(2,1)S(1)} async-done(((bf16[32,24,256]{2,1,0:T(8,128)(2,1)}), bf16[32,24,256]{2,1,0:T(8,128)(2,1)S(1)}, u32[]{:S(2)}, u32[]{:S(2)}) %all-to-all-start.1) | async-done | bytes 393248 | tf_op jit(solution)/shard_map/all_to_all | solution.py:233
  128.8 27.3 %all-gather.7.cloned.1.call-done = bf16[4096,1280]{1,0:T(8,128)(2,1)} async-done(((bf16[512,1280]{1,0:T(8,128)(2,1)}), bf16[4096,1280]{1,0:T(8,128)(2,1)}) %all-gather.7.cloned.1.call-update) | async-done | bytes 10485776 | tf_op jit(solution)/shard_map/all_gather | solution.py:198
  156.1 0.0 copy-start
  156.1 4.0 %copy-done = bf16[4096,1280]{1,0:T(8,128)(2,1)S(1)} copy-done((bf16[4096,1280]{1,0:T(8,128)(2,1)S(1)}, bf16[4096,1280]{1,0:T(8,128)(2,1)}, u32[]{:S(2)}) %copy-start) | copy-done | bytes 10485784
  160.1 6.8 %shard_map.115 = f32[128,1]{1,0:T(8,128)S(1)} custom-call(bf16[768,256]{1,0:T(8,128)(2,1)S(1)} %bitcast.17, s32[16,128]{1,0:T(8,128)S(1)} %get-tuple-element.9.place, s32[10,128]{1,0:T(8,128)S(1)} %bitcast.20, s32[128,1]{1,0:T(8,128)S(1)} %copy.14.labels, bf16[8,512,1280]{2,1,0:T(8,128)(2,1)S(1)} %bitcast.16), custom_call_target="tpu_custom_call" | custom-call | tf_op jit(solution)/shard_map/pallas_call | solution.py:237
  167.0 0.6 reduce
  (2 shorter events, 0.0 us)
Async XLA Ops:
  7.2 4.4 %copy-start.3 = (bf16[40,1,24576]{2,0,1:T(8,128)(2,1)S(1)}, bf16[40,1,24576]{2,0,1:T(8,128)(2,1)}, u32[]{:S(2)}) copy-start(bf16[40,1,24576]{2,0,1:T(8,128)(2,1)} %param.10) | copy-start | bytes 5898244
  7.2 98.9 %all-gather.5.cloned.1.call-start = ((), (), s32[]{:S(2)}) async-start(), calls=%async_computation.2 | async-start | bytes 1351680 | tf_op jit(solution)/shard_map/all_gather | solution.py:197
  7.9 148.2 %all-gather.7.cloned.1.call-start = ((), (), s32[]{:S(2)}) async-start(), calls=%async_computation.3 | async-start | bytes 11796480 | tf_op jit(solution)/shard_map/all_gather | solution.py:198
  64.7 41.4 %copy-start.2 = (f32[256]{0:T(256)S(1)}, f32[256]{0:T(256)}, u32[]{:S(2)}) copy-start(f32[256]{0:T(256)} %param.18) | copy-start | bytes 3076
  64.7 50.2 %copy-start.4 = (s32[10,1,128]{2,1,0:T(1,128)S(1)}, s32[10,1,128]{2,1,0:T(1,128)}, u32[]{:S(2)}) copy-start(s32[10,1,128]{2,1,0:T(1,128)} %param.14) | copy-start | bytes 15364
  106.1 8.8 %copy-start.5 = (s32[1,128]{1,0:T(1,128)S(1)}, s32[1,128]{1,0:T(1,128)}, u32[]{:S(2)}) copy-start(s32[1,128]{1,0:T(1,128)} %param.16) | copy-start | bytes 1540
  106.1 1.5 copy-start.1
  109.3 19.5 %all-to-all-start.1 = ((bf16[32,24,256]{2,1,0:T(8,128)(2,1)}), bf16[32,24,256]{2,1,0:T(8,128)(2,1)S(1)}, u32[]{:S(2)}, u32[]{:S(2)}) async-start(bf16[32,24,256]{2,1,0:T(8,128)(2,1)} %bitcast.5), calls=%async_computation.1 | async-start | bytes 786432 | tf_op jit(solution)/shard_map/all_to_all | solution.py:233
  156.1 4.0 %copy-start = (bf16[4096,1280]{1,0:T(8,128)(2,1)S(1)}, bf16[4096,1280]{1,0:T(8,128)(2,1)}, u32[]{:S(2)}) copy-start(bf16[4096,1280]{1,0:T(8,128)(2,1)} %all-gather.7.cloned.1.call-done) | copy-start | bytes 31457284
Sparse Core Ops, SparseCore 0:
  10.6 78.8 all-gather.4
  91.3 64.7 all-gather.6

commit v2 on v1

v2 whole, which is shorter than its diff:
```python
import functools

import jax
import jax.numpy as jnp
from jax import lax
from jax.experimental import pallas as pl
from jax.experimental.pallas import tpu as pltpu
from jax.sharding import PartitionSpec as P

FEAT = 32
NODE = 8
WIDTH = 40
INPUTS = 24576
ROWS = 6144
OWN = 192
FAN = 10
TARGETS = 128
HIDDEN = 256
UNION = 24
SLAB = 256
UNROLL = 16
TABLE_STEP = 8
F32 = jnp.float32
BF16 = jnp.bfloat16


def iota(shape, dim):
    return lax.broadcasted_iota(jnp.int32, shape, dim)


def contract(a, b, dim_a, dim_b):
    return lax.dot_general(a, b, (((dim_a,), (dim_b,)), ((), ())), preferred_element_type=F32)


def earlier(size):
    return jnp.where(iota((size, size), 0) < iota((size, size), 1), 1.0, 0.0).astype(BF16)


def add_all(terms):
    while len(terms) > 1:
        paired = [terms[k] + terms[k + 1] for k in range(0, len(terms) - 1, 2)]
        terms = paired + terms[len(terms) - len(terms) % 2 :]
    return terms[0]


def send_kernel(features, weights, neighbours, targets, send, place):
    owners, lanes = [], []
    named = jnp.zeros((FEAT, SLAB), F32)
    for slot in range(FAN + 1):
        index = neighbours[slot] if slot < FAN else targets[...]
        owner = ((index.astype(F32) + 0.5) * (1.0 / OWN)).astype(jnp.int32)
        row = index - owner * OWN
        owner_hot = jnp.where(iota((FEAT, TARGETS), 0) == owner, 1.0, 0.0).astype(BF16)
        row_hot = jnp.where(iota((SLAB, TARGETS), 0) == row, 1.0, 0.0)
        named = named + contract(owner_hot, row_hot.astype(BF16), 1, 1)
        owners.append((owner, owner_hot))
        lanes.append(row_hot)
    marked = jnp.where(named > 0.0, 1.0, 0.0)
    rank = contract(marked.astype(BF16), earlier(SLAB), 1, 0).astype(BF16)
    places = []
    for slot in range(FAN + 1):
        owner, owner_hot = owners[slot]
        mine = jnp.sum(contract(rank, owner_hot, 0, 0) * lanes[slot], axis=0, keepdims=True)
        places.append(owner * UNION + mine.astype(jnp.int32))
    place[...] = jnp.concatenate(places + [jnp.zeros((5, TARGETS), jnp.int32)], axis=0)

    shared = weights[...].astype(F32)
    for pair in range(FEAT // 2):
        block = features[:, pl.ds(pair * 2 * OWN, 2 * OWN)].astype(F32)
        for half in range(2):
            owner = 2 * pair + half
            own = block[:, half * OWN : (half + 1) * OWN]
            marks = marked[owner : owner + 1]
            last = jnp.concatenate(
                [
                    own[24:, 128:],
                    marks[:, :64],
                    marks[:, 64:128],
                    marks[:, 128:192],
                    jnp.zeros((5, 64), F32),
                ],
                axis=0,
            )
            send[owner] = jnp.concatenate(
                [shared, own[:, :128], jnp.concatenate([own[:24, 128:], last], axis=1)], axis=0
            ).astype(BF16)


def gather_kernel(slots, features, send, table, sums):
    def fill(step, carry):
        for part in range(TABLE_STEP):
            at = pl.multiple_of((step * TABLE_STEP + part) * 128, 128)
            block = jnp.concatenate(
                [features[:, pl.ds(at, 128)].astype(F32), jnp.ones((8, 128), F32)], axis=0
            )
            table[pl.ds(at, 128), pl.ds(0, WIDTH + 8)] = block.T
        return carry

    lax.fori_loop(0, INPUTS // 128 // TABLE_STEP, fill, 0)
    table[pl.ds(INPUTS, 8), :] = jnp.zeros((8, 128), F32)

    def owner_step(owner, carry):
        first = owner * OWN

        def block(step, inner):
            at = first + step * UNROLL
            lists = [slots.at[pl.ds(slot * ROWS + at, UNROLL)] for slot in range(FAN)]
            result = sums.at[pl.ds(pl.multiple_of(step * UNROLL, UNROLL), UNROLL), :]
            for row in range(UNROLL):
                result[pl.ds(row, 1), :] = add_all(
                    [table[pl.ds(lists[slot][row], 1), :] for slot in range(FAN)]
                )
            return inner

        lax.fori_loop(0, OWN // UNROLL, block, 0)
        head = sums[pl.ds(0, 128), :].T
        tail = sums[pl.ds(128, 64), :].T
        head = head[:WIDTH] / jnp.maximum(head[WIDTH : WIDTH + 1], 1.0)
        tail = tail[:WIDTH] / jnp.maximum(tail[WIDTH : WIDTH + 1], 1.0)
        last = jnp.concatenate([tail[24:], jnp.zeros((8, 64), F32)], axis=0)
        send[owner] = jnp.concatenate(
            [head, jnp.concatenate([tail[:24], last], axis=1)], axis=0
        ).astype(BF16)
        return carry

    lax.fori_loop(0, FEAT, owner_step, 0)


def hidden_kernel(
    core, mine, theirs, means, bias, hidden, rows, stacked, held, other, marks, chosen
):
    for source in range(FEAT):
        own = mine[source].astype(F32)
        mean = means[source].astype(F32)
        held[pl.ds(source * 80, 80), :] = own[:80].astype(BF16)
        other[pl.ds(source * 80, 80), :] = theirs[source].astype(F32).astype(BF16)
        last, mean_last = own[120:144], mean[40:64]
        stacked[pl.ds(source * 80, 80), pl.ds(0, 128)] = jnp.concatenate(
            [own[80:120], mean[:40]], axis=0
        ).astype(BF16)
        stacked[pl.ds(source * 80, 80), pl.ds(128, 64)] = jnp.concatenate(
            [last[:, :64], last[:16, 64:], mean_last[:, :64], mean_last[:16, 64:]], axis=0
        ).astype(BF16)
        marks[pl.ds(source, 1), :] = jnp.concatenate(
            [last[16:17, 64:], last[17:18, 64:], last[18:19, 64:], jnp.zeros((1, 64), F32)], axis=1
        )
    stacked[:, pl.ds(192, 64)] = jnp.zeros((FEAT * 80, 64), BF16)
    first = contract(stacked[...], held[...], 0, 0)[:OWN]
    second = contract(stacked[...], other[...], 0, 0)[:OWN]
    even = core[0] == 0
    pre = jnp.concatenate(
        [jnp.where(even, first, second), jnp.where(even, second, first)], axis=1
    )
    result = jnp.maximum(pre + bias[...], 0.0).astype(BF16)
    hidden[...] = result
    rank = contract(marks[...].astype(BF16), earlier(SLAB), 1, 0)
    for source in range(FEAT):
        hit = (iota((UNION, SLAB), 0).astype(F32) == rank[source : source + 1]) & (
            marks[pl.ds(source, 1), :] > 0.0
        )
        chosen[pl.ds(source * UNION, UNION), :] = jnp.where(hit, 1.0, 0.0)
    padded = jnp.concatenate([result, jnp.zeros((SLAB - OWN, HIDDEN), BF16)], axis=0)
    rows[...] = contract(chosen[...].astype(BF16), padded, 1, 0).astype(BF16)


def pick_kernel(place, mask, picks):
    spots = iota((FEAT * UNION, TARGETS), 0)
    total = jnp.zeros((FEAT * UNION, TARGETS), F32)
    for slot in range(FAN):
        used = mask[slot].astype(F32)
        total = total + jnp.where(spots == place[pl.ds(slot, 1), :], used, 0.0)
    picks[0] = total.astype(BF16)
    picks[1] = jnp.where(spots == place[pl.ds(FAN, 1), :], 1.0, 0.0).astype(BF16)


def loss_kernel(rows, picks, labels, weights, loss, inputs, wanted, largest, summed, picked):
    step = pl.program_id(0)
    width = weights.shape[2]

    @pl.when(step == 0)
    def _():
        count = contract(picks[0], jnp.ones((FEAT * UNION, 128), BF16), 0, 0)[:, :1]
        agg = contract(picks[0], rows[...], 0, 0) / jnp.maximum(count, 1.0)
        inputs[:, pl.ds(0, HIDDEN)] = contract(picks[1], rows[...], 0, 0).astype(BF16)
        inputs[:, pl.ds(HIDDEN, HIDDEN)] = agg.astype(BF16)
        spread = jnp.broadcast_to(labels[...].astype(F32), (TARGETS, TARGETS)).T
        wanted[...] = spread[:, :1].astype(jnp.int32)
        largest[...] = jnp.full((TARGETS, 1), -jnp.inf, F32)
        summed[...] = jnp.zeros((TARGETS, 1), F32)
        picked[...] = jnp.zeros((TARGETS, 1), F32)

    logits = contract(inputs[...], weights[0], 1, 0)
    before = largest[...]
    now = jnp.maximum(before, jnp.max(logits, axis=1, keepdims=True))
    part = jnp.sum(jnp.exp(logits - now), axis=1, keepdims=True)
    summed[...] = summed[...] * jnp.exp(before - now) + part
    largest[...] = now
    classes = iota((TARGETS, width), 1) + step * width
    picked[...] += jnp.sum(jnp.where(classes == wanted[...], logits, 0.0), axis=1, keepdims=True)

    @pl.when(step == NODE - 1)
    def _():
        column = largest[...] + jnp.log(summed[...]) - picked[...]
        loss[...] = jnp.broadcast_to(column, (TARGETS, TARGETS)).T[:1]


VMEM = pl.BlockSpec(memory_space=pltpu.VMEM)
SMEM = pl.BlockSpec(memory_space=pltpu.SMEM)


def body(
    features,
    first_neighbours,
    first_mask,
    second_neighbours,
    second_mask,
    target_index,
    labels,
    first_weight,
    first_bias,
    class_weight,
):
    slots = jnp.where(first_mask[:, 0, :] > 0, first_neighbours[:, 0, :], INPUTS).reshape(-1)
    core = lax.rem(lax.axis_index("node"), 2).astype(jnp.int32)
    half = lax.dynamic_slice(first_weight, (0, 0, core * 128), (2, WIDTH, 128))
    all_class = lax.all_gather(class_weight, "node", axis=0)
    table = features[:, 0, :]
    own, place = pl.pallas_call(
        send_kernel,
        out_shape=(
            jax.ShapeDtypeStruct((FEAT, 144, 128), BF16),
            jax.ShapeDtypeStruct((16, TARGETS), jnp.int32),
        ),
        grid=(1,),
        in_specs=[
            pl.BlockSpec((WIDTH, ROWS), lambda i: (0, 0)),
            pl.BlockSpec((2 * WIDTH, 128), lambda i: (0, 0)),
            pl.BlockSpec((FAN, 1, TARGETS), lambda i: (0, 0, 0)),
            pl.BlockSpec((1, TARGETS), lambda i: (0, 0)),
        ],
        out_specs=(
            pl.BlockSpec((FEAT, 144, 128), lambda i: (0, 0, 0)),
            pl.BlockSpec((16, TARGETS), lambda i: (0, 0)),
        ),
        compiler_params=pltpu.CompilerParams(vmem_limit_bytes=24 * 2**20),
        cost_estimate=pl.CostEstimate(flops=10**8, bytes_accessed=3 * 10**6, transcendentals=0),
    )(table, half.reshape(2 * WIDTH, 128), second_neighbours, target_index)
    own = lax.all_to_all(own, "feat", 0, 0)
    send = pl.pallas_call(
        gather_kernel,
        out_shape=jax.ShapeDtypeStruct((FEAT, 64, 128), BF16),
        in_specs=[SMEM, VMEM],
        out_specs=VMEM,
        scratch_shapes=[
            pltpu.VMEM((INPUTS + 8, 128), F32),
            pltpu.VMEM((OWN, 128), F32),
        ],
        compiler_params=pltpu.CompilerParams(vmem_limit_bytes=24 * 2**20),
        cost_estimate=pl.CostEstimate(flops=10**9, bytes_accessed=150 * 10**6, transcendentals=0),
    )(slots, table)
    swap = [(device, device ^ 1) for device in range(NODE)]
    theirs = lax.ppermute(own[:, : 2 * WIDTH], "node", swap)
    means = lax.all_to_all(send, "feat", 0, 0)
    hidden, rows = pl.pallas_call(
        hidden_kernel,
        out_shape=(
            jax.ShapeDtypeStruct((OWN, HIDDEN), BF16),
            jax.ShapeDtypeStruct((FEAT * UNION, HIDDEN), BF16),
        ),
        in_specs=[SMEM] + [VMEM] * 4,
        out_specs=(VMEM, VMEM),
        scratch_shapes=[
            pltpu.VMEM((FEAT * 80, 256), BF16),
            pltpu.VMEM((FEAT * 80, 128), BF16),
            pltpu.VMEM((FEAT * 80, 128), BF16),
            pltpu.VMEM((FEAT, SLAB), F32),
            pltpu.VMEM((FEAT * UNION, SLAB), F32),
        ],
        compiler_params=pltpu.CompilerParams(vmem_limit_bytes=24 * 2**20),
    )(core[None], own, theirs, means, first_bias[None, :])
    rows = lax.all_to_all(rows.reshape(FEAT, UNION, HIDDEN), "feat", 0, 0)
    rows = rows.reshape(FEAT * UNION, HIDDEN)
    picks = pl.pallas_call(
        pick_kernel,
        out_shape=jax.ShapeDtypeStruct((2, FEAT * UNION, TARGETS), BF16),
        in_specs=[VMEM] * 2,
        out_specs=VMEM,
        cost_estimate=pl.CostEstimate(flops=10**7, bytes_accessed=4 * 10**6, transcendentals=0),
    )(place, second_mask)
    width = class_weight.shape[1]
    whole = lambda *shape: pl.BlockSpec(shape, lambda i: (0,) * len(shape))
    loss = pl.pallas_call(
        loss_kernel,
        grid=(NODE,),
        out_shape=jax.ShapeDtypeStruct((1, TARGETS), F32),
        in_specs=[
            whole(FEAT * UNION, HIDDEN),
            whole(2, FEAT * UNION, TARGETS),
            whole(1, TARGETS),
            pl.BlockSpec((1, 2 * HIDDEN, width), lambda i: (i, 0, 0)),
        ],
        out_specs=whole(1, TARGETS),
        scratch_shapes=[
            pltpu.VMEM((TARGETS, 2 * HIDDEN), BF16),
            pltpu.VMEM((TARGETS, 1), jnp.int32),
            pltpu.VMEM((TARGETS, 1), F32),
            pltpu.VMEM((TARGETS, 1), F32),
            pltpu.VMEM((TARGETS, 1), F32),
        ],
        compiler_params=pltpu.CompilerParams(vmem_limit_bytes=24 * 2**20),
    )(rows, picks, labels, all_class)
    return (hidden[None], loss)


def solution(mesh):
    placed = (
        P("feat", "node", None),
        P(None, "node", None),
        P(None, "node", None),
        P(None, "node", "feat"),
        P(None, "node", "feat"),
        P("node", "feat"),
        P("node", "feat"),
        P(None, "feat", None),
        P(),
        P(None, "node"),
    )
    return jax.shard_map(
        body,
        mesh=mesh,
        in_specs=placed,
        out_specs=(P("node", "feat", None), P("node", "feat")),
        check_vma=False,
    )
```

time: 175 us -> 149 us (0.85); the launches traced: 174 us -> 147 us
  blocking collectives: 41.4 us -> 0 us
  starting transfers between devices: 5.64 us -> 29.2 us
  waiting for transfers between devices: 42.4 us -> 25.4 us
  Pallas kernels: 61.7 us -> 67.2 us
  local copies, waits for them, and re-layouts: 6.35 us -> 9.06 us
    all_to_all x1 -> x0, blocking collectives: 41.4 us -> none  [body(): got = lax.all_to_all(send, 'feat', 0, 0)]
    all_gather x1, waiting for transfers between devices: 27.3 us -> 0.01 us  [body(): all_class = lax.all_gather(class_weight, 'node', axis=0)]
    all_to_all x0 -> x2, starting transfers between devices: none -> 21.5 us  [the longest x1 12.2 us: body(): own = lax.all_to_all(own, 'feat', 0, 0)]
    all_to_all x0 -> x2, waiting for transfers between devices: none -> 13.7 us  [the longest x1 13.7 us: body(): means = lax.all_to_all(send, 'feat', 0, 0)]
    pallas_call x1 -> x3, Pallas kernels: 53.1 us -> 57.7 us  [the longest x1 54.4 us: body(): pl.pallas_call(gather_kernel, out_shape=jax.ShapeDtypeStruct((FEAT, 64, 1...]
    unnamed x14 -> x26, local copies, waits for them, and re-layouts: 6.16 us -> 9 us
    all_to_all x1, waiting for transfers between devices: 13.8 us -> 11 us  [body(): rows = lax.all_to_all(rows.reshape(FEAT, UNION, HIDDEN), 'feat', 0, 0)]
  transfers between devices with their start and end apart: 3 -> 5, of which waited for: 2 -> 2; matrix products, arithmetic and copies ran while one was open for 2% -> 1% of each run, Pallas kernels for 31% -> 41%
where the time goes in v2:
time: 149 us; the launch traced here: 147 us
  Pallas kernels  67.2 us (45%)
  starting transfers between devices  29.2 us (20%)
  waiting for transfers between devices  25.4 us (17%)
  between operations  14.2 us (10%)
  local copies, waits for them, and re-layouts  9.06 us (6%)
  other arithmetic  1.49 us (1%)
    pallas_call x1, Pallas kernels, body(): pl.pallas_call(gather_kernel, out_shape=jax.ShapeDtypeStruct((FEAT, 64, 1...  54.4 us
    all_to_all x1, waiting for transfers between devices, body(): means = lax.all_to_all(send, 'feat', 0, 0)  13.7 us
    all_to_all x1, starting transfers between devices, body(): own = lax.all_to_all(own, 'feat', 0, 0)  12.2 us
    all_to_all x1, waiting for transfers between devices, body(): rows = lax.all_to_all(rows.reshape(FEAT, UNION, HIDDEN), 'feat', 0, 0)  11 us
    all_to_all x1, starting transfers between devices, body(): means = lax.all_to_all(send, 'feat', 0, 0)  9.35 us
    unnamed x26, local copies, waits for them, and re-layouts  9 us
    pallas_call x1, Pallas kernels, body(): pl.pallas_call(loss_kernel, grid=(NODE,), out_shape=jax.ShapeDtypeStruct(...  7.15 us
    all_to_all x1, starting transfers between devices, body(): rows = lax.all_to_all(rows.reshape(FEAT, UNION, HIDDEN), 'feat', 0, 0)  6.08 us
  transfers between devices with their start and end apart: 5, of which 2 were waited for; matrix products, arithmetic and copies ran while one was open for 1% of the time, Pallas kernels for 41%

profile of v2, /device:TPU:1, one launch (start us, length us, event | category | flops | bytes accessed | tf_op | source)
XLA Modules:
  0.0 146.6 jit_solution(4899703119077007631)
XLA Ops:
  7.2 0.0 copy-start
  7.2 0.0 copy-start.8
  7.2 0.0 copy-start.11
  7.2 0.0 all-gather.3.cloned.1.call-start
  7.2 0.7 all-gather.3.cloned.1.call-update
  7.9 0.0 copy-done
  8.0 0.0 copy-done.8
  8.0 0.0 copy-done.11
  8.0 0.0 copy-start.2
  8.0 1.5 %copy-done.2 = bf16[40,1,24576]{2,0,1:T(8,128)(2,1)S(1)} copy-done((bf16[40,1,24576]{2,0,1:T(8,128)(2,1)S(1)}, bf16[40,1,24576]{2,0,1:T(8,128)(2,1)}, u32[]{:S(2)}) %copy-start.2) | copy-done | bytes 1966104
  9.5 1.4 shard_map.113
  10.9 0.0 copy-start.5
  11.0 1.0 copy-done.5
  12.0 0.6 copy-done.7
  12.6 12.2 %all-to-all-start = ((bf16[32,144,128]{2,1,0:T(8,128)(2,1)}), bf16[32,144,128]{2,1,0:T(8,128)(2,1)S(1)}, u32[]{:S(2)}, u32[]{:S(2)}) async-start(bf16[32,144,128]{2,1,0:T(8,128)(2,1)} %copy-done.5), calls=%async_computation | async-start | bytes 2359296 | tf_op jit(solution)/shard_map/all_to_all | solution.py:248
  24.8 1.5 %compare_select_fusion = s32[10,1,6144]{2,1,0:T(1,128)S(1)} fusion(s32[10,1,6144]{2,1,0:T(1,128)S(1)} %copy-done.12, s32[10,1,6144]{2,1,0:T(1,128)} %param.12), kind=kLoop, calls=%fused_computation | loop fusion | flops 122880 | bytes 737280 | tf_op jit(solution)/shard_map/jit(_where)/select_n | solution.py:223
  26.2 0.0 copy-done.3
  26.3 54.4 %shard_map.114 = bf16[32,64,128]{2,1,0:T(8,128)(2,1)S(1)} custom-call(s32[61440]{0:T(1024)S(1)} %bitcast.13, bf16[40,24576]{1,0:T(8,128)(2,1)S(1)} %bitcast.11), custom_call_target="tpu_custom_call" | custom-call | flops 1000000000 | bytes 150000000 | tf_op jit(solution)/shard_map/pallas_call | solution.py:249
  80.7 0.0 copy-start.6
  80.7 0.8 copy-done.6
  81.5 0.0 all-to-all-done.mine
  81.5 9.3 %all-to-all-start.1 = ((bf16[32,64,128]{2,1,0:T(8,128)(2,1)}), bf16[32,64,128]{2,1,0:T(8,128)(2,1)S(1)}, u32[]{:S(2)}, u32[]{:S(2)}) async-start(bf16[32,64,128]{2,1,0:T(8,128)(2,1)} %copy-done.6), calls=%async_computation.1 | async-start | bytes 1048576 | tf_op jit(solution)/shard_map/all_to_all | solution.py:263
  90.9 1.6 %collective-permute-start = (bf16[32,80,128]{2,1,0:T(8,128)(2,1)S(1)}, bf16[32,80,128]{2,1,0:T(8,128)(2,1)S(1)}, u32[]{:S(2)}, u32[]{:S(2)}) collective-permute-start(bf16[32,80,128]{2,1,0:T(8,128)(2,1)S(1)} %slice.4), channel_id=1, source_target_pairs={{0,1},{1,0},{2,3},{3,2},{4,5},{5,4},{6,7},{7,6},{8,9},{9,8},{10,11... | collective-permute-start | bytes 1966088 | tf_op jit(solution)/shard_map/ppermute | solution.py:262
  92.5 13.7 %all-to-all-done.1.means = bf16[32,64,128]{2,1,0:T(8,128)(2,1)S(1)} async-done(((bf16[32,64,128]{2,1,0:T(8,128)(2,1)}), bf16[32,64,128]{2,1,0:T(8,128)(2,1)S(1)}, u32[]{:S(2)}, u32[]{:S(2)}) %all-to-all-start.1) | async-done | bytes 524320 | tf_op jit(solution)/shard_map/all_to_all | solution.py:263
  106.3 0.0 collective-permute-done.theirs
  106.3 2.3 %shard_map.115 = (bf16[192,256]{1,0:T(8,128)(2,1)}, bf16[768,256]{1,0:T(8,128)(2,1)}) custom-call(s32[1]{0:T(128)} %bitcast.core, bf16[32,144,128]{2,1,0:T(8,128)(2,1)S(1)} %all-to-all-done.mine, bf16[32,80,128]{2,1,0:T(8,128)(2,1)S(1)} %collective-permute-done.theirs, bf16[32,64,128]{2,1,0:T(8,128)(2,1)S(1)} %all-to-all-done.1.means, f32[1,256]{1,0:T(1,128)S(1)} %bitcast.15), custom_call_target="tpu_custom_call" | custom-call | tf_op jit(solution)/shard_map/pallas_call | solution.py:264
  108.6 6.1 %all-to-all-start.2 = ((bf16[32,24,256]{2,1,0:T(8,128)(2,1)}), bf16[32,24,256]{2,1,0:T(8,128)(2,1)S(1)}, u32[]{:S(2)}, u32[]{:S(2)}) async-start(bf16[32,24,256]{2,1,0:T(8,128)(2,1)} %bitcast.6), calls=%async_computation.2 | async-start | bytes 786432 | tf_op jit(solution)/shard_map/all_to_all | solution.py:281
  114.7 1.9 %shard_map.116.picks = bf16[2,768,128]{2,1,0:T(8,128)(2,1)} custom-call(s32[16,128]{1,0:T(8,128)} %copy-done.7, s32[10,1,128]{2,1,0:T(1,128)} %mask.1), custom_call_target="tpu_custom_call" | custom-call | flops 10000000 | bytes 4000000 | tf_op jit(solution)/shard_map/pallas_call | solution.py:283
  116.6 11.0 %all-to-all-done.2 = bf16[32,24,256]{2,1,0:T(8,128)(2,1)S(1)} async-done(((bf16[32,24,256]{2,1,0:T(8,128)(2,1)}), bf16[32,24,256]{2,1,0:T(8,128)(2,1)S(1)}, u32[]{:S(2)}, u32[]{:S(2)}) %all-to-all-start.2) | async-done | bytes 393248 | tf_op jit(solution)/shard_map/all_to_all | solution.py:281
  127.6 4.0 %copy-done.1 = bf16[4096,1280]{1,0:T(8,128)(2,1)S(1)} copy-done((bf16[4096,1280]{1,0:T(8,128)(2,1)S(1)}, bf16[4096,1280]{1,0:T(8,128)(2,1)}, u32[]{:S(2)}) %copy-start.1) | copy-done | bytes 10485784
  131.6 1.0 copy-done.4
  132.6 7.2 %shard_map.117 = f32[1,128]{1,0:T(1,128)} custom-call(bf16[768,256]{1,0:T(8,128)(2,1)S(1)} %bitcast.12, bf16[2,768,128]{2,1,0:T(8,128)(2,1)S(1)} %copy-done.4, s32[1,128]{1,0:T(1,128)S(1)} %copy-done.10, bf16[8,512,1280]{2,1,0:T(8,128)(2,1)S(1)} %bitcast.9), custom_call_target="tpu_custom_call" | custom-call | tf_op jit(solution)/shard_map/pallas_call | solution.py:292
  (13 shorter events, 0.1 us)
Async XLA Ops:
  7.2 0.8 copy-start
  7.2 0.8 copy-start.8
  7.2 0.8 copy-start.11
  7.2 120.4 %all-gather.3.cloned.1.call-start = ((), (), s32[]{:S(2)}) async-start(), calls=%async_computation.3 | async-start | bytes 11796480 | tf_op jit(solution)/shard_map/all_gather | solution.py:226
  8.0 1.5 %copy-start.2 = (bf16[40,1,24576]{2,0,1:T(8,128)(2,1)S(1)}, bf16[40,1,24576]{2,0,1:T(8,128)(2,1)}, u32[]{:S(2)}) copy-start(bf16[40,1,24576]{2,0,1:T(8,128)(2,1)} %param.10) | copy-start | bytes 5898244
  10.9 1.0 copy-start.5
  12.0 0.6 copy-start.7
  12.6 12.2 %copy-start.12 = (s32[10,1,6144]{2,1,0:T(1,128)S(1)}, s32[10,1,6144]{2,1,0:T(1,128)}, u32[]{:S(2)}) copy-start(s32[10,1,6144]{2,1,0:T(1,128)} %param.11) | copy-start | bytes 737284
  12.6 13.7 %copy-start.3 = (bf16[40,1,24576]{2,0,1:T(8,128)(2,1)S(1)}, bf16[40,1,24576]{2,0,1:T(8,128)(2,1)}, u32[]{:S(2)}) copy-start(bf16[40,1,24576]{2,0,1:T(8,128)(2,1)} %param.10) | copy-start | bytes 5898244
  12.6 69.0 %all-to-all-start = ((bf16[32,144,128]{2,1,0:T(8,128)(2,1)}), bf16[32,144,128]{2,1,0:T(8,128)(2,1)S(1)}, u32[]{:S(2)}, u32[]{:S(2)}) async-start(bf16[32,144,128]{2,1,0:T(8,128)(2,1)} %copy-done.5), calls=%async_computation | async-start | bytes 2359296 | tf_op jit(solution)/shard_map/all_to_all | solution.py:248
  80.7 0.8 copy-start.6
  81.5 24.8 %copy-start.9 = (f32[256]{0:T(256)S(1)}, f32[256]{0:T(256)}, u32[]{:S(2)}) copy-start(f32[256]{0:T(256)} %param.18) | copy-start | bytes 3076
  81.5 24.7 %all-to-all-start.1 = ((bf16[32,64,128]{2,1,0:T(8,128)(2,1)}), bf16[32,64,128]{2,1,0:T(8,128)(2,1)S(1)}, u32[]{:S(2)}, u32[]{:S(2)}) async-start(bf16[32,64,128]{2,1,0:T(8,128)(2,1)} %copy-done.6), calls=%async_computation.1 | async-start | bytes 1048576 | tf_op jit(solution)/shard_map/all_to_all | solution.py:263
  90.9 15.3 %collective-permute-start = (bf16[32,80,128]{2,1,0:T(8,128)(2,1)S(1)}, bf16[32,80,128]{2,1,0:T(8,128)(2,1)S(1)}, u32[]{:S(2)}, u32[]{:S(2)}) collective-permute-start(bf16[32,80,128]{2,1,0:T(8,128)(2,1)S(1)} %slice.4), channel_id=1, source_target_pairs={{0,1},{1,0},{2,3},{3,2},{4,5},{5,4},{6,7},{7,6},{8,9},{9,8},{10,11... | collective-permute-start | bytes 1966088 | tf_op jit(solution)/shard_map/ppermute | solution.py:262
  106.3 21.3 %copy-start.10 = (s32[1,128]{1,0:T(1,128)S(1)}, s32[1,128]{1,0:T(1,128)}, u32[]{:S(2)}) copy-start(s32[1,128]{1,0:T(1,128)} %labels.1) | copy-start | bytes 1540
  108.6 19.0 %all-to-all-start.2 = ((bf16[32,24,256]{2,1,0:T(8,128)(2,1)}), bf16[32,24,256]{2,1,0:T(8,128)(2,1)S(1)}, u32[]{:S(2)}, u32[]{:S(2)}) async-start(bf16[32,24,256]{2,1,0:T(8,128)(2,1)} %bitcast.6), calls=%async_computation.2 | async-start | bytes 786432 | tf_op jit(solution)/shard_map/all_to_all | solution.py:281
  127.6 4.0 %copy-start.1 = (bf16[4096,1280]{1,0:T(8,128)(2,1)S(1)}, bf16[4096,1280]{1,0:T(8,128)(2,1)}, u32[]{:S(2)}) copy-start(bf16[4096,1280]{1,0:T(8,128)(2,1)} %all-gather.3.cloned.1.call-done) | copy-start | bytes 31457284
  131.6 1.0 copy-start.4
Sparse Core Ops, SparseCore 0:
  9.9 65.2 all-gather.2

commit v3 on v2

--- a/solution.py
+++ b/solution.py
@@ -18,7 +18,9 @@
 HIDDEN = 256
 UNION = 24
 SLAB = 256
-UNROLL = 16
+UNROLL = 64
+CHUNK = 1024
+PAIRS = 4
 TABLE_STEP = 8
 F32 = jnp.float32
 BF16 = jnp.bfloat16
@@ -69,65 +71,79 @@
         block = features[:, pl.ds(pair * 2 * OWN, 2 * OWN)].astype(F32)
         for half in range(2):
             owner = 2 * pair + half
-            own = block[:, half * OWN : (half + 1) * OWN]
-            marks = marked[owner : owner + 1]
-            last = jnp.concatenate(
-                [
-                    own[24:, 128:],
-                    marks[:, :64],
-                    marks[:, 64:128],
-                    marks[:, 128:192],
-                    jnp.zeros((5, 64), F32),
-                ],
-                axis=0,
-            )
-            send[owner] = jnp.concatenate(
-                [shared, own[:, :128], jnp.concatenate([own[:24, 128:], last], axis=1)], axis=0
-            ).astype(BF16)
-
-
-def gather_kernel(slots, features, send, table, sums):
+            marks = [marked[owner : owner + 1, k * 64 : (k + 1) * 64] for k in range(3)]
+            last = jnp.concatenate(marks + [jnp.zeros((5, 64), F32)], axis=0)
+            send[owner] = jnp.concatenate([shared, folded(block, half, last)], axis=0).astype(BF16)
+
+
+def folded(block, half, last):
+    rest = block[:, 128 + half * 64 : 192 + half * 64]
+    rest = jnp.concatenate([rest[:24], jnp.concatenate([rest[24:], last], axis=0)], axis=1)
+    return jnp.concatenate([block[:, half * 256 : half * 256 + 128], rest], axis=0)
+
+
+def mean_of(flipped):
+    thirds = [flipped[t * WIDTH : (t + 1) * WIDTH] for t in range(3)]
+    return (thirds[0] + thirds[1] + thirds[2]) / jnp.maximum(flipped[3 * WIDTH : 3 * WIDTH + 1], 1.0)
+
+
+def gather_kernel(slots, features, send, table, sums, lists, arrived):
+    def fetch(chunk):
+        span = pl.ds(pl.multiple_of(chunk * FAN * CHUNK, FAN * CHUNK), FAN * CHUNK)
+        return pltpu.make_async_copy(slots.at[span], lists.at[span], arrived.at[chunk])
+
+    for chunk in range(ROWS // CHUNK):
+        fetch(chunk).start()
+
+    lane = iota((128, 128), 1)
+    third = INPUTS // 3
+
     def fill(step, carry):
         for part in range(TABLE_STEP):
             at = pl.multiple_of((step * TABLE_STEP + part) * 128, 128)
-            block = jnp.concatenate(
-                [features[:, pl.ds(at, 128)].astype(F32), jnp.ones((8, 128), F32)], axis=0
-            )
-            table[pl.ds(at, 128), pl.ds(0, WIDTH + 8)] = block.T
+            blocks = [features[:, pl.ds(t * third + at, 128)].astype(F32) for t in range(3)]
+            flipped = jnp.concatenate(blocks + [jnp.ones((8, 128), F32)], axis=0).T
+            for t in range(3):
+                kept = ((lane >= t * WIDTH) & (lane < (t + 1) * WIDTH)) | (lane >= 3 * WIDTH)
+                table[pl.ds(t * third + at, 128), :] = jnp.where(kept, flipped, 0.0)
         return carry
 
-    lax.fori_loop(0, INPUTS // 128 // TABLE_STEP, fill, 0)
+    lax.fori_loop(0, third // 128 // TABLE_STEP, fill, 0)
     table[pl.ds(INPUTS, 8), :] = jnp.zeros((8, 128), F32)
 
-    def owner_step(owner, carry):
-        first = owner * OWN
+    def chunk_step(chunk, carry):
+        fetch(chunk).wait()
 
         def block(step, inner):
-            at = first + step * UNROLL
-            lists = [slots.at[pl.ds(slot * ROWS + at, UNROLL)] for slot in range(FAN)]
-            result = sums.at[pl.ds(pl.multiple_of(step * UNROLL, UNROLL), UNROLL), :]
+            first = chunk * FAN * CHUNK + step * UNROLL
+            named = [lists.at[pl.ds(first + slot * CHUNK, UNROLL)] for slot in range(FAN)]
+            at = pl.multiple_of(chunk * CHUNK + step * UNROLL, UNROLL)
+            result = sums.at[pl.ds(at, UNROLL), :]
             for row in range(UNROLL):
                 result[pl.ds(row, 1), :] = add_all(
-                    [table[pl.ds(lists[slot][row], 1), :] for slot in range(FAN)]
+                    [table[pl.ds(named[slot][row], 1), :] for slot in range(FAN)]
                 )
             return inner
 
-        lax.fori_loop(0, OWN // UNROLL, block, 0)
-        head = sums[pl.ds(0, 128), :].T
-        tail = sums[pl.ds(128, 64), :].T
-        head = head[:WIDTH] / jnp.maximum(head[WIDTH : WIDTH + 1], 1.0)
-        tail = tail[:WIDTH] / jnp.maximum(tail[WIDTH : WIDTH + 1], 1.0)
-        last = jnp.concatenate([tail[24:], jnp.zeros((8, 64), F32)], axis=0)
-        send[owner] = jnp.concatenate(
-            [head, jnp.concatenate([tail[:24], last], axis=1)], axis=0
-        ).astype(BF16)
+        return lax.fori_loop(0, CHUNK // UNROLL, block, carry)
+
+    lax.fori_loop(0, ROWS // CHUNK, chunk_step, 0)
+
+    def pair_step(step, carry):
+        for part in range(PAIRS):
+            pair = step * PAIRS + part
+            at = pl.multiple_of(pair * 2 * OWN, 128)
+            means = [mean_of(sums[pl.ds(at + k * 128, 128), :].T) for k in range(3)]
+            block = jnp.concatenate(means, axis=1)
+            for half in range(2):
+                send[2 * pair + half] = folded(block, half, jnp.zeros((8, 64), F32)).astype(BF16)
         return carry
 
-    lax.fori_loop(0, FEAT, owner_step, 0)
+    lax.fori_loop(0, FEAT // 2 // PAIRS, pair_step, 0)
 
 
 def hidden_kernel(
-    core, mine, theirs, means, bias, hidden, rows, stacked, held, other, marks, chosen
+    spot, mine, theirs, means, bias, hidden, rows, stacked, held, other, marks, chosen
 ):
     for source in range(FEAT):
         own = mine[source].astype(F32)
@@ -147,10 +163,11 @@
     stacked[:, pl.ds(192, 64)] = jnp.zeros((FEAT * 80, 64), BF16)
     first = contract(stacked[...], held[...], 0, 0)[:OWN]
     second = contract(stacked[...], other[...], 0, 0)[:OWN]
-    even = core[0] == 0
+    even = spot[0] == 0
     pre = jnp.concatenate(
         [jnp.where(even, first, second), jnp.where(even, second, first)], axis=1
     )
+    pre = jnp.where(spot[1] == 0, pre, jnp.concatenate([pre[128:], pre[:128]], axis=0))
     result = jnp.maximum(pre + bias[...], 0.0).astype(BF16)
     hidden[...] = result
     rank = contract(marks[...].astype(BF16), earlier(SLAB), 1, 0)
@@ -173,39 +190,73 @@
     picks[1] = jnp.where(spots == place[pl.ds(FAN, 1), :], 1.0, 0.0).astype(BF16)
 
 
-def loss_kernel(rows, picks, labels, weights, loss, inputs, wanted, largest, summed, picked):
-    step = pl.program_id(0)
+def loss_kernel(rows, picks, labels, weights, loss, inputs, logits):
+    count = contract(picks[0], jnp.ones((FEAT * UNION, 128), BF16), 0, 0)[:, :1]
+    agg = contract(picks[0], rows[...], 0, 0) / jnp.maximum(count, 1.0)
+    inputs[:, pl.ds(0, HIDDEN)] = contract(picks[1], rows[...], 0, 0).astype(BF16)
+    inputs[:, pl.ds(HIDDEN, HIDDEN)] = agg.astype(BF16)
+    offset = (
+        jnp.broadcast_to(labels[...].astype(F32), (TARGETS, TARGETS)).T.astype(jnp.int32)
+        - iota((TARGETS, TARGETS), 1)
+    )
     width = weights.shape[2]
-
-    @pl.when(step == 0)
-    def _():
-        count = contract(picks[0], jnp.ones((FEAT * UNION, 128), BF16), 0, 0)[:, :1]
-        agg = contract(picks[0], rows[...], 0, 0) / jnp.maximum(count, 1.0)
-        inputs[:, pl.ds(0, HIDDEN)] = contract(picks[1], rows[...], 0, 0).astype(BF16)
-        inputs[:, pl.ds(HIDDEN, HIDDEN)] = agg.astype(BF16)
-        spread = jnp.broadcast_to(labels[...].astype(F32), (TARGETS, TARGETS)).T
-        wanted[...] = spread[:, :1].astype(jnp.int32)
-        largest[...] = jnp.full((TARGETS, 1), -jnp.inf, F32)
-        summed[...] = jnp.zeros((TARGETS, 1), F32)
-        picked[...] = jnp.zeros((TARGETS, 1), F32)
-
-    logits = contract(inputs[...], weights[0], 1, 0)
-    before = largest[...]
-    now = jnp.maximum(before, jnp.max(logits, axis=1, keepdims=True))
-    part = jnp.sum(jnp.exp(logits - now), axis=1, keepdims=True)
-    summed[...] = summed[...] * jnp.exp(before - now) + part
-    largest[...] = now
-    classes = iota((TARGETS, width), 1) + step * width
-    picked[...] += jnp.sum(jnp.where(classes == wanted[...], logits, 0.0), axis=1, keepdims=True)
-
-    @pl.when(step == NODE - 1)
-    def _():
-        column = largest[...] + jnp.log(summed[...]) - picked[...]
-        loss[...] = jnp.broadcast_to(column, (TARGETS, TARGETS)).T[:1]
+    largest = jnp.full((TARGETS, TARGETS), -jnp.inf, F32)
+    summed = jnp.zeros((TARGETS, TARGETS), F32)
+    picked = jnp.zeros((TARGETS, TARGETS), F32)
+    for step in range(NODE + 1):
+        if step < NODE:
+            logits[step % 2] = contract(inputs[...], weights[step], 1, 0)
+        if step > 0:
+            spans = [pl.ds(k * 128, 128) for k in range(width // 128)]
+            held = logits.at[(step - 1) % 2]
+            now = largest
+            for span in spans:
+                now = jnp.maximum(now, held[:, span])
+            summed = summed * jnp.exp(largest - now)
+            for k, span in enumerate(spans):
+                part = held[:, span]
+                summed = summed + jnp.exp(part - now)
+                picked = picked + jnp.where(offset == (step - 1) * width + k * 128, part, 0.0)
+            largest = now
+    most = jnp.max(largest, axis=1, keepdims=True)
+    total = jnp.sum(summed * jnp.exp(largest - most), axis=1, keepdims=True)
+    column = most + jnp.log(total) - jnp.sum(picked, axis=1, keepdims=True)
+    loss[...] = jnp.broadcast_to(column, (TARGETS, TARGETS)).T[:1]
 
 
 VMEM = pl.BlockSpec(memory_space=pltpu.VMEM)
 SMEM = pl.BlockSpec(memory_space=pltpu.SMEM)
+
+
+def call_gather(slots, table):
+    return pl.pallas_call(
+        gather_kernel,
+        out_shape=jax.ShapeDtypeStruct((FEAT, 64, 128), BF16),
+        in_specs=[pl.BlockSpec(memory_space=pl.ANY), VMEM],
+        out_specs=VMEM,
+        scratch_shapes=[
+            pltpu.VMEM((INPUTS + 8, 128), F32),
+            pltpu.VMEM((ROWS, 128), F32),
+            pltpu.SMEM((FAN * ROWS,), jnp.int32),
+            pltpu.SemaphoreType.DMA((ROWS // CHUNK,)),
+        ],
+        compiler_params=pltpu.CompilerParams(vmem_limit_bytes=24 * 2**20),
+        cost_estimate=pl.CostEstimate(flops=10**9, bytes_accessed=150 * 10**6, transcendentals=0),
+    )(slots, table)
+
+
+def call_loss(rows, picks, labels, weights):
+    return pl.pallas_call(
+        loss_kernel,
+        out_shape=jax.ShapeDtypeStruct((1, TARGETS), F32),
+        in_specs=[VMEM] * 4,
+        out_specs=VMEM,
+        scratch_shapes=[
+            pltpu.VMEM((TARGETS, 2 * HIDDEN), BF16),
+            pltpu.VMEM((2, TARGETS, weights.shape[2]), F32),
+        ],
+        compiler_params=pltpu.CompilerParams(vmem_limit_bytes=24 * 2**20),
+    )(rows, picks, labels, weights)
 
 
 def body(
@@ -220,7 +271,8 @@
     first_bias,
     class_weight,
 ):
-    slots = jnp.where(first_mask[:, 0, :] > 0, first_neighbours[:, 0, :], INPUTS).reshape(-1)
+    slots = jnp.where(first_mask[:, 0, :] > 0, first_neighbours[:, 0, :], INPUTS)
+    slots = slots.reshape(FAN, ROWS // CHUNK, CHUNK).transpose(1, 0, 2).reshape(-1)
     core = lax.rem(lax.axis_index("node"), 2).astype(jnp.int32)
     half = lax.dynamic_slice(first_weight, (0, 0, core * 128), (2, WIDTH, 128))
     all_class = lax.all_gather(class_weight, "node", axis=0)
@@ -246,21 +298,12 @@
         cost_estimate=pl.CostEstimate(flops=10**8, bytes_accessed=3 * 10**6, transcendentals=0),
     )(table, half.reshape(2 * WIDTH, 128), second_neighbours, target_index)
     own = lax.all_to_all(own, "feat", 0, 0)
-    send = pl.pallas_call(
-        gather_kernel,
-        out_shape=jax.ShapeDtypeStruct((FEAT, 64, 128), BF16),
-        in_specs=[SMEM, VMEM],
-        out_specs=VMEM,
-        scratch_shapes=[
-            pltpu.VMEM((INPUTS + 8, 128), F32),
-            pltpu.VMEM((OWN, 128), F32),
-        ],
-        compiler_params=pltpu.CompilerParams(vmem_limit_bytes=24 * 2**20),
-        cost_estimate=pl.CostEstimate(flops=10**9, bytes_accessed=150 * 10**6, transcendentals=0),
-    )(slots, table)
+    send = call_gather(slots, table)
     swap = [(device, device ^ 1) for device in range(NODE)]
     theirs = lax.ppermute(own[:, : 2 * WIDTH], "node", swap)
     means = lax.all_to_all(send, "feat", 0, 0)
+    means, all_class = lax.optimization_barrier((means, all_class))
+    spot = jnp.stack([core, lax.rem(lax.axis_index("feat"), 2).astype(jnp.int32)])
     hidden, rows = pl.pallas_call(
         hidden_kernel,
         out_shape=(
@@ -277,7 +320,7 @@
             pltpu.VMEM((FEAT * UNION, SLAB), F32),
         ],
         compiler_params=pltpu.CompilerParams(vmem_limit_bytes=24 * 2**20),
-    )(core[None], own, theirs, means, first_bias[None, :])
+    )(spot, own, theirs, means, first_bias[None, :])
     rows = lax.all_to_all(rows.reshape(FEAT, UNION, HIDDEN), "feat", 0, 0)
     rows = rows.reshape(FEAT * UNION, HIDDEN)
     picks = pl.pallas_call(
@@ -287,28 +330,7 @@
         out_specs=VMEM,
         cost_estimate=pl.CostEstimate(flops=10**7, bytes_accessed=4 * 10**6, transcendentals=0),
     )(place, second_mask)
-    width = class_weight.shape[1]
-    whole = lambda *shape: pl.BlockSpec(shape, lambda i: (0,) * len(shape))
-    loss = pl.pallas_call(
-        loss_kernel,
-        grid=(NODE,),
-        out_shape=jax.ShapeDtypeStruct((1, TARGETS), F32),
-        in_specs=[
-            whole(FEAT * UNION, HIDDEN),
-            whole(2, FEAT * UNION, TARGETS),
-            whole(1, TARGETS),
-            pl.BlockSpec((1, 2 * HIDDEN, width), lambda i: (i, 0, 0)),
-        ],
-        out_specs=whole(1, TARGETS),
-        scratch_shapes=[
-            pltpu.VMEM((TARGETS, 2 * HIDDEN), BF16),
-            pltpu.VMEM((TARGETS, 1), jnp.int32),
-            pltpu.VMEM((TARGETS, 1), F32),
-            pltpu.VMEM((TARGETS, 1), F32),
-            pltpu.VMEM((TARGETS, 1), F32),
-        ],
-        compiler_params=pltpu.CompilerParams(vmem_limit_bytes=24 * 2**20),
-    )(rows, picks, labels, all_class)
+    loss = call_loss(rows, picks, labels, all_class)
     return (hidden[None], loss)
 
 

time: 149 us -> 134 us (0.90)
  Pallas kernels: 67.2 us -> 49.1 us
  local copies, waits for them, and re-layouts: 9.06 us -> 11.1 us
    pallas_call x2, Pallas kernels: 61.6 us -> 41.8 us  [the longest x1 38.5 us: call_gather(): pl.pallas_call(gather_kernel, out_shape=jax.ShapeDtypeStruct((FEAT, 64, 1...]
    select_n x0 -> x2, local copies, waits for them, and re-layouts: none -> 2.01 us  [body(): jnp.where(first_mask[:, 0, :] > 0, first_neighbours[:, 0, :], INPUTS)]
    unnamed x26 -> x24, local copies, waits for them, and re-layouts: 9 us -> 7.95 us
  transfers between devices with their start and end apart: 5 -> 5, of which waited for: 2 -> 2; matrix products, arithmetic and copies ran while one was open for 1% -> 4% of each run, Pallas kernels for 41% -> 33%
where the time goes in v3:
time: 134 us; the launch traced here: 132 us
  Pallas kernels  49.1 us (37%)
  starting transfers between devices  29.3 us (22%)
  waiting for transfers between devices  25.3 us (19%)
  between operations  14.2 us (11%)
  local copies, waits for them, and re-layouts  11.1 us (8%)
  other arithmetic  2.8 us (2%)
    pallas_call x1, Pallas kernels, call_gather(): pl.pallas_call(gather_kernel, out_shape=jax.ShapeDtypeStruct((FEAT, 64, 1...  38.5 us
    all_to_all x1, waiting for transfers between devices, body(): means = lax.all_to_all(send, 'feat', 0, 0)  13.6 us
    all_to_all x1, starting transfers between devices, body(): own = lax.all_to_all(own, 'feat', 0, 0)  12.2 us
    all_to_all x1, waiting for transfers between devices, body(): rows = lax.all_to_all(rows.reshape(FEAT, UNION, HIDDEN), 'feat', 0, 0)  11 us
    all_to_all x1, starting transfers between devices, body(): means = lax.all_to_all(send, 'feat', 0, 0)  9.4 us
    unnamed x24, local copies, waits for them, and re-layouts  7.95 us
    all_to_all x1, starting transfers between devices, body(): rows = lax.all_to_all(rows.reshape(FEAT, UNION, HIDDEN), 'feat', 0, 0)  6.05 us
    pallas_call x1, Pallas kernels, call_loss(): pl.pallas_call(loss_kernel, out_shape=jax.ShapeDtypeStruct((1, TARGETS),...  3.29 us
  transfers between devices with their start and end apart: 5, of which 2 were waited for; matrix products, arithmetic and copies ran while one was open for 4% of the time, Pallas kernels for 33%

profile of v3, /device:TPU:1, one launch (start us, length us, event | category | flops | bytes accessed | tf_op | source)
XLA Modules:
  0.0 131.8 jit_solution(17362642846987968813)
XLA Ops:
  7.2 0.0 copy-start
  7.2 0.0 all-gather.3.cloned.1.call-start
  7.2 0.7 all-gather.3.cloned.1.call-update
  7.9 0.0 copy-done
  8.0 0.0 copy-done.7
  8.0 0.0 copy-done.10
  8.0 0.0 copy-start.2
  8.0 1.5 %copy-done.2 = bf16[40,1,24576]{2,0,1:T(8,128)(2,1)S(1)} copy-done((bf16[40,1,24576]{2,0,1:T(8,128)(2,1)S(1)}, bf16[40,1,24576]{2,0,1:T(8,128)(2,1)}, u32[]{:S(2)}) %copy-start.2) | copy-done | bytes 1966104
  9.5 2.6 %shard_map.113 = (bf16[32,144,128]{2,1,0:T(8,128)(2,1)}, s32[16,128]{1,0:T(8,128)S(1)}) custom-call(bf16[40,24576]{1,0:T(8,128)(2,1)S(1)} %bitcast.13, bf16[80,128]{1,0:T(8,128)(2,1)S(1)} %bitcast.16, s32[10,1,128]{2,1,0:T(1,128)S(1)} %copy-done.7, s32[1,128]{1,0:T(1,128)S(1)} %copy-done.10), custom_call_target="tpu_custom_call" | custom-call | flops 100000000 | bytes 3000000 | tf_op jit(solution)/shard_map/pallas_call | solution.py:280
  12.2 0.6 copy-done.6
  12.8 12.2 %all-to-all-start = ((bf16[32,144,128]{2,1,0:T(8,128)(2,1)}), bf16[32,144,128]{2,1,0:T(8,128)(2,1)S(1)}, u32[]{:S(2)}, u32[]{:S(2)}) async-start(bf16[32,144,128]{2,1,0:T(8,128)(2,1)} %get-tuple-element.8), calls=%async_computation | async-start | bytes 2359296 | tf_op jit(solution)/shard_map/all_to_all | solution.py:300
  24.9 0.0 copy-start.3
  25.0 2.7 %fusion = s32[10,6144]{1,0:T(8,128)} fusion(s32[10,1,6144]{2,1,0:T(1,128)S(1)} %copy-done.11, s32[10,1,6144]{2,1,0:T(1,128)} %param.12), kind=kLoop, calls=%fused_computation.2 | loop fusion | flops 122880 | bytes 737280 | tf_op jit(solution)/shard_map/jit(_where)/select_n | solution.py:274
  27.7 1.1 select_n.13
  28.8 0.9 copy.14
  29.7 1.0 reshape.24.slots
  30.7 38.5 %shard_map.114 = bf16[32,64,128]{2,1,0:T(8,128)(2,1)S(1)} custom-call(s32[61440]{0:T(1024)S(1)} %reshape.24.slots, bf16[40,24576]{1,0:T(8,128)(2,1)S(1)} %bitcast.14), custom_call_target="tpu_custom_call" | custom-call | flops 1000000000 | bytes 150000000 | tf_op jit(solution)/shard_map/pallas_call | solution.py:232
  69.2 0.8 copy-done.5
  70.0 0.0 all-to-all-done.mine
  70.0 9.4 %all-to-all-start.1 = ((bf16[32,64,128]{2,1,0:T(8,128)(2,1)}), bf16[32,64,128]{2,1,0:T(8,128)(2,1)S(1)}, u32[]{:S(2)}, u32[]{:S(2)}) async-start(bf16[32,64,128]{2,1,0:T(8,128)(2,1)} %copy-done.5), calls=%async_computation.1 | async-start | bytes 1048576 | tf_op jit(solution)/shard_map/all_to_all | solution.py:304
  79.5 1.7 %collective-permute-start = (bf16[32,80,128]{2,1,0:T(8,128)(2,1)S(1)}, bf16[32,80,128]{2,1,0:T(8,128)(2,1)S(1)}, u32[]{:S(2)}, u32[]{:S(2)}) collective-permute-start(bf16[32,80,128]{2,1,0:T(8,128)(2,1)S(1)} %slice.4), channel_id=1, source_target_pairs={{0,1},{1,0},{2,3},{3,2},{4,5},{5,4},{6,7},{7,6},{8,9},{9,8},{10,11... | collective-permute-start | bytes 1966088 | tf_op jit(solution)/shard_map/ppermute | solution.py:303
  81.2 0.1 pad_add_fusion.spot
  81.2 13.6 %all-to-all-done.1.means = bf16[32,64,128]{2,1,0:T(8,128)(2,1)S(1)} async-done(((bf16[32,64,128]{2,1,0:T(8,128)(2,1)}), bf16[32,64,128]{2,1,0:T(8,128)(2,1)S(1)}, u32[]{:S(2)}, u32[]{:S(2)}) %all-to-all-start.1) | async-done | bytes 524320 | tf_op jit(solution)/shard_map/all_to_all | solution.py:304
  94.9 0.0 collective-permute-done.theirs
  94.9 0.0 copy-start.9
  94.9 2.8 %shard_map.115 = (bf16[192,256]{1,0:T(8,128)(2,1)}, bf16[768,256]{1,0:T(8,128)(2,1)}) custom-call(s32[2]{0:T(128)S(1)} %pad_add_fusion.spot, bf16[32,144,128]{2,1,0:T(8,128)(2,1)S(1)} %all-to-all-done.mine, bf16[32,80,128]{2,1,0:T(8,128)(2,1)S(1)} %collective-permute-done.theirs, bf16[32,64,128]{2,1,0:T(8,128)(2,1)S(1)} %all-to-all-done.1.means, ...), custom_call_target="tpu_custom_call" | custom-call | tf_op jit(solution)/shard_map/pallas_call | solution.py:307
  97.7 6.0 %all-to-all-start.2 = ((bf16[32,24,256]{2,1,0:T(8,128)(2,1)}), bf16[32,24,256]{2,1,0:T(8,128)(2,1)S(1)}, u32[]{:S(2)}, u32[]{:S(2)}) async-start(bf16[32,24,256]{2,1,0:T(8,128)(2,1)} %bitcast.8), calls=%async_computation.2 | async-start | bytes 786432 | tf_op jit(solution)/shard_map/all_to_all | solution.py:324
  103.8 1.9 %shard_map.116.picks = bf16[2,768,128]{2,1,0:T(8,128)(2,1)} custom-call(s32[16,128]{1,0:T(8,128)} %copy-done.6, s32[10,1,128]{2,1,0:T(1,128)} %mask.1), custom_call_target="tpu_custom_call" | custom-call | flops 10000000 | bytes 4000000 | tf_op jit(solution)/shard_map/pallas_call | solution.py:326
  105.7 11.0 %all-to-all-done.2 = bf16[32,24,256]{2,1,0:T(8,128)(2,1)S(1)} async-done(((bf16[32,24,256]{2,1,0:T(8,128)(2,1)}), bf16[32,24,256]{2,1,0:T(8,128)(2,1)S(1)}, u32[]{:S(2)}, u32[]{:S(2)}) %all-to-all-start.2) | async-done | bytes 393248 | tf_op jit(solution)/shard_map/all_to_all | solution.py:324
  116.7 4.0 %copy-done.1 = bf16[4096,1280]{1,0:T(8,128)(2,1)S(1)} copy-done((bf16[4096,1280]{1,0:T(8,128)(2,1)S(1)}, bf16[4096,1280]{1,0:T(8,128)(2,1)}, u32[]{:S(2)}) %copy-start.1) | copy-done | bytes 10485784
  120.7 1.0 copy-done.4
  121.7 3.3 %shard_map.117 = f32[1,128]{1,0:T(1,128)} custom-call(bf16[768,256]{1,0:T(8,128)(2,1)S(1)} %bitcast.15, bf16[2,768,128]{2,1,0:T(8,128)(2,1)S(1)} %copy-done.4, s32[1,128]{1,0:T(1,128)S(1)} %copy-done.9, bf16[8,512,1280]{2,1,0:T(8,128)(2,1)S(1)} %bitcast.12), custom_call_target="tpu_custom_call" | custom-call | tf_op jit(solution)/shard_map/pallas_call | solution.py:249
  (15 shorter events, 0.1 us)
Async XLA Ops:
  7.2 0.8 copy-start
  7.2 0.8 copy-start.7
  7.2 0.8 copy-start.10
  7.2 87.7 %all-gather.3.cloned.1.call-start = ((), (), s32[]{:S(2)}) async-start(), calls=%async_computation.3 | async-start | bytes 11796480 | tf_op jit(solution)/shard_map/all_gather | solution.py:278
  8.0 1.5 %copy-start.2 = (bf16[40,1,24576]{2,0,1:T(8,128)(2,1)S(1)}, bf16[40,1,24576]{2,0,1:T(8,128)(2,1)}, u32[]{:S(2)}) copy-start(bf16[40,1,24576]{2,0,1:T(8,128)(2,1)} %param.10) | copy-start | bytes 5898244
  12.2 0.6 copy-start.6
  12.8 12.2 %copy-start.11 = (s32[10,1,6144]{2,1,0:T(1,128)S(1)}, s32[10,1,6144]{2,1,0:T(1,128)}, u32[]{:S(2)}) copy-start(s32[10,1,6144]{2,1,0:T(1,128)} %param.11) | copy-start | bytes 737284
  12.8 57.3 %all-to-all-start = ((bf16[32,144,128]{2,1,0:T(8,128)(2,1)}), bf16[32,144,128]{2,1,0:T(8,128)(2,1)S(1)}, u32[]{:S(2)}, u32[]{:S(2)}) async-start(bf16[32,144,128]{2,1,0:T(8,128)(2,1)} %get-tuple-element.8), calls=%async_computation | async-start | bytes 2359296 | tf_op jit(solution)/shard_map/all_to_all | solution.py:300
  24.9 5.8 %copy-start.3 = (bf16[40,1,24576]{2,0,1:T(8,128)(2,1)S(1)}, bf16[40,1,24576]{2,0,1:T(8,128)(2,1)}, u32[]{:S(2)}) copy-start(bf16[40,1,24576]{2,0,1:T(8,128)(2,1)} %param.10) | copy-start | bytes 5898244
  69.2 0.8 copy-start.5
  70.0 24.8 %copy-start.8 = (f32[256]{0:T(256)S(1)}, f32[256]{0:T(256)}, u32[]{:S(2)}) copy-start(f32[256]{0:T(256)} %param.18) | copy-start | bytes 3076
  70.0 24.8 %all-to-all-start.1 = ((bf16[32,64,128]{2,1,0:T(8,128)(2,1)}), bf16[32,64,128]{2,1,0:T(8,128)(2,1)S(1)}, u32[]{:S(2)}, u32[]{:S(2)}) async-start(bf16[32,64,128]{2,1,0:T(8,128)(2,1)} %copy-done.5), calls=%async_computation.1 | async-start | bytes 1048576 | tf_op jit(solution)/shard_map/all_to_all | solution.py:304
  79.5 15.4 %collective-permute-start = (bf16[32,80,128]{2,1,0:T(8,128)(2,1)S(1)}, bf16[32,80,128]{2,1,0:T(8,128)(2,1)S(1)}, u32[]{:S(2)}, u32[]{:S(2)}) collective-permute-start(bf16[32,80,128]{2,1,0:T(8,128)(2,1)S(1)} %slice.4), channel_id=1, source_target_pairs={{0,1},{1,0},{2,3},{3,2},{4,5},{5,4},{6,7},{7,6},{8,9},{9,8},{10,11... | collective-permute-start | bytes 1966088 | tf_op jit(solution)/shard_map/ppermute | solution.py:303
  94.9 21.8 %copy-start.9 = (s32[1,128]{1,0:T(1,128)S(1)}, s32[1,128]{1,0:T(1,128)}, u32[]{:S(2)}) copy-start(s32[1,128]{1,0:T(1,128)} %labels.1) | copy-start | bytes 1540
  97.7 19.0 %all-to-all-start.2 = ((bf16[32,24,256]{2,1,0:T(8,128)(2,1)}), bf16[32,24,256]{2,1,0:T(8,128)(2,1)S(1)}, u32[]{:S(2)}, u32[]{:S(2)}) async-start(bf16[32,24,256]{2,1,0:T(8,128)(2,1)} %bitcast.8), calls=%async_computation.2 | async-start | bytes 786432 | tf_op jit(solution)/shard_map/all_to_all | solution.py:324
  116.7 4.0 %copy-start.1 = (bf16[4096,1280]{1,0:T(8,128)(2,1)S(1)}, bf16[4096,1280]{1,0:T(8,128)(2,1)}, u32[]{:S(2)}) copy-start(bf16[4096,1280]{1,0:T(8,128)(2,1)} %all-gather.3.cloned.1.call-done) | copy-start | bytes 31457284
  120.7 1.0 copy-start.4
Sparse Core Ops, SparseCore 0:
  9.9 65.2 all-gather.2

commit v4 on v3

--- a/solution.py
+++ b/solution.py
@@ -19,6 +19,8 @@
 UNION = 24
 SLAB = 256
 UNROLL = 64
+LEAST = 3
+LINES = ROWS // 128
 CHUNK = 1024
 PAIRS = 4
 TABLE_STEP = 8
@@ -82,14 +84,62 @@
     return jnp.concatenate([block[:, half * 256 : half * 256 + 128], rest], axis=0)
 
 
+def order_kernel(neighbours, mask, lists, ranks, columns):
+    used = [jnp.where(mask[slot] > 0, 1, 0) for slot in range(FAN)]
+    before = [jnp.zeros((LINES, 128), jnp.int32)]
+    for slot in range(FAN):
+        before.append(before[slot] + used[slot])
+    count = before[FAN]
+    for place in range(FAN):
+        node = jnp.where(count > place, 0, INPUTS)
+        for slot in range(place, FAN):
+            here = (used[slot] > 0) & (before[slot] == place)
+            node = node + jnp.where(here, neighbours[slot], 0)
+        high = node >> 8
+        columns[place] = high.astype(F32)
+        columns[16 + place] = (node - high * 256).astype(F32)
+    columns[FAN] = jnp.zeros((LINES, 128), F32)
+    columns[16 + FAN] = count.astype(F32)
+    hot = [jnp.where(count == amount, 1.0, 0.0) for amount in range(FAN + 1)]
+    stacked = jnp.concatenate(hot, axis=0).astype(BF16)
+    second = iota(((FAN + 1) * LINES, 128), 0) % 2 == 1
+    earlier_same = contract(stacked, earlier(128), 1, 0)
+    all_same = contract(stacked, jnp.ones((128, 128), BF16), 1, 0)
+    above = pltpu.roll(all_same, 1, 0)
+    below = pltpu.roll(all_same, (FAN + 1) * LINES - 1, 0)
+    earlier_same = earlier_same + jnp.where(second, above, 0.0)
+    all_same = all_same + jnp.where(second, above, below)
+    rank = jnp.zeros((LINES, 128), F32)
+    higher = jnp.zeros((LINES, 128), F32)
+    for amount in reversed(range(FAN + 1)):
+        span = slice(amount * LINES, (amount + 1) * LINES)
+        rank = rank + hot[amount] * (earlier_same[span] + higher)
+        higher = higher + all_same[span]
+    ranks[...] = rank.astype(jnp.int32)
+    for line in range(0, LINES, 2):
+        part = contract(columns[:, line, :].astype(BF16), moved(ranks, line), 1, 1)
+        part += contract(columns[:, line + 1, :].astype(BF16), moved(ranks, line + 1), 1, 1)
+        part = (part[:16] * 256.0 + part[16:]).astype(jnp.int32)
+        first = line // 8 * 8 * (FAN + 1) + line % 8
+        for half in range(2):
+            here = part[: FAN + 1, half * 128 : (half + 1) * 128]
+            lists[pl.ds(first + half, FAN + 1, stride=8), :] = here
+
+
+def moved(ranks, line):
+    return jnp.where(iota((256, 128), 0) == ranks[pl.ds(line, 1), :], 1.0, 0.0).astype(BF16)
+
+
 def mean_of(flipped):
     thirds = [flipped[t * WIDTH : (t + 1) * WIDTH] for t in range(3)]
     return (thirds[0] + thirds[1] + thirds[2]) / jnp.maximum(flipped[3 * WIDTH : 3 * WIDTH + 1], 1.0)
 
 
-def gather_kernel(slots, features, send, table, sums, lists, arrived):
+def gather_kernel(slots, ranks, features, send, table, sums, lists, arrived):
+    size = (FAN + 1) * CHUNK
+
     def fetch(chunk):
-        span = pl.ds(pl.multiple_of(chunk * FAN * CHUNK, FAN * CHUNK), FAN * CHUNK)
+        span = pl.ds(pl.multiple_of(chunk * size, size), size)
         return pltpu.make_async_copy(slots.at[span], lists.at[span], arrived.at[chunk])
 
     for chunk in range(ROWS // CHUNK):
@@ -115,14 +165,30 @@
         fetch(chunk).wait()
 
         def block(step, inner):
-            first = chunk * FAN * CHUNK + step * UNROLL
-            named = [lists.at[pl.ds(first + slot * CHUNK, UNROLL)] for slot in range(FAN)]
+            first = chunk * size + step * UNROLL
             at = pl.multiple_of(chunk * CHUNK + step * UNROLL, UNROLL)
             result = sums.at[pl.ds(at, UNROLL), :]
-            for row in range(UNROLL):
-                result[pl.ds(row, 1), :] = add_all(
-                    [table[pl.ds(named[slot][row], 1), :] for slot in range(FAN)]
+
+            def add(depth):
+                named = [lists.at[pl.ds(first + slot * CHUNK, UNROLL)] for slot in range(depth)]
+                for row in range(UNROLL):
+                    result[pl.ds(row, 1), :] = add_all(
+                        [table[pl.ds(named[slot][row], 1), :] for slot in range(depth)]
+                    )
+
+            def choose(low, high):
+                if low == high:
+                    add(low)
+                    return
+                middle = (low + high) // 2
+                lax.cond(
+                    deepest <= middle,
+                    lambda: choose(low, middle),
+                    lambda: choose(middle + 1, high),
                 )
+
+            deepest = lists[first + FAN * CHUNK]
+            choose(LEAST, FAN)
             return inner
 
         return lax.fori_loop(0, CHUNK // UNROLL, block, carry)
@@ -130,13 +196,21 @@
     lax.fori_loop(0, ROWS // CHUNK, chunk_step, 0)
 
     def pair_step(step, carry):
-        for part in range(PAIRS):
-            pair = step * PAIRS + part
-            at = pl.multiple_of(pair * 2 * OWN, 128)
-            means = [mean_of(sums[pl.ds(at + k * 128, 128), :].T) for k in range(3)]
-            block = jnp.concatenate(means, axis=1)
-            for half in range(2):
-                send[2 * pair + half] = folded(block, half, jnp.zeros((8, 64), F32)).astype(BF16)
+        for part in range(0, PAIRS, 2):
+            line = (step * PAIRS + part) * 3
+            blocks = []
+            for k in range(0, 6, 2):
+                at = pl.multiple_of((line + k) * 128, 128)
+                means = [mean_of(sums[pl.ds(at + half * 128, 128), :].T) for half in range(2)]
+                means = jnp.concatenate(means, axis=1).astype(BF16)
+                for half in range(2):
+                    blocks.append(contract(means, moved(ranks, line + k + half), 1, 0))
+            for pair in range(2):
+                block = jnp.concatenate(blocks[pair * 3 : pair * 3 + 3], axis=1)
+                owner = 2 * (step * PAIRS + part + pair)
+                for half in range(2):
+                    tile = folded(block, half, jnp.zeros((8, 64), F32))
+                    send[owner + half] = tile.astype(BF16)
         return carry
 
     lax.fori_loop(0, FEAT // 2 // PAIRS, pair_step, 0)
@@ -190,7 +264,12 @@
     picks[1] = jnp.where(spots == place[pl.ds(FAN, 1), :], 1.0, 0.0).astype(BF16)
 
 
-def loss_kernel(rows, picks, labels, weights, loss, inputs, logits):
+def loss_kernel(rows, picks, labels, weights, loss, inputs, logits, held, arrived):
+    copies = [
+        pltpu.make_async_copy(weights.at[k], held.at[k], arrived.at[k]) for k in range(NODE)
+    ]
+    for copy in copies:
+        copy.start()
     count = contract(picks[0], jnp.ones((FEAT * UNION, 128), BF16), 0, 0)[:, :1]
     agg = contract(picks[0], rows[...], 0, 0) / jnp.maximum(count, 1.0)
     inputs[:, pl.ds(0, HIDDEN)] = contract(picks[1], rows[...], 0, 0).astype(BF16)
@@ -205,16 +284,17 @@
     picked = jnp.zeros((TARGETS, TARGETS), F32)
     for step in range(NODE + 1):
         if step < NODE:
-            logits[step % 2] = contract(inputs[...], weights[step], 1, 0)
+            copies[step].wait()
+            logits[step % 2] = contract(inputs[...], held[step], 1, 0)
         if step > 0:
             spans = [pl.ds(k * 128, 128) for k in range(width // 128)]
-            held = logits.at[(step - 1) % 2]
+            last = logits.at[(step - 1) % 2]
             now = largest
             for span in spans:
-                now = jnp.maximum(now, held[:, span])
+                now = jnp.maximum(now, last[:, span])
             summed = summed * jnp.exp(largest - now)
             for k, span in enumerate(spans):
-                part = held[:, span]
+                part = last[:, span]
                 summed = summed + jnp.exp(part - now)
                 picked = picked + jnp.where(offset == (step - 1) * width + k * 128, part, 0.0)
             largest = now
@@ -228,34 +308,51 @@
 SMEM = pl.BlockSpec(memory_space=pltpu.SMEM)
 
 
-def call_gather(slots, table):
+def call_order(neighbours, mask):
+    return pl.pallas_call(
+        order_kernel,
+        out_shape=(
+            jax.ShapeDtypeStruct((LINES * (FAN + 1), 128), jnp.int32),
+            jax.ShapeDtypeStruct((LINES, 128), jnp.int32),
+        ),
+        in_specs=[VMEM, VMEM],
+        out_specs=(VMEM, VMEM),
+        scratch_shapes=[pltpu.VMEM((32, LINES, 128), F32)],
+        compiler_params=pltpu.CompilerParams(vmem_limit_bytes=24 * 2**20),
+        cost_estimate=pl.CostEstimate(flops=10**8, bytes_accessed=10**7, transcendentals=0),
+    )(neighbours.reshape(FAN, LINES, 128), mask.reshape(FAN, LINES, 128))
+
+
+def call_gather(slots, ranks, table):
     return pl.pallas_call(
         gather_kernel,
         out_shape=jax.ShapeDtypeStruct((FEAT, 64, 128), BF16),
-        in_specs=[pl.BlockSpec(memory_space=pl.ANY), VMEM],
+        in_specs=[pl.BlockSpec(memory_space=pl.ANY), VMEM, VMEM],
         out_specs=VMEM,
         scratch_shapes=[
             pltpu.VMEM((INPUTS + 8, 128), F32),
             pltpu.VMEM((ROWS, 128), F32),
-            pltpu.SMEM((FAN * ROWS,), jnp.int32),
+            pltpu.SMEM(((FAN + 1) * ROWS,), jnp.int32),
             pltpu.SemaphoreType.DMA((ROWS // CHUNK,)),
         ],
         compiler_params=pltpu.CompilerParams(vmem_limit_bytes=24 * 2**20),
         cost_estimate=pl.CostEstimate(flops=10**9, bytes_accessed=150 * 10**6, transcendentals=0),
-    )(slots, table)
+    )(slots, ranks, table)
 
 
 def call_loss(rows, picks, labels, weights):
     return pl.pallas_call(
         loss_kernel,
         out_shape=jax.ShapeDtypeStruct((1, TARGETS), F32),
-        in_specs=[VMEM] * 4,
+        in_specs=[VMEM] * 3 + [pl.BlockSpec(memory_space=pl.ANY)],
         out_specs=VMEM,
         scratch_shapes=[
             pltpu.VMEM((TARGETS, 2 * HIDDEN), BF16),
             pltpu.VMEM((2, TARGETS, weights.shape[2]), F32),
+            pltpu.VMEM(weights.shape, BF16),
+            pltpu.SemaphoreType.DMA((NODE,)),
         ],
-        compiler_params=pltpu.CompilerParams(vmem_limit_bytes=24 * 2**20),
+        compiler_params=pltpu.CompilerParams(vmem_limit_bytes=56 * 2**20),
     )(rows, picks, labels, weights)
 
 
@@ -271,8 +368,6 @@
     first_bias,
     class_weight,
 ):
-    slots = jnp.where(first_mask[:, 0, :] > 0, first_neighbours[:, 0, :], INPUTS)
-    slots = slots.reshape(FAN, ROWS // CHUNK, CHUNK).transpose(1, 0, 2).reshape(-1)
     core = lax.rem(lax.axis_index("node"), 2).astype(jnp.int32)
     half = lax.dynamic_slice(first_weight, (0, 0, core * 128), (2, WIDTH, 128))
     all_class = lax.all_gather(class_weight, "node", axis=0)
@@ -298,7 +393,8 @@
         cost_estimate=pl.CostEstimate(flops=10**8, bytes_accessed=3 * 10**6, transcendentals=0),
     )(table, half.reshape(2 * WIDTH, 128), second_neighbours, target_index)
     own = lax.all_to_all(own, "feat", 0, 0)
-    send = call_gather(slots, table)
+    slots, ranks = call_order(first_neighbours, first_mask)
+    send = call_gather(slots.reshape(-1), ranks, table)
     swap = [(device, device ^ 1) for device in range(NODE)]
     theirs = lax.ppermute(own[:, : 2 * WIDTH], "node", swap)
     means = lax.all_to_all(send, "feat", 0, 0)

time: 134 us -> 122 us (0.910)
  the two profiles are of different devices: /device:TPU:1 before, /device:TPU:2 now
where the time goes in v4:
time: 122 us; the launch traced here: 121 us
  Pallas kernels  44.3 us (36%)
  waiting for transfers between devices  30.2 us (25%)
  starting transfers between devices  26.4 us (22%)
  between operations  14.2 us (12%)
  local copies, waits for them, and re-layouts  5.79 us (5%)
    pallas_call x1, Pallas kernels, call_gather(): pl.pallas_call(gather_kernel, out_shape=jax.ShapeDtypeStruct((FEAT, 64, 1...  28.8 us
    all_to_all x1, waiting for transfers between devices, body(): means = lax.all_to_all(send, 'feat', 0, 0)  17.3 us
    all_to_all x1, waiting for transfers between devices, body(): rows = lax.all_to_all(rows.reshape(FEAT, UNION, HIDDEN), 'feat', 0, 0)  12.3 us
    all_to_all x1, starting transfers between devices, body(): own = lax.all_to_all(own, 'feat', 0, 0)  11.6 us
    all_to_all x1, starting transfers between devices, body(): means = lax.all_to_all(send, 'feat', 0, 0)  9.9 us
    pallas_call x1, Pallas kernels, call_loss(): pl.pallas_call(loss_kernel, out_shape=jax.ShapeDtypeStruct((1, TARGETS),...  7.08 us
    unnamed x24, local copies, waits for them, and re-layouts  5.73 us
    all_to_all x1, starting transfers between devices, body(): rows = lax.all_to_all(rows.reshape(FEAT, UNION, HIDDEN), 'feat', 0, 0)  4.77 us
  transfers between devices with their start and end apart: 5, of which 2 were waited for; matrix products, arithmetic and copies ran while one was open for 0% of the time, Pallas kernels for 28%

profile of v4, /device:TPU:2, one launch (start us, length us, event | category | flops | bytes accessed | tf_op | source)
XLA Modules:
  0.0 121.1 jit_solution(2132628753954184778)
XLA Ops:
  7.2 0.0 copy-start
  7.2 0.0 copy-start.8
  7.2 0.0 copy-start.10
  7.2 0.0 all-gather.3.cloned.1.call-start
  7.2 0.7 all-gather.3.cloned.1.call-update
  7.9 0.0 copy-done
  8.0 0.0 copy-done.8
  8.0 0.0 copy-done.10
  8.0 0.0 copy-start.1
  8.0 1.5 %copy-done.1 = bf16[40,1,24576]{2,0,1:T(8,128)(2,1)S(1)} copy-done((bf16[40,1,24576]{2,0,1:T(8,128)(2,1)S(1)}, bf16[40,1,24576]{2,0,1:T(8,128)(2,1)}, u32[]{:S(2)}) %copy-start.1) | copy-done | bytes 1966104
  9.5 1.6 %shard_map.113 = (bf16[32,144,128]{2,1,0:T(8,128)(2,1)S(1)}, s32[16,128]{1,0:T(8,128)S(1)}) custom-call(bf16[40,24576]{1,0:T(8,128)(2,1)S(1)} %bitcast.12, bf16[80,128]{1,0:T(8,128)(2,1)S(1)} %bitcast.16, s32[10,1,128]{2,1,0:T(1,128)S(1)} %copy-done.8, s32[1,128]{1,0:T(1,128)S(1)} %copy-done.10), custom_call_target="tpu_custom_call" | custom-call | flops 100000000 | bytes 3000000 | tf_op jit(solution)/shard_map/pallas_call | solution.py:375
  11.2 1.0 copy-done.3
  12.2 0.6 copy-done.7
  12.8 11.6 %all-to-all-start = ((bf16[32,144,128]{2,1,0:T(8,128)(2,1)}), bf16[32,144,128]{2,1,0:T(8,128)(2,1)S(1)}, u32[]{:S(2)}, u32[]{:S(2)}) async-start(bf16[32,144,128]{2,1,0:T(8,128)(2,1)} %copy-done.3), calls=%async_computation | async-start | bytes 2359296 | tf_op jit(solution)/shard_map/all_to_all | solution.py:395
  24.4 0.0 copy-start.6
  24.4 1.0 copy-done.6
  25.4 2.1 %shard_map.114 = (s32[528,128]{1,0:T(8,128)S(1)}, s32[48,128]{1,0:T(8,128)S(1)}) custom-call(s32[10,48,128]{2,1,0:T(8,128)S(1)} %bitcast.14, s32[10,48,128]{2,1,0:T(8,128)S(1)} %bitcast.15), custom_call_target="tpu_custom_call" | custom-call | flops 100000000 | bytes 10000000 | tf_op jit(solution)/shard_map/pallas_call | solution.py:312
  27.6 0.0 copy-done.2
  27.6 28.8 %shard_map.115 = bf16[32,64,128]{2,1,0:T(8,128)(2,1)S(1)} custom-call(s32[67584]{0:T(1024)S(1)} %bitcast.18, s32[48,128]{1,0:T(8,128)S(1)} %get-tuple-element.12.ranks, bf16[40,24576]{1,0:T(8,128)(2,1)S(1)} %bitcast.13), custom_call_target="tpu_custom_call" | custom-call | flops 1000000000 | bytes 150000000 | tf_op jit(solution)/shard_map/pallas_call | solution.py:327
  56.4 0.8 copy-done.4
  57.2 0.0 all-to-all-done.mine
  57.2 9.9 %all-to-all-start.1 = ((bf16[32,64,128]{2,1,0:T(8,128)(2,1)}), bf16[32,64,128]{2,1,0:T(8,128)(2,1)S(1)}, u32[]{:S(2)}, u32[]{:S(2)}) async-start(bf16[32,64,128]{2,1,0:T(8,128)(2,1)} %copy-done.4), calls=%async_computation.1 | async-start | bytes 1048576 | tf_op jit(solution)/shard_map/all_to_all | solution.py:400
  67.1 0.1 collective-permute-start
  67.2 0.1 pad_add_fusion.spot
  67.3 17.3 %all-to-all-done.1.means = bf16[32,64,128]{2,1,0:T(8,128)(2,1)S(1)} async-done(((bf16[32,64,128]{2,1,0:T(8,128)(2,1)}), bf16[32,64,128]{2,1,0:T(8,128)(2,1)S(1)}, u32[]{:S(2)}, u32[]{:S(2)}) %all-to-all-start.1) | async-done | bytes 524320 | tf_op jit(solution)/shard_map/all_to_all | solution.py:400
  84.6 0.0 collective-permute-done.theirs
  84.6 2.8 %shard_map.116 = (bf16[192,256]{1,0:T(8,128)(2,1)}, bf16[768,256]{1,0:T(8,128)(2,1)}) custom-call(s32[2]{0:T(128)S(1)} %pad_add_fusion.spot, bf16[32,144,128]{2,1,0:T(8,128)(2,1)S(1)} %all-to-all-done.mine, bf16[32,80,128]{2,1,0:T(8,128)(2,1)S(1)} %collective-permute-done.theirs, bf16[32,64,128]{2,1,0:T(8,128)(2,1)S(1)} %all-to-all-done.1.means, ...), custom_call_target="tpu_custom_call" | custom-call | tf_op jit(solution)/shard_map/pallas_call | solution.py:403
  87.4 4.8 %all-to-all-start.2 = ((bf16[32,24,256]{2,1,0:T(8,128)(2,1)}), bf16[32,24,256]{2,1,0:T(8,128)(2,1)S(1)}, u32[]{:S(2)}, u32[]{:S(2)}) async-start(bf16[32,24,256]{2,1,0:T(8,128)(2,1)} %bitcast.10), calls=%async_computation.2 | async-start | bytes 786432 | tf_op jit(solution)/shard_map/all_to_all | solution.py:420
  92.2 1.9 %shard_map.117.picks = bf16[2,768,128]{2,1,0:T(8,128)(2,1)} custom-call(s32[16,128]{1,0:T(8,128)} %copy-done.7, s32[10,1,128]{2,1,0:T(1,128)} %mask.1), custom_call_target="tpu_custom_call" | custom-call | flops 10000000 | bytes 4000000 | tf_op jit(solution)/shard_map/pallas_call | solution.py:422
  94.1 12.3 %all-to-all-done.2 = bf16[32,24,256]{2,1,0:T(8,128)(2,1)S(1)} async-done(((bf16[32,24,256]{2,1,0:T(8,128)(2,1)}), bf16[32,24,256]{2,1,0:T(8,128)(2,1)S(1)}, u32[]{:S(2)}, u32[]{:S(2)}) %all-to-all-start.2) | async-done | bytes 393248 | tf_op jit(solution)/shard_map/all_to_all | solution.py:420
  106.4 0.8 copy-done.11
  107.1 7.1 %shard_map.118 = f32[1,128]{1,0:T(1,128)} custom-call(bf16[768,256]{1,0:T(8,128)(2,1)} %bitcast.20, bf16[2,768,128]{2,1,0:T(8,128)(2,1)} %shard_map.117.picks, s32[1,128]{1,0:T(1,128)} %labels.1, bf16[8,512,1280]{2,1,0:T(8,128)(2,1)} %bitcast.19), custom_call_target="tpu_custom_call" | custom-call | tf_op jit(solution)/shard_map/pallas_call | solution.py:344
  (12 shorter events, 0.1 us)
Async XLA Ops:
  7.2 0.8 copy-start
  7.2 0.8 copy-start.8
  7.2 0.8 copy-start.10
  7.2 77.4 %all-gather.3.cloned.1.call-start = ((), (), s32[]{:S(2)}) async-start(), calls=%async_computation.3 | async-start | bytes 11796480 | tf_op jit(solution)/shard_map/all_gather | solution.py:373
  8.0 1.5 %copy-start.1 = (bf16[40,1,24576]{2,0,1:T(8,128)(2,1)S(1)}, bf16[40,1,24576]{2,0,1:T(8,128)(2,1)}, u32[]{:S(2)}) copy-start(bf16[40,1,24576]{2,0,1:T(8,128)(2,1)} %param.10) | copy-start | bytes 5898244
  11.2 1.0 copy-start.3
  12.2 0.6 copy-start.7
  12.8 11.6 %copy-start.5 = (s32[10,1,6144]{2,1,0:T(1,128)S(1)}, s32[10,1,6144]{2,1,0:T(1,128)}, u32[]{:S(2)}) copy-start(s32[10,1,6144]{2,1,0:T(1,128)} %param.11) | copy-start | bytes 737284
  12.8 14.8 %copy-start.2 = (bf16[40,1,24576]{2,0,1:T(8,128)(2,1)S(1)}, bf16[40,1,24576]{2,0,1:T(8,128)(2,1)}, u32[]{:S(2)}) copy-start(bf16[40,1,24576]{2,0,1:T(8,128)(2,1)} %param.10) | copy-start | bytes 5898244
  12.8 44.4 %all-to-all-start = ((bf16[32,144,128]{2,1,0:T(8,128)(2,1)}), bf16[32,144,128]{2,1,0:T(8,128)(2,1)S(1)}, u32[]{:S(2)}, u32[]{:S(2)}) async-start(bf16[32,144,128]{2,1,0:T(8,128)(2,1)} %copy-done.3), calls=%async_computation | async-start | bytes 2359296 | tf_op jit(solution)/shard_map/all_to_all | solution.py:395
  24.4 1.0 copy-start.6
  56.3 0.8 copy-start.4
  57.2 27.4 %copy-start.9 = (f32[256]{0:T(256)S(1)}, f32[256]{0:T(256)}, u32[]{:S(2)}) copy-start(f32[256]{0:T(256)} %param.18) | copy-start | bytes 3076
  57.2 27.4 %all-to-all-start.1 = ((bf16[32,64,128]{2,1,0:T(8,128)(2,1)}), bf16[32,64,128]{2,1,0:T(8,128)(2,1)S(1)}, u32[]{:S(2)}, u32[]{:S(2)}) async-start(bf16[32,64,128]{2,1,0:T(8,128)(2,1)} %copy-done.4), calls=%async_computation.1 | async-start | bytes 1048576 | tf_op jit(solution)/shard_map/all_to_all | solution.py:400
  67.1 17.4 %collective-permute-start = (bf16[32,80,128]{2,1,0:T(8,128)(2,1)S(1)}, bf16[32,80,128]{2,1,0:T(8,128)(2,1)S(1)}, u32[]{:S(2)}, u32[]{:S(2)}) collective-permute-start(bf16[32,80,128]{2,1,0:T(8,128)(2,1)S(1)} %slice.4), channel_id=1, source_target_pairs={{0,1},{1,0},{2,3},{3,2},{4,5},{5,4},{6,7},{7,6},{8,9},{9,8},{10,11... | collective-permute-start | bytes 1966088 | tf_op jit(solution)/shard_map/ppermute | solution.py:399
  87.4 18.9 %all-to-all-start.2 = ((bf16[32,24,256]{2,1,0:T(8,128)(2,1)}), bf16[32,24,256]{2,1,0:T(8,128)(2,1)S(1)}, u32[]{:S(2)}, u32[]{:S(2)}) async-start(bf16[32,24,256]{2,1,0:T(8,128)(2,1)} %bitcast.10), calls=%async_computation.2 | async-start | bytes 786432 | tf_op jit(solution)/shard_map/all_to_all | solution.py:420
  106.4 0.8 copy-start.11
Sparse Core Ops, SparseCore 0:
  9.9 63.3 all-gather.2

commit v5 on v4

--- a/solution.py
+++ b/solution.py
@@ -24,6 +24,7 @@
 CHUNK = 1024
 PAIRS = 4
 TABLE_STEP = 8
+STAGED = [(0, 0), (1, 0), (2, 0), (3, 0), (3, 256), (4, 0), (5, 0), (6, 0), (7, 0), (7, 256)]
 F32 = jnp.float32
 BF16 = jnp.bfloat16
 
@@ -47,7 +48,7 @@
     return terms[0]
 
 
-def send_kernel(features, weights, neighbours, targets, send, place):
+def send_kernel(features, weights, neighbours, targets, send, place, built, sent):
     owners, lanes = [], []
     named = jnp.zeros((FEAT, SLAB), F32)
     for slot in range(FAN + 1):
@@ -75,7 +76,16 @@
             owner = 2 * pair + half
             marks = [marked[owner : owner + 1, k * 64 : (k + 1) * 64] for k in range(3)]
             last = jnp.concatenate(marks + [jnp.zeros((5, 64), F32)], axis=0)
-            send[owner] = jnp.concatenate([shared, folded(block, half, last)], axis=0).astype(BF16)
+            built[owner] = jnp.concatenate([shared, folded(block, half, last)], axis=0).astype(BF16)
+        if pair % 4 == 3:
+            copies_out(built, send, sent, pair // 4).start()
+    for step in range(FEAT // 8):
+        copies_out(built, send, sent, step).wait()
+
+
+def copies_out(built, send, sent, step):
+    span = pl.ds(step * 8, 8)
+    return pltpu.make_async_copy(built.at[span], send.at[span], sent.at[step])
 
 
 def folded(block, half, last):
@@ -135,7 +145,9 @@
     return (thirds[0] + thirds[1] + thirds[2]) / jnp.maximum(flipped[3 * WIDTH : 3 * WIDTH + 1], 1.0)
 
 
-def gather_kernel(slots, ranks, features, send, table, sums, lists, arrived):
+def gather_kernel(
+    slots, ranks, features, send, table, sums, lists, built, arrived, sent
+):
     size = (FAN + 1) * CHUNK
 
     def fetch(chunk):
@@ -210,10 +222,13 @@
                 owner = 2 * (step * PAIRS + part + pair)
                 for half in range(2):
                     tile = folded(block, half, jnp.zeros((8, 64), F32))
-                    send[owner + half] = tile.astype(BF16)
+                    built[owner + half] = tile.astype(BF16)
+        copies_out(built, send, sent, step).start()
         return carry
 
     lax.fori_loop(0, FEAT // 2 // PAIRS, pair_step, 0)
+    for step in range(FEAT // 8):
+        copies_out(built, send, sent, step).wait()
 
 
 def hidden_kernel(
@@ -254,7 +269,14 @@
     rows[...] = contract(chosen[...].astype(BF16), padded, 1, 0).astype(BF16)
 
 
-def pick_kernel(place, mask, picks):
+def stage_kernel(place, mask, *refs):
+    blocks, (picks, held, arrived) = refs[:-3], refs[-3:]
+    copies = []
+    for block in blocks:
+        slot, first = STAGED[len(copies)]
+        span = held.at[slot, pl.ds(first, block.shape[0]), :]
+        copies.append(pltpu.make_async_copy(block, span, arrived.at[len(copies)]))
+        copies[-1].start()
     spots = iota((FEAT * UNION, TARGETS), 0)
     total = jnp.zeros((FEAT * UNION, TARGETS), F32)
     for slot in range(FAN):
@@ -262,14 +284,11 @@
         total = total + jnp.where(spots == place[pl.ds(slot, 1), :], used, 0.0)
     picks[0] = total.astype(BF16)
     picks[1] = jnp.where(spots == place[pl.ds(FAN, 1), :], 1.0, 0.0).astype(BF16)
-
-
-def loss_kernel(rows, picks, labels, weights, loss, inputs, logits, held, arrived):
-    copies = [
-        pltpu.make_async_copy(weights.at[k], held.at[k], arrived.at[k]) for k in range(NODE)
-    ]
     for copy in copies:
-        copy.start()
+        copy.wait()
+
+
+def loss_kernel(bases, rows, picks, labels, held, loss, inputs, logits):
     count = contract(picks[0], jnp.ones((FEAT * UNION, 128), BF16), 0, 0)[:, :1]
     agg = contract(picks[0], rows[...], 0, 0) / jnp.maximum(count, 1.0)
     inputs[:, pl.ds(0, HIDDEN)] = contract(picks[1], rows[...], 0, 0).astype(BF16)
@@ -278,17 +297,17 @@
         jnp.broadcast_to(labels[...].astype(F32), (TARGETS, TARGETS)).T.astype(jnp.int32)
         - iota((TARGETS, TARGETS), 1)
     )
-    width = weights.shape[2]
+    width = held.shape[2]
     largest = jnp.full((TARGETS, TARGETS), -jnp.inf, F32)
     summed = jnp.zeros((TARGETS, TARGETS), F32)
     picked = jnp.zeros((TARGETS, TARGETS), F32)
     for step in range(NODE + 1):
         if step < NODE:
-            copies[step].wait()
             logits[step % 2] = contract(inputs[...], held[step], 1, 0)
         if step > 0:
             spans = [pl.ds(k * 128, 128) for k in range(width // 128)]
             last = logits.at[(step - 1) % 2]
+            here = offset - bases[step - 1]
             now = largest
             for span in spans:
                 now = jnp.maximum(now, last[:, span])
@@ -296,7 +315,7 @@
             for k, span in enumerate(spans):
                 part = last[:, span]
                 summed = summed + jnp.exp(part - now)
-                picked = picked + jnp.where(offset == (step - 1) * width + k * 128, part, 0.0)
+                picked = picked + jnp.where(here == k * 128, part, 0.0)
             largest = now
     most = jnp.max(largest, axis=1, keepdims=True)
     total = jnp.sum(summed * jnp.exp(largest - most), axis=1, keepdims=True)
@@ -305,6 +324,7 @@
 
 
 VMEM = pl.BlockSpec(memory_space=pltpu.VMEM)
+HBM = pl.BlockSpec(memory_space=pltpu.HBM)
 SMEM = pl.BlockSpec(memory_space=pltpu.SMEM)
 
 
@@ -328,32 +348,48 @@
         gather_kernel,
         out_shape=jax.ShapeDtypeStruct((FEAT, 64, 128), BF16),
         in_specs=[pl.BlockSpec(memory_space=pl.ANY), VMEM, VMEM],
-        out_specs=VMEM,
+        out_specs=HBM,
         scratch_shapes=[
             pltpu.VMEM((INPUTS + 8, 128), F32),
             pltpu.VMEM((ROWS, 128), F32),
             pltpu.SMEM(((FAN + 1) * ROWS,), jnp.int32),
+            pltpu.VMEM((FEAT, 64, 128), BF16),
             pltpu.SemaphoreType.DMA((ROWS // CHUNK,)),
+            pltpu.SemaphoreType.DMA((FEAT // 8,)),
         ],
         compiler_params=pltpu.CompilerParams(vmem_limit_bytes=24 * 2**20),
-        cost_estimate=pl.CostEstimate(flops=10**9, bytes_accessed=150 * 10**6, transcendentals=0),
+        cost_estimate=pl.CostEstimate(flops=10**9, bytes_accessed=90 * 10**6, transcendentals=0),
     )(slots, ranks, table)
 
 
-def call_loss(rows, picks, labels, weights):
+def call_stage(place, mask, blocks):
+    width = blocks[0].shape[1]
+    return pl.pallas_call(
+        stage_kernel,
+        out_shape=(
+            jax.ShapeDtypeStruct((2, FEAT * UNION, TARGETS), BF16),
+            jax.ShapeDtypeStruct((NODE, 2 * HIDDEN, width), BF16),
+        ),
+        in_specs=[VMEM] * 2 + [HBM] * len(blocks),
+        out_specs=(VMEM, VMEM),
+        scratch_shapes=[pltpu.SemaphoreType.DMA((len(blocks),))],
+        compiler_params=pltpu.CompilerParams(vmem_limit_bytes=16 * 2**20),
+        cost_estimate=pl.CostEstimate(flops=10**7, bytes_accessed=20 * 10**6, transcendentals=0),
+    )(place, mask, *blocks)
+
+
+def call_loss(bases, rows, picks, labels, held):
     return pl.pallas_call(
         loss_kernel,
         out_shape=jax.ShapeDtypeStruct((1, TARGETS), F32),
-        in_specs=[VMEM] * 3 + [pl.BlockSpec(memory_space=pl.ANY)],
+        in_specs=[SMEM] + [VMEM] * 4,
         out_specs=VMEM,
         scratch_shapes=[
             pltpu.VMEM((TARGETS, 2 * HIDDEN), BF16),
-            pltpu.VMEM((2, TARGETS, weights.shape[2]), F32),
-            pltpu.VMEM(weights.shape, BF16),
-            pltpu.SemaphoreType.DMA((NODE,)),
+            pltpu.VMEM((2, TARGETS, held.shape[2]), F32),
         ],
-        compiler_params=pltpu.CompilerParams(vmem_limit_bytes=56 * 2**20),
-    )(rows, picks, labels, weights)
+        compiler_params=pltpu.CompilerParams(vmem_limit_bytes=16 * 2**20),
+    )(bases, rows, picks, labels, held)
 
 
 def body(
@@ -368,38 +404,46 @@
     first_bias,
     class_weight,
 ):
-    core = lax.rem(lax.axis_index("node"), 2).astype(jnp.int32)
+    spot = lax.axis_index("node").astype(jnp.int32)
+    core = spot & 1
     half = lax.dynamic_slice(first_weight, (0, 0, core * 128), (2, WIDTH, 128))
-    all_class = lax.all_gather(class_weight, "node", axis=0)
     table = features[:, 0, :]
+    slots, ranks = call_order(first_neighbours, first_mask)
+    up = [(device, (device + 2) % NODE) for device in range(NODE)]
+    down = [(device, (device - 2) % NODE) for device in range(NODE)]
+    swap = [(device, device ^ 1) for device in range(NODE)]
+    below = lax.ppermute(class_weight, "node", up)
+    above = lax.ppermute(class_weight, "node", down)
+    swapped = [lax.ppermute(class_weight, "node", swap)]
+    table, slots, ranks = lax.optimization_barrier((table, slots, ranks))
     own, place = pl.pallas_call(
         send_kernel,
         out_shape=(
             jax.ShapeDtypeStruct((FEAT, 144, 128), BF16),
             jax.ShapeDtypeStruct((16, TARGETS), jnp.int32),
         ),
-        grid=(1,),
-        in_specs=[
-            pl.BlockSpec((WIDTH, ROWS), lambda i: (0, 0)),
-            pl.BlockSpec((2 * WIDTH, 128), lambda i: (0, 0)),
-            pl.BlockSpec((FAN, 1, TARGETS), lambda i: (0, 0, 0)),
-            pl.BlockSpec((1, TARGETS), lambda i: (0, 0)),
+        in_specs=[VMEM] * 4,
+        out_specs=(HBM, VMEM),
+        scratch_shapes=[
+            pltpu.VMEM((FEAT, 144, 128), BF16),
+            pltpu.SemaphoreType.DMA((FEAT // 8,)),
         ],
-        out_specs=(
-            pl.BlockSpec((FEAT, 144, 128), lambda i: (0, 0, 0)),
-            pl.BlockSpec((16, TARGETS), lambda i: (0, 0)),
-        ),
-        compiler_params=pltpu.CompilerParams(vmem_limit_bytes=24 * 2**20),
+        compiler_params=pltpu.CompilerParams(vmem_limit_bytes=16 * 2**20),
         cost_estimate=pl.CostEstimate(flops=10**8, bytes_accessed=3 * 10**6, transcendentals=0),
     )(table, half.reshape(2 * WIDTH, 128), second_neighbours, target_index)
     own = lax.all_to_all(own, "feat", 0, 0)
-    slots, ranks = call_order(first_neighbours, first_mask)
     send = call_gather(slots.reshape(-1), ranks, table)
-    swap = [(device, device ^ 1) for device in range(NODE)]
+    send, below, above, own = lax.optimization_barrier((send, below, above, own))
+    far = [
+        lax.ppermute(below[:HIDDEN], "node", up),
+        lax.ppermute(above[HIDDEN:], "node", down),
+    ]
+    swapped += [lax.ppermute(below, "node", swap), lax.ppermute(above, "node", swap)]
     theirs = lax.ppermute(own[:, : 2 * WIDTH], "node", swap)
     means = lax.all_to_all(send, "feat", 0, 0)
-    means, all_class = lax.optimization_barrier((means, all_class))
-    spot = jnp.stack([core, lax.rem(lax.axis_index("feat"), 2).astype(jnp.int32)])
+    means, far = lax.optimization_barrier((means, far))
+    swapped += [lax.ppermute(part, "node", swap) for part in far]
+    side = jnp.stack([core, lax.axis_index("feat").astype(jnp.int32) & 1])
     hidden, rows = pl.pallas_call(
         hidden_kernel,
         out_shape=(
@@ -416,17 +460,13 @@
             pltpu.VMEM((FEAT * UNION, SLAB), F32),
         ],
         compiler_params=pltpu.CompilerParams(vmem_limit_bytes=24 * 2**20),
-    )(spot, own, theirs, means, first_bias[None, :])
+    )(side, own, theirs, means, first_bias[None, :])
     rows = lax.all_to_all(rows.reshape(FEAT, UNION, HIDDEN), "feat", 0, 0)
     rows = rows.reshape(FEAT * UNION, HIDDEN)
-    picks = pl.pallas_call(
-        pick_kernel,
-        out_shape=jax.ShapeDtypeStruct((2, FEAT * UNION, TARGETS), BF16),
-        in_specs=[VMEM] * 2,
-        out_specs=VMEM,
-        cost_estimate=pl.CostEstimate(flops=10**7, bytes_accessed=4 * 10**6, transcendentals=0),
-    )(place, second_mask)
-    loss = call_loss(rows, picks, labels, all_class)
+    picks, held = call_stage(place, second_mask, [class_weight, below, above, *far, *swapped])
+    order = jnp.stack([spot, spot + 6, spot + 2, spot + 4]) & 7
+    bases = jnp.concatenate([order, order ^ 1]) * class_weight.shape[1]
+    loss = call_loss(bases, rows, picks, labels, held)
     return (hidden[None], loss)
 
 

time: 122 us -> 122 us (level)
  the two profiles are of different devices: /device:TPU:2 before, /device:TPU:1 now
where the time goes in v5:
time: 122 us; the launch traced here: 121 us
  Pallas kernels  44.8 us (37%)
  starting transfers between devices  42.5 us (35%)
  local copies, waits for them, and re-layouts  19 us (16%)
  waiting for transfers between devices  14 us (11%)
    pallas_call x1, Pallas kernels, call_gather(): pl.pallas_call(gather_kernel, out_shape=jax.ShapeDtypeStruct((FEAT, 64, 1...  29.7 us
    unnamed x26, local copies, waits for them, and re-layouts  15.1 us
    all_to_all x1, starting transfers between devices, body(): own = lax.all_to_all(own, 'feat', 0, 0)  12 us
    ppermute x1, waiting for transfers between devices, body(): lax.ppermute(below[:HIDDEN], 'node', up)  11.3 us
    all_to_all x1, starting transfers between devices, body(): means = lax.all_to_all(send, 'feat', 0, 0)  9.21 us
    all_to_all x1, starting transfers between devices, body(): rows = lax.all_to_all(rows.reshape(FEAT, UNION, HIDDEN), 'feat', 0, 0)  8.93 us
    ppermute x2, starting transfers between devices, body(): swapped += [lax.ppermute(part, 'node', swap) for part in far]  4.03 us
    pallas_call x1, Pallas kernels, call_loss(): pl.pallas_call(loss_kernel, out_shape=jax.ShapeDtypeStruct((1, TARGETS),...  3.82 us
  transfers between devices with their start and end apart: 13, of which 3 were waited for; matrix products, arithmetic and copies ran while one was open for 3% of the time, Pallas kernels for 30%

profile of v5, /device:TPU:1, one launch (start us, length us, event | category | flops | bytes accessed | tf_op | source)
XLA Modules:
  0.0 121.2 jit_solution(1143589524340892409)
XLA Ops:
  0.7 0.9 copy-done.6
  1.6 0.9 copy-done.7
  2.5 2.1 %shard_map.113 = (s32[528,128]{1,0:T(8,128)S(1)}, s32[48,128]{1,0:T(8,128)S(1)}) custom-call(s32[10,48,128]{2,1,0:T(8,128)S(1)} %bitcast.18, s32[10,48,128]{2,1,0:T(8,128)S(1)} %bitcast.19), custom_call_target="tpu_custom_call" | custom-call | flops 100000000 | bytes 10000000 | tf_op jit(solution)/shard_map/pallas_call | solution.py:332
  4.7 1.5 %copy-done.3 = bf16[40,1,24576]{2,0,1:T(8,128)(2,1)S(1)} copy-done((bf16[40,1,24576]{2,0,1:T(8,128)(2,1)S(1)}, bf16[40,1,24576]{2,0,1:T(8,128)(2,1)}, u32[]{:S(2)}) %copy-start.3) | copy-done | bytes 1966104
  6.3 0.7 copy-done.8
  7.0 0.7 copy-done.12
  7.6 2.4 %shard_map.115 = (bf16[32,144,128]{2,1,0:T(8,128)(2,1)}, s32[16,128]{1,0:T(8,128)S(1)}) custom-call(bf16[40,24576]{1,0:T(8,128)(2,1)S(1)} %bitcast.15, bf16[80,128]{1,0:T(8,128)(2,1)S(1)} %bitcast.20, s32[10,1,128]{2,1,0:T(1,128)S(1)} %copy-done.8, s32[1,128]{1,0:T(1,128)S(1)} %copy-done.12), custom_call_target="tpu_custom_call" | custom-call | flops 100000000 | bytes 3000000 | tf_op jit(solution)/shard_map/pallas_call | solution.py:419
  10.0 12.0 %all-to-all-start = ((bf16[32,144,128]{2,1,0:T(8,128)(2,1)}), bf16[32,144,128]{2,1,0:T(8,128)(2,1)S(1)}, u32[]{:S(2)}, u32[]{:S(2)}) async-start(bf16[32,144,128]{2,1,0:T(8,128)(2,1)} %get-tuple-element.25), calls=%async_computation | async-start | bytes 2359296 | tf_op jit(solution)/shard_map/all_to_all | solution.py:434
  22.0 2.6 %collective-permute-start.1 = (bf16[512,1280]{1,0:T(8,128)(2,1)}, bf16[512,1280]{1,0:T(8,128)(2,1)S(1)}, u32[]{:S(2)}, u32[]{:S(2)}) collective-permute-start(bf16[512,1280]{1,0:T(8,128)(2,1)} %refs_0_.1), channel_id=1, source_target_pairs={{0,6},{1,7},{2,0},{3,1},{4,2},{5,3},{6,4},{7,5},{8,14},{9,15},{10,... | collective-permute-start | bytes 3932168 | tf_op jit(solution)/shard_map/ppermute | solution.py:416
  24.6 1.5 %copy-done.4 = bf16[40,1,24576]{2,0,1:T(8,128)(2,1)S(1)} copy-done((bf16[40,1,24576]{2,0,1:T(8,128)(2,1)S(1)}, bf16[40,1,24576]{2,0,1:T(8,128)(2,1)}, u32[]{:S(2)}) %copy-start.4) | copy-done | bytes 1966104
  26.1 29.7 %shard_map.114 = bf16[32,64,128]{2,1,0:T(8,128)(2,1)S(1)} custom-call(s32[67584]{0:T(1024)S(1)} %bitcast.22, s32[48,128]{1,0:T(8,128)S(1)} %get-tuple-element.23.ranks, bf16[40,24576]{1,0:T(8,128)(2,1)S(1)} %bitcast.16), custom_call_target="tpu_custom_call" | custom-call | flops 1000000000 | bytes 90000000 | tf_op jit(solution)/shard_map/pallas_call | solution.py:347
  55.8 0.8 copy-done.5
  56.7 0.9 slice.11
  57.6 2.6 %collective-permute-start.4 = (bf16[256,1280]{1,0:T(8,128)(2,1)}, bf16[256,1280]{1,0:T(8,128)(2,1)}, u32[]{:S(2)}, u32[]{:S(2)}) collective-permute-start(bf16[256,1280]{1,0:T(8,128)(2,1)} %slice.11), channel_id=1, source_target_pairs={{0,6},{1,7},{2,0},{3,1},{4,2},{5,3},{6,4},{7,5},{8,14},{9,15},{10,... | collective-permute-start | bytes 1966088 | tf_op jit(solution)/shard_map/ppermute | solution.py:439
  60.2 9.2 %all-to-all-start.1 = ((bf16[32,64,128]{2,1,0:T(8,128)(2,1)}), bf16[32,64,128]{2,1,0:T(8,128)(2,1)S(1)}, u32[]{:S(2)}, u32[]{:S(2)}) async-start(bf16[32,64,128]{2,1,0:T(8,128)(2,1)} %copy-done.5), calls=%async_computation.1 | async-start | bytes 1048576 | tf_op jit(solution)/shard_map/all_to_all | solution.py:443
  69.4 2.0 %slice.10 = bf16[256,1280]{1,0:T(8,128)(2,1)} slice(bf16[512,1280]{1,0:T(8,128)(2,1)} %collective-permute-done.refs_1_), slice={[0:256], [0:1280]} | slice | bytes 1310720 | tf_op jit(solution)/shard_map/slice | solution.py:438
  71.4 0.9 slice.9
  72.3 2.4 %collective-permute-start.2 = (bf16[32,80,128]{2,1,0:T(8,128)(2,1)}, bf16[32,80,128]{2,1,0:T(8,128)(2,1)}, u32[]{:S(2)}, u32[]{:S(2)}) collective-permute-start(bf16[32,80,128]{2,1,0:T(8,128)(2,1)} %slice.9), channel_id=1, source_target_pairs={{0,1},{1,0},{2,3},{3,2},{4,5},{5,4},{6,7},{7,6},{8,9},{9,8},{10,11... | collective-permute-start | bytes 1966088 | tf_op jit(solution)/shard_map/ppermute | solution.py:442
  74.7 0.5 collective-permute-start.6
  75.2 0.2 collective-permute-start.7
  75.5 11.3 %collective-permute-done.3.refs_3_ = bf16[256,1280]{1,0:T(8,128)(2,1)} collective-permute-done((bf16[256,1280]{1,0:T(8,128)(2,1)}, bf16[256,1280]{1,0:T(8,128)(2,1)}, u32[]{:S(2)}, u32[]{:S(2)}) %collective-permute-start.3) | collective-permute-done | bytes 655392 | tf_op jit(solution)/shard_map/ppermute | solution.py:438
  86.9 3.4 %shard_map.116 = (bf16[192,256]{1,0:T(8,128)(2,1)}, bf16[768,256]{1,0:T(8,128)(2,1)}) custom-call(s32[2]{0:T(128)S(1)} %pad_add_fusion.spot, bf16[32,144,128]{2,1,0:T(8,128)(2,1)S(1)} %all-to-all-done.mine, bf16[32,80,128]{2,1,0:T(8,128)(2,1)} %collective-permute-done.2.theirs, bf16[32,64,128]{2,1,0:T(8,128)(2,1)S(1)} %all-to-all-done.1.means, ...), custom_call_target="tpu_custom_call" | custom-call | tf_op jit(solution)/shard_map/pallas_call | solution.py:447
  90.2 8.9 %all-to-all-start.2 = ((bf16[32,24,256]{2,1,0:T(8,128)(2,1)}), bf16[32,24,256]{2,1,0:T(8,128)(2,1)S(1)}, u32[]{:S(2)}, u32[]{:S(2)}) async-start(bf16[32,24,256]{2,1,0:T(8,128)(2,1)} %bitcast.13), calls=%async_computation.2 | async-start | bytes 786432 | tf_op jit(solution)/shard_map/all_to_all | solution.py:464
  99.2 3.9 %collective-permute-start.8 = (bf16[256,1280]{1,0:T(8,128)(2,1)}, bf16[256,1280]{1,0:T(8,128)(2,1)S(1)}, u32[]{:S(2)}, u32[]{:S(2)}) collective-permute-start(bf16[256,1280]{1,0:T(8,128)(2,1)} %collective-permute-done.3.refs_3_), channel_id=1, source_target_pairs={{0,1},{1,0},{2,3},{3,2},{4,5},{5,4},{6,7},{7,6},{8,9},{9,8},{10,11... | collective-permute-start | bytes 1966088 | tf_op jit(solution)/shard_map/ppermute | solution.py:445
  103.1 0.1 collective-permute-start.9
  103.2 0.1 broadcast_xor_fusion
  103.4 1.7 %collective-permute-done.8.refs_8_ = bf16[256,1280]{1,0:T(8,128)(2,1)S(1)} collective-permute-done((bf16[256,1280]{1,0:T(8,128)(2,1)}, bf16[256,1280]{1,0:T(8,128)(2,1)S(1)}, u32[]{:S(2)}, u32[]{:S(2)}) %collective-permute-start.8) | collective-permute-done | bytes 655392 | tf_op jit(solution)/shard_map/ppermute | solution.py:445
  105.0 0.9 collective-permute-done.9.refs_9_
  106.0 3.4 %shard_map.117 = (bf16[2,768,128]{2,1,0:T(8,128)(2,1)S(1)}, bf16[8,512,1280]{2,1,0:T(8,128)(2,1)S(1)}) custom-call(s32[16,128]{1,0:T(8,128)S(1)} %get-tuple-element.33.place, s32[10,1,128]{2,1,0:T(1,128)S(1)} %copy-done.9, bf16[512,1280]{1,0:T(8,128)(2,1)} %refs_0_.1, bf16[512,1280]{1,0:T(8,128)(2,1)} %collective-permute-done.refs_1_, ...), custom_call_target="tpu_custom_call" | custom-call | flops 10000000 | bytes 20000000 | tf_op jit(solution)/shard_map/pallas_call | solution.py:367
  109.4 4.0 %copy-done.1 = bf16[8,512,1280]{2,1,0:T(8,128)(2,1)} copy-done((bf16[8,512,1280]{2,1,0:T(8,128)(2,1)}, bf16[8,512,1280]{2,1,0:T(8,128)(2,1)S(1)}, u32[]{:S(2)}) %copy-start.1) | copy-done | bytes 10485784
  113.4 4.0 %copy-done.2 = bf16[8,512,1280]{2,1,0:T(8,128)(2,1)S(1)} copy-done((bf16[8,512,1280]{2,1,0:T(8,128)(2,1)S(1)}, bf16[8,512,1280]{2,1,0:T(8,128)(2,1)}, u32[]{:S(2)}) %copy-start.2) | copy-done | bytes 10485784
  117.4 3.8 %shard_map.118 = f32[1,128]{1,0:T(1,128)} custom-call(s32[8]{0:T(128)S(1)} %add_multiply_fusion.bases, bf16[768,256]{1,0:T(8,128)(2,1)S(1)} %bitcast.17, bf16[2,768,128]{2,1,0:T(8,128)(2,1)S(1)} %get-tuple-element.36.picks, s32[1,128]{1,0:T(1,128)S(1)} %copy-done.11, bf16[8,512,1280]{2,1,0:T(8,128)(2,1)S(1)} %copy-done.2), custom_call_target="tpu_custom_call" | custom-call | tf_op jit(solution)/shard_map/pallas_call | solution.py:382
  (33 shorter events, 0.2 us)
Async XLA Ops:
  0.6 4.1 %copy-start = (bf16[2,40,256]{2,1,0:T(8,128)(2,1)S(1)}, bf16[2,40,256]{2,1,0:T(8,128)(2,1)}, u32[]{:S(2)}) copy-start(bf16[2,40,256]{2,1,0:T(8,128)(2,1)} %param.17) | copy-start | bytes 122884
  0.7 0.9 copy-start.6
  1.6 0.9 copy-start.7
  4.7 1.5 %copy-start.3 = (bf16[40,1,24576]{2,0,1:T(8,128)(2,1)S(1)}, bf16[40,1,24576]{2,0,1:T(8,128)(2,1)}, u32[]{:S(2)}) copy-start(bf16[40,1,24576]{2,0,1:T(8,128)(2,1)} %param.10) | copy-start | bytes 5898244
  6.3 0.7 copy-start.8
  7.0 0.7 copy-start.12
  10.0 46.7 %all-to-all-start = ((bf16[32,144,128]{2,1,0:T(8,128)(2,1)}), bf16[32,144,128]{2,1,0:T(8,128)(2,1)S(1)}, u32[]{:S(2)}, u32[]{:S(2)}) async-start(bf16[32,144,128]{2,1,0:T(8,128)(2,1)} %get-tuple-element.25), calls=%async_computation | async-start | bytes 2359296 | tf_op jit(solution)/shard_map/all_to_all | solution.py:434
  22.0 34.6 %collective-permute-start.1 = (bf16[512,1280]{1,0:T(8,128)(2,1)}, bf16[512,1280]{1,0:T(8,128)(2,1)S(1)}, u32[]{:S(2)}, u32[]{:S(2)}) collective-permute-start(bf16[512,1280]{1,0:T(8,128)(2,1)} %refs_0_.1), channel_id=1, source_target_pairs={{0,6},{1,7},{2,0},{3,1},{4,2},{5,3},{6,4},{7,5},{8,14},{9,15},{10,... | collective-permute-start | bytes 3932168 | tf_op jit(solution)/shard_map/ppermute | solution.py:416
  24.6 32.1 %collective-permute-start = (bf16[512,1280]{1,0:T(8,128)(2,1)}, bf16[512,1280]{1,0:T(8,128)(2,1)}, u32[]{:S(2)}, u32[]{:S(2)}) collective-permute-start(bf16[512,1280]{1,0:T(8,128)(2,1)} %refs_0_.1), channel_id=1, source_target_pairs={{0,2},{1,3},{2,4},{3,5},{4,6},{5,7},{6,0},{7,1},{8,10},{9,11},{10,... | collective-permute-start | bytes 3932168 | tf_op jit(solution)/shard_map/ppermute | solution.py:415
  24.6 1.5 %copy-start.4 = (bf16[40,1,24576]{2,0,1:T(8,128)(2,1)S(1)}, bf16[40,1,24576]{2,0,1:T(8,128)(2,1)}, u32[]{:S(2)}) copy-start(bf16[40,1,24576]{2,0,1:T(8,128)(2,1)} %param.10) | copy-start | bytes 5898244
  55.8 0.8 copy-start.5
  57.6 17.7 %collective-permute-start.4 = (bf16[256,1280]{1,0:T(8,128)(2,1)}, bf16[256,1280]{1,0:T(8,128)(2,1)}, u32[]{:S(2)}, u32[]{:S(2)}) collective-permute-start(bf16[256,1280]{1,0:T(8,128)(2,1)} %slice.11), channel_id=1, source_target_pairs={{0,6},{1,7},{2,0},{3,1},{4,2},{5,3},{6,4},{7,5},{8,14},{9,15},{10,... | collective-permute-start | bytes 1966088 | tf_op jit(solution)/shard_map/ppermute | solution.py:439
  60.2 26.7 %all-to-all-start.1 = ((bf16[32,64,128]{2,1,0:T(8,128)(2,1)}), bf16[32,64,128]{2,1,0:T(8,128)(2,1)S(1)}, u32[]{:S(2)}, u32[]{:S(2)}) async-start(bf16[32,64,128]{2,1,0:T(8,128)(2,1)} %copy-done.5), calls=%async_computation.1 | async-start | bytes 1048576 | tf_op jit(solution)/shard_map/all_to_all | solution.py:443
  69.4 17.5 %copy-start.10 = (f32[256]{0:T(256)S(1)}, f32[256]{0:T(256)}, u32[]{:S(2)}) copy-start(f32[256]{0:T(256)} %param.18) | copy-start | bytes 3076
  71.4 15.4 %collective-permute-start.3 = (bf16[256,1280]{1,0:T(8,128)(2,1)}, bf16[256,1280]{1,0:T(8,128)(2,1)}, u32[]{:S(2)}, u32[]{:S(2)}) collective-permute-start(bf16[256,1280]{1,0:T(8,128)(2,1)} %slice.10), channel_id=1, source_target_pairs={{0,2},{1,3},{2,4},{3,5},{4,6},{5,7},{6,0},{7,1},{8,10},{9,11},{10,... | collective-permute-start | bytes 1966088 | tf_op jit(solution)/shard_map/ppermute | solution.py:438
  72.3 14.5 %collective-permute-start.2 = (bf16[32,80,128]{2,1,0:T(8,128)(2,1)}, bf16[32,80,128]{2,1,0:T(8,128)(2,1)}, u32[]{:S(2)}, u32[]{:S(2)}) collective-permute-start(bf16[32,80,128]{2,1,0:T(8,128)(2,1)} %slice.9), channel_id=1, source_target_pairs={{0,1},{1,0},{2,3},{3,2},{4,5},{5,4},{6,7},{7,6},{8,9},{9,8},{10,11... | collective-permute-start | bytes 1966088 | tf_op jit(solution)/shard_map/ppermute | solution.py:442
  74.7 28.7 %collective-permute-start.5 = (bf16[512,1280]{1,0:T(8,128)(2,1)}, bf16[512,1280]{1,0:T(8,128)(2,1)}, u32[]{:S(2)}, u32[]{:S(2)}) collective-permute-start(bf16[512,1280]{1,0:T(8,128)(2,1)} %refs_0_.1), channel_id=1, source_target_pairs={{0,1},{1,0},{2,3},{3,2},{4,5},{5,4},{6,7},{7,6},{8,9},{9,8},{10,11... | collective-permute-start | bytes 3932168 | tf_op jit(solution)/shard_map/ppermute | solution.py:417
  74.7 28.7 %collective-permute-start.6 = (bf16[512,1280]{1,0:T(8,128)(2,1)}, bf16[512,1280]{1,0:T(8,128)(2,1)}, u32[]{:S(2)}, u32[]{:S(2)}) collective-permute-start(bf16[512,1280]{1,0:T(8,128)(2,1)} %collective-permute-done.refs_1_), channel_id=1, source_target_pairs={{0,1},{1,0},{2,3},{3,2},{4,5},{5,4},{6,7},{7,6},{8,9},{9,8},{10,11... | collective-permute-start | bytes 3932168 | tf_op jit(solution)/shard_map/ppermute | solution.py:441
  75.2 28.2 %collective-permute-start.7 = (bf16[512,1280]{1,0:T(8,128)(2,1)S(1)}, bf16[512,1280]{1,0:T(8,128)(2,1)}, u32[]{:S(2)}, u32[]{:S(2)}) collective-permute-start(bf16[512,1280]{1,0:T(8,128)(2,1)S(1)} %collective-permute-done.1.refs_2_), channel_id=1, source_target_pairs={{0,1},{1,0},{2,3},{3,2},{4,5},{5,4},{6,7},{7,6},{8,9},{9,8},{10,11... | collective-permute-start | bytes 3932168 | tf_op jit(solution)/shard_map/ppermute | solution.py:441
  86.8 19.1 %copy-start.9 = (s32[10,1,128]{2,1,0:T(1,128)S(1)}, s32[10,1,128]{2,1,0:T(1,128)}, u32[]{:S(2)}) copy-start(s32[10,1,128]{2,1,0:T(1,128)} %mask.1) | copy-start | bytes 15364
  90.2 23.1 %all-to-all-start.2 = ((bf16[32,24,256]{2,1,0:T(8,128)(2,1)}), bf16[32,24,256]{2,1,0:T(8,128)(2,1)S(1)}, u32[]{:S(2)}, u32[]{:S(2)}) async-start(bf16[32,24,256]{2,1,0:T(8,128)(2,1)} %bitcast.13), calls=%async_computation.2 | async-start | bytes 786432 | tf_op jit(solution)/shard_map/all_to_all | solution.py:464
  99.2 5.9 %collective-permute-start.8 = (bf16[256,1280]{1,0:T(8,128)(2,1)}, bf16[256,1280]{1,0:T(8,128)(2,1)S(1)}, u32[]{:S(2)}, u32[]{:S(2)}) collective-permute-start(bf16[256,1280]{1,0:T(8,128)(2,1)} %collective-permute-done.3.refs_3_), channel_id=1, source_target_pairs={{0,1},{1,0},{2,3},{3,2},{4,5},{5,4},{6,7},{7,6},{8,9},{9,8},{10,11... | collective-permute-start | bytes 1966088 | tf_op jit(solution)/shard_map/ppermute | solution.py:445
  103.1 2.9 %collective-permute-start.9 = (bf16[256,1280]{1,0:T(8,128)(2,1)}, bf16[256,1280]{1,0:T(8,128)(2,1)S(1)}, u32[]{:S(2)}, u32[]{:S(2)}) collective-permute-start(bf16[256,1280]{1,0:T(8,128)(2,1)} %collective-permute-done.4.refs_4_), channel_id=1, source_target_pairs={{0,1},{1,0},{2,3},{3,2},{4,5},{5,4},{6,7},{7,6},{8,9},{9,8},{10,11... | collective-permute-start | bytes 1966088 | tf_op jit(solution)/shard_map/ppermute | solution.py:445
  106.0 7.4 %copy-start.11 = (s32[1,128]{1,0:T(1,128)S(1)}, s32[1,128]{1,0:T(1,128)}, u32[]{:S(2)}) copy-start(s32[1,128]{1,0:T(1,128)} %labels.1) | copy-start | bytes 1540
  109.4 4.0 %copy-start.1 = (bf16[8,512,1280]{2,1,0:T(8,128)(2,1)}, bf16[8,512,1280]{2,1,0:T(8,128)(2,1)S(1)}, u32[]{:S(2)}) copy-start(bf16[8,512,1280]{2,1,0:T(8,128)(2,1)S(1)} %get-tuple-element.37.held) | copy-start | bytes 31457284
  113.4 4.0 %copy-start.2 = (bf16[8,512,1280]{2,1,0:T(8,128)(2,1)S(1)}, bf16[8,512,1280]{2,1,0:T(8,128)(2,1)}, u32[]{:S(2)}) copy-start(bf16[8,512,1280]{2,1,0:T(8,128)(2,1)} %copy-done.1) | copy-start | bytes 31457284

commit v6 on v5

--- a/solution.py
+++ b/solution.py
@@ -17,6 +17,7 @@
 TARGETS = 128
 HIDDEN = 256
 UNION = 24
+NAMED = FEAT * UNION
 SLAB = 256
 UNROLL = 64
 LEAST = 3
@@ -24,7 +25,7 @@
 CHUNK = 1024
 PAIRS = 4
 TABLE_STEP = 8
-STAGED = [(0, 0), (1, 0), (2, 0), (3, 0), (3, 256), (4, 0), (5, 0), (6, 0), (7, 0), (7, 256)]
+MOST = 60 * 2**20
 F32 = jnp.float32
 BF16 = jnp.bfloat16
 
@@ -48,7 +49,21 @@
     return terms[0]
 
 
-def send_kernel(features, weights, neighbours, targets, send, place, built, sent):
+def prepare_kernel(core, *refs):
+    sources, (send, place, lists, ranks), held, (built, columns, sent, arrived) = (
+        refs[:6],
+        refs[6:10],
+        refs[10:16],
+        refs[16:],
+    )
+    fetches = []
+    for source, ref in zip(sources, held):
+        part = source if source.shape == ref.shape else source.at[:, pl.ds(0, ROWS)]
+        fetches.append(pltpu.make_async_copy(part, ref, arrived.at[len(fetches)]))
+        fetches[-1].start()
+    neighbours, targets, weights, features, given, filled = held
+    fetches[0].wait()
+    fetches[1].wait()
     owners, lanes = [], []
     named = jnp.zeros((FEAT, SLAB), F32)
     for slot in range(FAN + 1):
@@ -69,7 +84,11 @@
         places.append(owner * UNION + mine.astype(jnp.int32))
     place[...] = jnp.concatenate(places + [jnp.zeros((5, TARGETS), jnp.int32)], axis=0)
 
+    fetches[2].wait()
+    fetches[3].wait()
     shared = weights[...].astype(F32)
+    shared = jnp.where(core[0] == 0, shared[:, :, :128], shared[:, :, 128:])
+    shared = shared.reshape(2 * WIDTH, 128)
     for pair in range(FEAT // 2):
         block = features[:, pl.ds(pair * 2 * OWN, 2 * OWN)].astype(F32)
         for half in range(2):
@@ -79,22 +98,14 @@
             built[owner] = jnp.concatenate([shared, folded(block, half, last)], axis=0).astype(BF16)
         if pair % 4 == 3:
             copies_out(built, send, sent, pair // 4).start()
+    fetches[4].wait()
+    fetches[5].wait()
+    order_rows(given, filled, lists, ranks, columns)
     for step in range(FEAT // 8):
         copies_out(built, send, sent, step).wait()
 
 
-def copies_out(built, send, sent, step):
-    span = pl.ds(step * 8, 8)
-    return pltpu.make_async_copy(built.at[span], send.at[span], sent.at[step])
-
-
-def folded(block, half, last):
-    rest = block[:, 128 + half * 64 : 192 + half * 64]
-    rest = jnp.concatenate([rest[:24], jnp.concatenate([rest[24:], last], axis=0)], axis=1)
-    return jnp.concatenate([block[:, half * 256 : half * 256 + 128], rest], axis=0)
-
-
-def order_kernel(neighbours, mask, lists, ranks, columns):
+def order_rows(neighbours, mask, lists, ranks, columns):
     used = [jnp.where(mask[slot] > 0, 1, 0) for slot in range(FAN)]
     before = [jnp.zeros((LINES, 128), jnp.int32)]
     for slot in range(FAN):
@@ -136,6 +147,17 @@
             lists[pl.ds(first + half, FAN + 1, stride=8), :] = here
 
 
+def copies_out(built, send, sent, step):
+    span = pl.ds(step * 8, 8)
+    return pltpu.make_async_copy(built.at[span], send.at[span], sent.at[step])
+
+
+def folded(block, half, last):
+    rest = block[:, 128 + half * 64 : 192 + half * 64]
+    rest = jnp.concatenate([rest[:24], jnp.concatenate([rest[24:], last], axis=0)], axis=1)
+    return jnp.concatenate([block[:, half * 256 : half * 256 + 128], rest], axis=0)
+
+
 def moved(ranks, line):
     return jnp.where(iota((256, 128), 0) == ranks[pl.ds(line, 1), :], 1.0, 0.0).astype(BF16)
 
@@ -146,7 +168,7 @@
 
 
 def gather_kernel(
-    slots, ranks, features, send, table, sums, lists, built, arrived, sent
+    slots, ranks, source, send, table, sums, lists, built, features, arrived, loaded, sent
 ):
     size = (FAN + 1) * CHUNK
 
@@ -154,13 +176,24 @@
         span = pl.ds(pl.multiple_of(chunk * size, size), size)
         return pltpu.make_async_copy(slots.at[span], lists.at[span], arrived.at[chunk])
 
+    third = INPUTS // 3
+    piece = 128 * TABLE_STEP
+
+    def load(step, t):
+        span = pl.ds(pl.multiple_of(t * third + step * piece, piece), piece)
+        return pltpu.make_async_copy(source.at[:, span], features.at[:, span], loaded.at[step, t])
+
+    for step in range(third // piece):
+        for t in range(3):
+            load(step, t).start()
     for chunk in range(ROWS // CHUNK):
         fetch(chunk).start()
 
     lane = iota((128, 128), 1)
-    third = INPUTS // 3
 
     def fill(step, carry):
+        for t in range(3):
+            load(step, t).wait()
         for part in range(TABLE_STEP):
             at = pl.multiple_of((step * TABLE_STEP + part) * 128, 128)
             blocks = [features[:, pl.ds(t * third + at, 128)].astype(F32) for t in range(3)]
@@ -232,7 +265,7 @@
 
 
 def hidden_kernel(
-    spot, mine, theirs, means, bias, hidden, rows, stacked, held, other, marks, chosen
+    seen, spot, mine, theirs, means, bias, hidden, rows, stacked, held, other, marks, chosen
 ):
     for source in range(FEAT):
         own = mine[source].astype(F32)
@@ -269,45 +302,66 @@
     rows[...] = contract(chosen[...].astype(BF16), padded, 1, 0).astype(BF16)
 
 
-def stage_kernel(place, mask, *refs):
-    blocks, (picks, held, arrived) = refs[:-3], refs[-3:]
-    copies = []
-    for block in blocks:
-        slot, first = STAGED[len(copies)]
-        span = held.at[slot, pl.ds(first, block.shape[0]), :]
-        copies.append(pltpu.make_async_copy(block, span, arrived.at[len(copies)]))
-        copies[-1].start()
-    spots = iota((FEAT * UNION, TARGETS), 0)
-    total = jnp.zeros((FEAT * UNION, TARGETS), F32)
+def pick_kernel(place, mask, labels, picks):
+    spots = iota((NAMED, TARGETS), 0)
+    total = jnp.zeros((NAMED, TARGETS), F32)
     for slot in range(FAN):
         used = mask[slot].astype(F32)
         total = total + jnp.where(spots == place[pl.ds(slot, 1), :], used, 0.0)
-    picks[0] = total.astype(BF16)
-    picks[1] = jnp.where(spots == place[pl.ds(FAN, 1), :], 1.0, 0.0).astype(BF16)
+    own = jnp.where(spots == place[pl.ds(FAN, 1), :], 1.0, 0.0)
+    line = iota((16, TARGETS), 0)
+    label = jnp.broadcast_to(labels[...], (16, TARGETS))
+    high = label >> 7
+    parts = jnp.where(line == 0, high, jnp.where(line == 1, label - high * 128, 0))
+    blank = jnp.zeros((16, TARGETS), F32)
+    picks[0] = jnp.concatenate([total, parts.astype(F32)], axis=0).astype(BF16)
+    picks[1] = jnp.concatenate([own, blank], axis=0).astype(BF16)
+
+
+def loss_kernel(bases, *refs):
+    sources, (stats, other) = refs[: 4 + NODE // 2], refs[4 + NODE // 2 : 6 + NODE // 2]
+    inputs, logits, *held, arrived = refs[6 + NODE // 2 :]
+    copies = [
+        pltpu.make_async_copy(source, ref, arrived.at[k])
+        for k, (source, ref) in enumerate(zip(sources, held))
+    ]
     for copy in copies:
-        copy.wait()
-
-
-def loss_kernel(bases, rows, picks, labels, held, loss, inputs, logits):
-    count = contract(picks[0], jnp.ones((FEAT * UNION, 128), BF16), 0, 0)[:, :1]
-    agg = contract(picks[0], rows[...], 0, 0) / jnp.maximum(count, 1.0)
-    inputs[:, pl.ds(0, HIDDEN)] = contract(picks[1], rows[...], 0, 0).astype(BF16)
-    inputs[:, pl.ds(HIDDEN, HIDDEN)] = agg.astype(BF16)
-    offset = (
-        jnp.broadcast_to(labels[...].astype(F32), (TARGETS, TARGETS)).T.astype(jnp.int32)
-        - iota((TARGETS, TARGETS), 1)
+        copy.start()
+    offsets = []
+    for side in range(2):
+        copies[2 * side].wait()
+        copies[2 * side + 1].wait()
+        rows, picks = held[2 * side], held[2 * side + 1]
+        total, own = picks[0][:NAMED], picks[1][:NAMED]
+        count = contract(total, jnp.ones((NAMED, 128), BF16), 0, 0)[:, :1]
+        agg = contract(total, rows[...], 0, 0) / jnp.maximum(count, 1.0)
+        span = pl.ds(side * TARGETS, TARGETS)
+        inputs[span, pl.ds(0, HIDDEN)] = contract(own, rows[...], 0, 0).astype(BF16)
+        inputs[span, pl.ds(HIDDEN, HIDDEN)] = agg.astype(BF16)
+        parts = picks[0][NAMED:].astype(F32)
+        label = jnp.broadcast_to(parts[:1] * 128.0 + parts[1:2], (TARGETS, TARGETS)).T
+        offsets.append(label.astype(jnp.int32) - iota((TARGETS, TARGETS), 1))
+    blocks = held[4:]
+    width = blocks[0].shape[1]
+    start = (
+        jnp.full((TARGETS, TARGETS), -jnp.inf, F32),
+        jnp.zeros((TARGETS, TARGETS), F32),
+        jnp.zeros((TARGETS, TARGETS), F32),
     )
-    width = held.shape[2]
-    largest = jnp.full((TARGETS, TARGETS), -jnp.inf, F32)
-    summed = jnp.zeros((TARGETS, TARGETS), F32)
-    picked = jnp.zeros((TARGETS, TARGETS), F32)
-    for step in range(NODE + 1):
-        if step < NODE:
-            logits[step % 2] = contract(inputs[...], held[step], 1, 0)
+    running = [start, start]
+    for step in range(2 * len(blocks) + 1):
+        block, side = step // 2, step % 2
+        if block < len(blocks):
+            if side == 0:
+                copies[4 + block].wait()
+            mine = inputs[pl.ds(side * TARGETS, TARGETS), :]
+            logits[step % 2] = contract(mine, blocks[block][...], 1, 0)
         if step > 0:
+            block, side = (step - 1) // 2, (step - 1) % 2
+            last = logits.at[(step - 1) % 2]
+            largest, summed, picked = running[side]
             spans = [pl.ds(k * 128, 128) for k in range(width // 128)]
-            last = logits.at[(step - 1) % 2]
-            here = offset - bases[step - 1]
+            here = offsets[side] - bases[block]
             now = largest
             for span in spans:
                 now = jnp.maximum(now, last[:, span])
@@ -316,11 +370,15 @@
                 part = last[:, span]
                 summed = summed + jnp.exp(part - now)
                 picked = picked + jnp.where(here == k * 128, part, 0.0)
-            largest = now
-    most = jnp.max(largest, axis=1, keepdims=True)
-    total = jnp.sum(summed * jnp.exp(largest - most), axis=1, keepdims=True)
-    column = most + jnp.log(total) - jnp.sum(picked, axis=1, keepdims=True)
-    loss[...] = jnp.broadcast_to(column, (TARGETS, TARGETS)).T[:1]
+            running[side] = (now, summed, picked)
+    for side, ref in ((0, stats), (1, other)):
+        largest, summed, picked = running[side]
+        most = jnp.max(largest, axis=1, keepdims=True)
+        total = jnp.sum(summed * jnp.exp(largest - most), axis=1, keepdims=True)
+        found = jnp.sum(picked, axis=1, keepdims=True)
+        lane = iota((TARGETS, TARGETS), 1)
+        table = jnp.where(lane == 0, most, jnp.where(lane == 1, total, found))
+        ref[...] = table.T[:8]
 
 
 VMEM = pl.BlockSpec(memory_space=pltpu.VMEM)
@@ -328,68 +386,78 @@
 SMEM = pl.BlockSpec(memory_space=pltpu.SMEM)
 
 
-def call_order(neighbours, mask):
+def call_prepare(core, arrays):
+    shapes = [array.shape for array in arrays]
+    shapes[3] = (WIDTH, ROWS)
     return pl.pallas_call(
-        order_kernel,
+        prepare_kernel,
         out_shape=(
+            jax.ShapeDtypeStruct((FEAT, 144, 128), BF16),
+            jax.ShapeDtypeStruct((16, TARGETS), jnp.int32),
             jax.ShapeDtypeStruct((LINES * (FAN + 1), 128), jnp.int32),
             jax.ShapeDtypeStruct((LINES, 128), jnp.int32),
         ),
-        in_specs=[VMEM, VMEM],
-        out_specs=(VMEM, VMEM),
-        scratch_shapes=[pltpu.VMEM((32, LINES, 128), F32)],
-        compiler_params=pltpu.CompilerParams(vmem_limit_bytes=24 * 2**20),
+        in_specs=[SMEM] + [HBM] * 6,
+        out_specs=(HBM, VMEM, VMEM, VMEM),
+        scratch_shapes=[
+            *[pltpu.VMEM(shape, array.dtype) for shape, array in zip(shapes, arrays)],
+            pltpu.VMEM((FEAT, 144, 128), BF16),
+            pltpu.VMEM((32, LINES, 128), F32),
+            pltpu.SemaphoreType.DMA((FEAT // 8,)),
+            pltpu.SemaphoreType.DMA((6,)),
+        ],
+        compiler_params=pltpu.CompilerParams(vmem_limit_bytes=MOST),
         cost_estimate=pl.CostEstimate(flops=10**8, bytes_accessed=10**7, transcendentals=0),
-    )(neighbours.reshape(FAN, LINES, 128), mask.reshape(FAN, LINES, 128))
+    )(core, *arrays)
 
 
 def call_gather(slots, ranks, table):
     return pl.pallas_call(
         gather_kernel,
         out_shape=jax.ShapeDtypeStruct((FEAT, 64, 128), BF16),
-        in_specs=[pl.BlockSpec(memory_space=pl.ANY), VMEM, VMEM],
+        in_specs=[pl.BlockSpec(memory_space=pl.ANY), VMEM, HBM],
         out_specs=HBM,
         scratch_shapes=[
             pltpu.VMEM((INPUTS + 8, 128), F32),
             pltpu.VMEM((ROWS, 128), F32),
             pltpu.SMEM(((FAN + 1) * ROWS,), jnp.int32),
             pltpu.VMEM((FEAT, 64, 128), BF16),
+            pltpu.VMEM((WIDTH, INPUTS), BF16),
             pltpu.SemaphoreType.DMA((ROWS // CHUNK,)),
+            pltpu.SemaphoreType.DMA((INPUTS // 3 // 128 // TABLE_STEP, 3)),
             pltpu.SemaphoreType.DMA((FEAT // 8,)),
         ],
-        compiler_params=pltpu.CompilerParams(vmem_limit_bytes=24 * 2**20),
-        cost_estimate=pl.CostEstimate(flops=10**9, bytes_accessed=90 * 10**6, transcendentals=0),
+        compiler_params=pltpu.CompilerParams(vmem_limit_bytes=MOST),
+        cost_estimate=pl.CostEstimate(flops=0, bytes_accessed=0, transcendentals=0),
     )(slots, ranks, table)
 
 
-def call_stage(place, mask, blocks):
-    width = blocks[0].shape[1]
+def call_pick(place, mask, labels):
     return pl.pallas_call(
-        stage_kernel,
-        out_shape=(
-            jax.ShapeDtypeStruct((2, FEAT * UNION, TARGETS), BF16),
-            jax.ShapeDtypeStruct((NODE, 2 * HIDDEN, width), BF16),
-        ),
-        in_specs=[VMEM] * 2 + [HBM] * len(blocks),
-        out_specs=(VMEM, VMEM),
-        scratch_shapes=[pltpu.SemaphoreType.DMA((len(blocks),))],
+        pick_kernel,
+        out_shape=jax.ShapeDtypeStruct((2, NAMED + 16, TARGETS), BF16),
+        in_specs=[VMEM] * 3,
+        out_specs=VMEM,
         compiler_params=pltpu.CompilerParams(vmem_limit_bytes=16 * 2**20),
-        cost_estimate=pl.CostEstimate(flops=10**7, bytes_accessed=20 * 10**6, transcendentals=0),
-    )(place, mask, *blocks)
-
-
-def call_loss(bases, rows, picks, labels, held):
+        cost_estimate=pl.CostEstimate(flops=10**7, bytes_accessed=4 * 10**6, transcendentals=0),
+    )(place, mask, labels)
+
+
+def call_loss(bases, rows, picks, rows_there, picks_there, blocks):
+    sources = [rows, picks, rows_there, picks_there, *blocks]
     return pl.pallas_call(
         loss_kernel,
-        out_shape=jax.ShapeDtypeStruct((1, TARGETS), F32),
-        in_specs=[SMEM] + [VMEM] * 4,
-        out_specs=VMEM,
+        out_shape=[jax.ShapeDtypeStruct((8, TARGETS), F32)] * 2,
+        in_specs=[SMEM] + [HBM] * len(sources),
+        out_specs=[VMEM, VMEM],
         scratch_shapes=[
-            pltpu.VMEM((TARGETS, 2 * HIDDEN), BF16),
-            pltpu.VMEM((2, TARGETS, held.shape[2]), F32),
+            pltpu.VMEM((2 * TARGETS, 2 * HIDDEN), BF16),
+            pltpu.VMEM((2, TARGETS, blocks[0].shape[1]), F32),
+            *[pltpu.VMEM(source.shape, BF16) for source in sources],
+            pltpu.SemaphoreType.DMA((len(sources),)),
         ],
-        compiler_params=pltpu.CompilerParams(vmem_limit_bytes=16 * 2**20),
-    )(bases, rows, picks, labels, held)
+        compiler_params=pltpu.CompilerParams(vmem_limit_bytes=MOST),
+    )(bases, *sources)
 
 
 def body(
@@ -406,43 +474,28 @@
 ):
     spot = lax.axis_index("node").astype(jnp.int32)
     core = spot & 1
-    half = lax.dynamic_slice(first_weight, (0, 0, core * 128), (2, WIDTH, 128))
     table = features[:, 0, :]
-    slots, ranks = call_order(first_neighbours, first_mask)
-    up = [(device, (device + 2) % NODE) for device in range(NODE)]
-    down = [(device, (device - 2) % NODE) for device in range(NODE)]
     swap = [(device, device ^ 1) for device in range(NODE)]
-    below = lax.ppermute(class_weight, "node", up)
-    above = lax.ppermute(class_weight, "node", down)
-    swapped = [lax.ppermute(class_weight, "node", swap)]
-    table, slots, ranks = lax.optimization_barrier((table, slots, ranks))
-    own, place = pl.pallas_call(
-        send_kernel,
-        out_shape=(
-            jax.ShapeDtypeStruct((FEAT, 144, 128), BF16),
-            jax.ShapeDtypeStruct((16, TARGETS), jnp.int32),
-        ),
-        in_specs=[VMEM] * 4,
-        out_specs=(HBM, VMEM),
-        scratch_shapes=[
-            pltpu.VMEM((FEAT, 144, 128), BF16),
-            pltpu.SemaphoreType.DMA((FEAT // 8,)),
+    blocks = [class_weight]
+    for hops in (4, 2, 6):
+        around = [(device, (device + hops) % NODE) for device in range(NODE)]
+        blocks.append(lax.ppermute(class_weight, "node", around))
+    own, place, slots, ranks = call_prepare(
+        core[None],
+        [
+            second_neighbours,
+            target_index,
+            first_weight,
+            table,
+            first_neighbours.reshape(FAN, LINES, 128),
+            first_mask.reshape(FAN, LINES, 128),
         ],
-        compiler_params=pltpu.CompilerParams(vmem_limit_bytes=16 * 2**20),
-        cost_estimate=pl.CostEstimate(flops=10**8, bytes_accessed=3 * 10**6, transcendentals=0),
-    )(table, half.reshape(2 * WIDTH, 128), second_neighbours, target_index)
+    )
     own = lax.all_to_all(own, "feat", 0, 0)
     send = call_gather(slots.reshape(-1), ranks, table)
-    send, below, above, own = lax.optimization_barrier((send, below, above, own))
-    far = [
-        lax.ppermute(below[:HIDDEN], "node", up),
-        lax.ppermute(above[HIDDEN:], "node", down),
-    ]
-    swapped += [lax.ppermute(below, "node", swap), lax.ppermute(above, "node", swap)]
     theirs = lax.ppermute(own[:, : 2 * WIDTH], "node", swap)
     means = lax.all_to_all(send, "feat", 0, 0)
-    means, far = lax.optimization_barrier((means, far))
-    swapped += [lax.ppermute(part, "node", swap) for part in far]
+    seen = jnp.stack([block[0, 0] for block in blocks[2:]]).astype(F32)
     side = jnp.stack([core, lax.axis_index("feat").astype(jnp.int32) & 1])
     hidden, rows = pl.pallas_call(
         hidden_kernel,
@@ -450,7 +503,7 @@
             jax.ShapeDtypeStruct((OWN, HIDDEN), BF16),
             jax.ShapeDtypeStruct((FEAT * UNION, HIDDEN), BF16),
         ),
-        in_specs=[SMEM] + [VMEM] * 4,
+        in_specs=[SMEM] * 2 + [VMEM] * 4,
         out_specs=(VMEM, VMEM),
         scratch_shapes=[
             pltpu.VMEM((FEAT * 80, 256), BF16),
@@ -460,13 +513,18 @@
             pltpu.VMEM((FEAT * UNION, SLAB), F32),
         ],
         compiler_params=pltpu.CompilerParams(vmem_limit_bytes=24 * 2**20),
-    )(side, own, theirs, means, first_bias[None, :])
+    )(seen, side, own, theirs, means, first_bias[None, :])
+    picks = call_pick(place, second_mask, labels)
+    picks_there = lax.ppermute(picks, "node", swap)
     rows = lax.all_to_all(rows.reshape(FEAT, UNION, HIDDEN), "feat", 0, 0)
     rows = rows.reshape(FEAT * UNION, HIDDEN)
-    picks, held = call_stage(place, second_mask, [class_weight, below, above, *far, *swapped])
-    order = jnp.stack([spot, spot + 6, spot + 2, spot + 4]) & 7
-    bases = jnp.concatenate([order, order ^ 1]) * class_weight.shape[1]
-    loss = call_loss(bases, rows, picks, labels, held)
+    rows_there = lax.ppermute(rows, "node", swap)
+    bases = (jnp.stack([spot, spot + 4, spot + 6, spot + 2]) & 7) * class_weight.shape[1]
+    here, there = call_loss(bases, rows, picks, rows_there, picks_there, blocks)
+    there = lax.ppermute(there, "node", swap)
+    most = jnp.maximum(here[0:1], there[0:1])
+    total = here[1:2] * jnp.exp(here[0:1] - most) + there[1:2] * jnp.exp(there[0:1] - most)
+    loss = most + jnp.log(total) - (here[2:3] + there[2:3])
     return (hidden[None], loss)
 
 

time: 122 us -> 113 us (0.926)
  local copies, waits for them, and re-layouts: 19 us -> 3.29 us
  waiting for transfers between devices: 14 us -> 18.6 us
  other arithmetic: 0.23 us -> 3.43 us
  starting transfers between devices: 42.5 us -> 40.6 us
    unnamed x26 -> x16, local copies, waits for them, and re-layouts: 15.1 us -> 0.89 us
    ppermute x9 -> x6, waiting for transfers between devices: 13.9 us -> 1.75 us  [the longest x1 1.07 us: body(): there = lax.ppermute(there, 'node', swap)]
    all_to_all x1, waiting for transfers between devices: 0.01 us -> 9.73 us  [body(): rows = lax.all_to_all(rows.reshape(FEAT, UNION, HIDDEN), 'feat', 0, 0)]
    all_to_all x1, waiting for transfers between devices: 0.01 us -> 7.07 us  [body(): means = lax.all_to_all(send, 'feat', 0, 0)]
    all_to_all x1, starting transfers between devices: 8.93 us -> 6.32 us  [body(): rows = lax.all_to_all(rows.reshape(FEAT, UNION, HIDDEN), 'feat', 0, 0)]
    pallas_call x1, Pallas kernels: 29.7 us -> 31.4 us  [call_gather(): pl.pallas_call(gather_kernel, out_shape=jax.ShapeDtypeStruct((FEAT, 64, 1...]
    convert_element_type x0 -> x1, other arithmetic: none -> 1.37 us  [body(): seen = jnp.stack([block[0, 0] for block in blocks[2:]]).astype(F32)]
    sub x0 -> x1, other arithmetic: none -> 1.33 us  [body(): loss = most + jnp.log(total) - (here[2:3] + there[2:3])]
  transfers between devices with their start and end apart: 13 -> 10, of which waited for: 3 -> 4; matrix products, arithmetic and copies ran while one was open for 3% -> 4% of each run, Pallas kernels for 30% -> 31%
where the time goes in v6:
time: 113 us; the launch traced here: 112 us
  Pallas kernels  45.6 us (40%)
  starting transfers between devices  40.6 us (36%)
  waiting for transfers between devices  18.6 us (16%)
  other arithmetic  3.43 us (3%)
  local copies, waits for them, and re-layouts  3.29 us (3%)
    pallas_call x1, Pallas kernels, call_gather(): pl.pallas_call(gather_kernel, out_shape=jax.ShapeDtypeStruct((FEAT, 64, 1...  31.4 us
    all_to_all x1, starting transfers between devices, body(): own = lax.all_to_all(own, 'feat', 0, 0)  12 us
    all_to_all x1, waiting for transfers between devices, body(): rows = lax.all_to_all(rows.reshape(FEAT, UNION, HIDDEN), 'feat', 0, 0)  9.73 us
    all_to_all x1, starting transfers between devices, body(): means = lax.all_to_all(send, 'feat', 0, 0)  9.23 us
    all_to_all x1, waiting for transfers between devices, body(): means = lax.all_to_all(send, 'feat', 0, 0)  7.07 us
    all_to_all x1, starting transfers between devices, body(): rows = lax.all_to_all(rows.reshape(FEAT, UNION, HIDDEN), 'feat', 0, 0)  6.32 us
    pallas_call x1, Pallas kernels, call_loss(): pl.pallas_call(loss_kernel, out_shape=[jax.ShapeDtypeStruct((8, TARGETS),...  5.84 us
    pallas_call x1, Pallas kernels, call_prepare(): pl.pallas_call(prepare_kernel, out_shape=(jax.ShapeDtypeStruct((FEAT, 144...  5.09 us
  transfers between devices with their start and end apart: 10, of which 4 were waited for; matrix products, arithmetic and copies ran while one was open for 4% of the time, Pallas kernels for 31%

profile of v6, /device:TPU:1, one launch (start us, length us, event | category | flops | bytes accessed | tf_op | source)
XLA Modules:
  0.0 112.3 jit_solution(2913392954122427025)
XLA Ops:
  0.6 5.1 %shard_map.113 = (bf16[32,144,128]{2,1,0:T(8,128)(2,1)}, s32[16,128]{1,0:T(8,128)}, s32[528,128]{1,0:T(8,128)}, s32[48,128]{1,0:T(8,128)}) custom-call(s32[1]{0:T(128)} %bitcast.2.core, s32[10,1,128]{2,1,0:T(1,128)} %refs_0_.1, s32[1,128]{1,0:T(1,128)} %refs_1_.1, bf16[2,40,256]{2,1,0:T(8,128)(2,1)} %refs_2_.1, bf16[40,24576]{1,0:T(8,128)(2,1)} %bitcast.17, ...), custom_call_target="tpu_custom_call" | custom-call | flops 100000000 | bytes 10000000 | tf_op jit(solution)/shard_map/pallas_call | solution.py:392
  5.7 12.0 %all-to-all-start = ((bf16[32,144,128]{2,1,0:T(8,128)(2,1)}), bf16[32,144,128]{2,1,0:T(8,128)(2,1)S(1)}, u32[]{:S(2)}, u32[]{:S(2)}) async-start(bf16[32,144,128]{2,1,0:T(8,128)(2,1)} %get-tuple-element.10), calls=%async_computation | async-start | bytes 2359296 | tf_op jit(solution)/shard_map/all_to_all | solution.py:494
  17.8 2.6 %collective-permute-start.1 = (bf16[512,1280]{1,0:T(8,128)(2,1)}, bf16[512,1280]{1,0:T(8,128)(2,1)}, u32[]{:S(2)}, u32[]{:S(2)}) collective-permute-start(bf16[512,1280]{1,0:T(8,128)(2,1)} %refs_4_.1), channel_id=1, source_target_pairs={{0,6},{1,7},{2,0},{3,1},{4,2},{5,3},{6,4},{7,5},{8,14},{9,15},{10,... | collective-permute-start | bytes 3932168 | tf_op jit(solution)/shard_map/ppermute | solution.py:482
  20.3 0.0 collective-permute-start
  20.3 31.4 %shard_map.114 = bf16[32,64,128]{2,1,0:T(8,128)(2,1)} custom-call(s32[67584]{0:T(1024)} %bitcast.21, s32[48,128]{1,0:T(8,128)} %get-tuple-element.12.ranks, bf16[40,24576]{1,0:T(8,128)(2,1)} %bitcast.18), custom_call_target="tpu_custom_call" | custom-call | tf_op jit(solution)/shard_map/pallas_call | solution.py:415
  51.8 0.0 copy-start.3
  51.8 0.0 all-to-all-done.mine
  51.8 9.2 %all-to-all-start.1 = ((bf16[32,64,128]{2,1,0:T(8,128)(2,1)}), bf16[32,64,128]{2,1,0:T(8,128)(2,1)S(1)}, u32[]{:S(2)}, u32[]{:S(2)}) async-start(bf16[32,64,128]{2,1,0:T(8,128)(2,1)} %shard_map.114), calls=%async_computation.1 | async-start | bytes 1048576 | tf_op jit(solution)/shard_map/all_to_all | solution.py:497
  61.1 2.1 %collective-permute-start.2 = (bf16[32,80,128]{2,1,0:T(8,128)(2,1)S(1)}, bf16[32,80,128]{2,1,0:T(8,128)(2,1)S(1)}, u32[]{:S(2)}, u32[]{:S(2)}) collective-permute-start(bf16[32,80,128]{2,1,0:T(8,128)(2,1)S(1)} %slice.40), channel_id=1, source_target_pairs={{0,1},{1,0},{2,3},{3,2},{4,5},{5,4},{6,7},{7,6},{8,9},{9,8},{10,11... | collective-permute-start | bytes 1966088 | tf_op jit(solution)/shard_map/ppermute | solution.py:496
  63.2 2.0 %collective-permute-start.5 = (bf16[512,1280]{1,0:T(8,128)(2,1)}, bf16[512,1280]{1,0:T(8,128)(2,1)}, u32[]{:S(2)}, u32[]{:S(2)}) collective-permute-start(bf16[512,1280]{1,0:T(8,128)(2,1)} %refs_4_.1), channel_id=1, source_target_pairs={{0,4},{1,5},{2,6},{3,7},{4,0},{5,1},{6,2},{7,3},{8,12},{9,13},{10,... | collective-permute-start | bytes 3932168 | tf_op jit(solution)/shard_map/ppermute | solution.py:482
  65.2 0.1 pad_add_fusion.spot
  65.2 0.0 collective-permute-done.1.refs_7_
  65.2 1.2 %slice.39 = bf16[1,1]{1,0:T(2,128)(2,1)} slice(bf16[512,1280]{1,0:T(8,128)(2,1)} %collective-permute-done.1.refs_7_), slice={[0:1], [0:1]} | slice | bytes 4 | tf_op jit(solution)/shard_map/slice | solution.py:498
  66.4 1.2 %slice.38 = bf16[1,1]{1,0:T(2,128)(2,1)} slice(bf16[512,1280]{1,0:T(8,128)(2,1)} %collective-permute-done.refs_6_), slice={[0:1], [0:1]} | slice | bytes 4 | tf_op jit(solution)/shard_map/slice | solution.py:498
  67.6 1.4 %maximum_convert_fusion.seen = f32[2]{0:T(128)S(1)} fusion(bf16[1]{0:T(256)(128)(2,1)} %bitcast.1, bf16[1]{0:T(256)(128)(2,1)} %bitcast), kind=kLoop, calls=%fused_computation | loop fusion | flops 8 | bytes 12 | tf_op jit(solution)/shard_map/convert_element_type | solution.py:498
  69.0 7.1 %all-to-all-done.1.means = bf16[32,64,128]{2,1,0:T(8,128)(2,1)S(1)} async-done(((bf16[32,64,128]{2,1,0:T(8,128)(2,1)}), bf16[32,64,128]{2,1,0:T(8,128)(2,1)S(1)}, u32[]{:S(2)}, u32[]{:S(2)}) %all-to-all-start.1) | async-done | bytes 524320 | tf_op jit(solution)/shard_map/all_to_all | solution.py:497
  76.0 0.0 copy-start.2
  76.1 0.0 copy-start.4
  76.1 2.8 %shard_map.115 = (bf16[192,256]{1,0:T(8,128)(2,1)}, bf16[768,256]{1,0:T(8,128)(2,1)}) custom-call(f32[2]{0:T(128)S(1)} %maximum_convert_fusion.seen, s32[2]{0:T(128)S(1)} %pad_add_fusion.spot, bf16[32,144,128]{2,1,0:T(8,128)(2,1)S(1)} %all-to-all-done.mine, bf16[32,80,128]{2,1,0:T(8,128)(2,1)S(1)} %collective-permute-done.2.theirs, ...), custom_call_target="tpu_custom_call" | custom-call | tf_op jit(solution)/shard_map/pallas_call | solution.py:500
  78.9 6.3 %all-to-all-start.2 = ((bf16[32,24,256]{2,1,0:T(8,128)(2,1)}), bf16[32,24,256]{2,1,0:T(8,128)(2,1)S(1)}, u32[]{:S(2)}, u32[]{:S(2)}) async-start(bf16[32,24,256]{2,1,0:T(8,128)(2,1)} %bitcast.14), calls=%async_computation.2 | async-start | bytes 786432 | tf_op jit(solution)/shard_map/all_to_all | solution.py:519
  85.3 0.4 shard_map.116.refs_1_
  85.7 2.3 %collective-permute-start.4 = (bf16[2,784,128]{2,1,0:T(8,128)(2,1)S(1)}, bf16[2,784,128]{2,1,0:T(8,128)(2,1)S(1)}, u32[]{:S(2)}, u32[]{:S(2)}) collective-permute-start(bf16[2,784,128]{2,1,0:T(8,128)(2,1)S(1)} %shard_map.116.refs_1_), channel_id=1, source_target_pairs={{0,1},{1,0},{2,3},{3,2},{4,5},{5,4},{6,7},{7,6},{8,9},{9,8},{10,11... | collective-permute-start | bytes 1204232 | tf_op jit(solution)/shard_map/ppermute | solution.py:518
  88.0 9.7 %all-to-all-done.2 = bf16[32,24,256]{2,1,0:T(8,128)(2,1)S(1)} async-done(((bf16[32,24,256]{2,1,0:T(8,128)(2,1)}), bf16[32,24,256]{2,1,0:T(8,128)(2,1)S(1)}, u32[]{:S(2)}, u32[]{:S(2)}) %all-to-all-start.2) | async-done | bytes 393248 | tf_op jit(solution)/shard_map/all_to_all | solution.py:519
  97.8 3.7 %collective-permute-start.3 = (bf16[768,256]{1,0:T(8,128)(2,1)S(1)}, bf16[768,256]{1,0:T(8,128)(2,1)S(1)}, u32[]{:S(2)}, u32[]{:S(2)}) collective-permute-start(bf16[768,256]{1,0:T(8,128)(2,1)S(1)} %bitcast.19), channel_id=1, source_target_pairs={{0,1},{1,0},{2,3},{3,2},{4,5},{5,4},{6,7},{7,6},{8,9},{9,8},{10,11... | collective-permute-start | bytes 1179656 | tf_op jit(solution)/shard_map/ppermute | solution.py:521
  101.4 0.7 fusion.bases
  102.1 0.7 collective-permute-done.3.refs_2_
  102.8 0.1 copy-done.6
  102.9 0.8 copy-done.7
  103.7 5.8 %shard_map.117 = (f32[8,128]{1,0:T(8,128)}, f32[8,128]{1,0:T(8,128)}) custom-call(s32[4]{0:T(128)} %fusion.bases, bf16[768,256]{1,0:T(8,128)(2,1)} %bitcast.20, bf16[2,784,128]{2,1,0:T(8,128)(2,1)} %copy-done, bf16[768,256]{1,0:T(8,128)(2,1)} %copy-done.7, bf16[2,784,128]{2,1,0:T(8,128)(2,1)} %copy-done.6, bf16[512,1280]{1,0:T(8,128)(2,1)} %refs_4_.1, ...), custom_call_target="tpu_custom_call" | custom-call | tf_op jit(solution)/shard_map/pallas_call | solution.py:448
  109.5 0.4 collective-permute-start.6
  109.9 1.1 collective-permute-done.6
  111.0 1.3 %add_subtract_fusion = f32[1,128]{1,0:T(1,128)} fusion(f32[8,128]{1,0:T(8,128)S(1)} %collective-permute-done.6, f32[8,128]{1,0:T(8,128)} %get-tuple-element.16), kind=kLoop, calls=%fused_computation.4 | loop fusion | flops 1152 | bytes 3584 | tf_op jit(solution)/shard_map/sub | solution.py:527
  (16 shorter events, 0.1 us)
Async XLA Ops:
  5.7 46.1 %all-to-all-start = ((bf16[32,144,128]{2,1,0:T(8,128)(2,1)}), bf16[32,144,128]{2,1,0:T(8,128)(2,1)S(1)}, u32[]{:S(2)}, u32[]{:S(2)}) async-start(bf16[32,144,128]{2,1,0:T(8,128)(2,1)} %get-tuple-element.10), calls=%async_computation | async-start | bytes 2359296 | tf_op jit(solution)/shard_map/all_to_all | solution.py:494
  17.8 47.4 %collective-permute-start.1 = (bf16[512,1280]{1,0:T(8,128)(2,1)}, bf16[512,1280]{1,0:T(8,128)(2,1)}, u32[]{:S(2)}, u32[]{:S(2)}) collective-permute-start(bf16[512,1280]{1,0:T(8,128)(2,1)} %refs_4_.1), channel_id=1, source_target_pairs={{0,6},{1,7},{2,0},{3,1},{4,2},{5,3},{6,4},{7,5},{8,14},{9,15},{10,... | collective-permute-start | bytes 3932168 | tf_op jit(solution)/shard_map/ppermute | solution.py:482
  20.3 46.1 %collective-permute-start = (bf16[512,1280]{1,0:T(8,128)(2,1)}, bf16[512,1280]{1,0:T(8,128)(2,1)}, u32[]{:S(2)}, u32[]{:S(2)}) collective-permute-start(bf16[512,1280]{1,0:T(8,128)(2,1)} %refs_4_.1), channel_id=1, source_target_pairs={{0,2},{1,3},{2,4},{3,5},{4,6},{5,7},{6,0},{7,1},{8,10},{9,11},{10,... | collective-permute-start | bytes 3932168 | tf_op jit(solution)/shard_map/ppermute | solution.py:482
  51.8 24.2 %copy-start.3 = (f32[256]{0:T(256)S(1)}, f32[256]{0:T(256)}, u32[]{:S(2)}) copy-start(f32[256]{0:T(256)} %param.18) | copy-start | bytes 3076
  51.8 24.2 %all-to-all-start.1 = ((bf16[32,64,128]{2,1,0:T(8,128)(2,1)}), bf16[32,64,128]{2,1,0:T(8,128)(2,1)S(1)}, u32[]{:S(2)}, u32[]{:S(2)}) async-start(bf16[32,64,128]{2,1,0:T(8,128)(2,1)} %shard_map.114), calls=%async_computation.1 | async-start | bytes 1048576 | tf_op jit(solution)/shard_map/all_to_all | solution.py:497
  61.1 14.9 %collective-permute-start.2 = (bf16[32,80,128]{2,1,0:T(8,128)(2,1)S(1)}, bf16[32,80,128]{2,1,0:T(8,128)(2,1)S(1)}, u32[]{:S(2)}, u32[]{:S(2)}) collective-permute-start(bf16[32,80,128]{2,1,0:T(8,128)(2,1)S(1)} %slice.40), channel_id=1, source_target_pairs={{0,1},{1,0},{2,3},{3,2},{4,5},{5,4},{6,7},{7,6},{8,9},{9,8},{10,11... | collective-permute-start | bytes 1966088 | tf_op jit(solution)/shard_map/ppermute | solution.py:496
  63.2 38.9 %collective-permute-start.5 = (bf16[512,1280]{1,0:T(8,128)(2,1)}, bf16[512,1280]{1,0:T(8,128)(2,1)}, u32[]{:S(2)}, u32[]{:S(2)}) collective-permute-start(bf16[512,1280]{1,0:T(8,128)(2,1)} %refs_4_.1), channel_id=1, source_target_pairs={{0,4},{1,5},{2,6},{3,7},{4,0},{5,1},{6,2},{7,3},{8,12},{9,13},{10,... | collective-permute-start | bytes 3932168 | tf_op jit(solution)/shard_map/ppermute | solution.py:482
  76.0 9.2 %copy-start.1 = (s32[16,128]{1,0:T(8,128)S(1)}, s32[16,128]{1,0:T(8,128)}, u32[]{:S(2)}) copy-start(s32[16,128]{1,0:T(8,128)} %get-tuple-element.15.place) | copy-start | bytes 24580
  76.0 9.2 %copy-start.2 = (s32[10,1,128]{2,1,0:T(1,128)S(1)}, s32[10,1,128]{2,1,0:T(1,128)}, u32[]{:S(2)}) copy-start(s32[10,1,128]{2,1,0:T(1,128)} %mask.1) | copy-start | bytes 15364
  76.1 9.2 %copy-start.4 = (s32[1,128]{1,0:T(1,128)S(1)}, s32[1,128]{1,0:T(1,128)}, u32[]{:S(2)}) copy-start(s32[1,128]{1,0:T(1,128)} %labels.1) | copy-start | bytes 1540
  78.9 18.9 %all-to-all-start.2 = ((bf16[32,24,256]{2,1,0:T(8,128)(2,1)}), bf16[32,24,256]{2,1,0:T(8,128)(2,1)S(1)}, u32[]{:S(2)}, u32[]{:S(2)}) async-start(bf16[32,24,256]{2,1,0:T(8,128)(2,1)} %bitcast.14), calls=%async_computation.2 | async-start | bytes 786432 | tf_op jit(solution)/shard_map/all_to_all | solution.py:519
  85.7 17.1 %copy-start = (bf16[2,784,128]{2,1,0:T(8,128)(2,1)}, bf16[2,784,128]{2,1,0:T(8,128)(2,1)S(1)}, u32[]{:S(2)}) copy-start(bf16[2,784,128]{2,1,0:T(8,128)(2,1)S(1)} %shard_map.116.refs_1_) | copy-start | bytes 1204228
  85.7 16.4 %collective-permute-start.4 = (bf16[2,784,128]{2,1,0:T(8,128)(2,1)S(1)}, bf16[2,784,128]{2,1,0:T(8,128)(2,1)S(1)}, u32[]{:S(2)}, u32[]{:S(2)}) collective-permute-start(bf16[2,784,128]{2,1,0:T(8,128)(2,1)S(1)} %shard_map.116.refs_1_), channel_id=1, source_target_pairs={{0,1},{1,0},{2,3},{3,2},{4,5},{5,4},{6,7},{7,6},{8,9},{9,8},{10,11... | collective-permute-start | bytes 1204232 | tf_op jit(solution)/shard_map/ppermute | solution.py:518
  97.8 5.0 %copy-start.5 = (bf16[32,24,256]{2,1,0:T(8,128)(2,1)}, bf16[32,24,256]{2,1,0:T(8,128)(2,1)S(1)}, u32[]{:S(2)}) copy-start(bf16[32,24,256]{2,1,0:T(8,128)(2,1)S(1)} %all-to-all-done.2) | copy-start | bytes 1179652
  97.8 5.0 %collective-permute-start.3 = (bf16[768,256]{1,0:T(8,128)(2,1)S(1)}, bf16[768,256]{1,0:T(8,128)(2,1)S(1)}, u32[]{:S(2)}, u32[]{:S(2)}) collective-permute-start(bf16[768,256]{1,0:T(8,128)(2,1)S(1)} %bitcast.19), channel_id=1, source_target_pairs={{0,1},{1,0},{2,3},{3,2},{4,5},{5,4},{6,7},{7,6},{8,9},{9,8},{10,11... | collective-permute-start | bytes 1179656 | tf_op jit(solution)/shard_map/ppermute | solution.py:521
  102.1 0.8 copy-start.6
  102.9 0.8 copy-start.7
  109.5 1.5 %collective-permute-start.6 = (f32[8,128]{1,0:T(8,128)}, f32[8,128]{1,0:T(8,128)S(1)}, u32[]{:S(2)}, u32[]{:S(2)}) collective-permute-start(f32[8,128]{1,0:T(8,128)} %get-tuple-element.17), channel_id=1, source_target_pairs={{0,1},{1,0},{2,3},{3,2},{4,5},{5,4},{6,7},{7,6},{8,9},{9,8},{10,11... | collective-permute-start | bytes 12296 | tf_op jit(solution)/shard_map/ppermute | solution.py:524

commit v7 on v6

--- a/solution.py
+++ b/solution.py
@@ -19,12 +19,13 @@
 UNION = 24
 NAMED = FEAT * UNION
 SLAB = 256
+HOPS = (0, 4, 6, 2)
 UNROLL = 64
 LEAST = 3
 LINES = ROWS // 128
 CHUNK = 1024
 PAIRS = 4
-TABLE_STEP = 8
+TABLE_STEP = 16
 MOST = 60 * 2**20
 F32 = jnp.float32
 BF16 = jnp.bfloat16
@@ -183,10 +184,11 @@
         span = pl.ds(pl.multiple_of(t * third + step * piece, piece), piece)
         return pltpu.make_async_copy(source.at[:, span], features.at[:, span], loaded.at[step, t])
 
+    fetch(0).start()
     for step in range(third // piece):
         for t in range(3):
             load(step, t).start()
-    for chunk in range(ROWS // CHUNK):
+    for chunk in range(1, ROWS // CHUNK):
         fetch(chunk).start()
 
     lane = iota((128, 128), 1)
@@ -265,7 +267,7 @@
 
 
 def hidden_kernel(
-    seen, spot, mine, theirs, means, bias, hidden, rows, stacked, held, other, marks, chosen
+    spot, mine, theirs, means, bias, hidden, rows, stacked, held, other, marks, chosen
 ):
     for source in range(FEAT):
         own = mine[source].astype(F32)
@@ -318,19 +320,11 @@
     picks[1] = jnp.concatenate([own, blank], axis=0).astype(BF16)
 
 
-def loss_kernel(bases, *refs):
-    sources, (stats, other) = refs[: 4 + NODE // 2], refs[4 + NODE // 2 : 6 + NODE // 2]
-    inputs, logits, *held, arrived = refs[6 + NODE // 2 :]
-    copies = [
-        pltpu.make_async_copy(source, ref, arrived.at[k])
-        for k, (source, ref) in enumerate(zip(sources, held))
-    ]
-    for copy in copies:
-        copy.start()
+def loss_kernel(spot, *refs):
+    held, blocks = refs[:4], refs[4 : 4 + NODE // 2]
+    stats, other, inputs, logits = refs[4 + NODE // 2 :]
     offsets = []
     for side in range(2):
-        copies[2 * side].wait()
-        copies[2 * side + 1].wait()
         rows, picks = held[2 * side], held[2 * side + 1]
         total, own = picks[0][:NAMED], picks[1][:NAMED]
         count = contract(total, jnp.ones((NAMED, 128), BF16), 0, 0)[:, :1]
@@ -341,7 +335,6 @@
         parts = picks[0][NAMED:].astype(F32)
         label = jnp.broadcast_to(parts[:1] * 128.0 + parts[1:2], (TARGETS, TARGETS)).T
         offsets.append(label.astype(jnp.int32) - iota((TARGETS, TARGETS), 1))
-    blocks = held[4:]
     width = blocks[0].shape[1]
     start = (
         jnp.full((TARGETS, TARGETS), -jnp.inf, F32),
@@ -352,8 +345,6 @@
     for step in range(2 * len(blocks) + 1):
         block, side = step // 2, step % 2
         if block < len(blocks):
-            if side == 0:
-                copies[4 + block].wait()
             mine = inputs[pl.ds(side * TARGETS, TARGETS), :]
             logits[step % 2] = contract(mine, blocks[block][...], 1, 0)
         if step > 0:
@@ -361,7 +352,7 @@
             last = logits.at[(step - 1) % 2]
             largest, summed, picked = running[side]
             spans = [pl.ds(k * 128, 128) for k in range(width // 128)]
-            here = offsets[side] - bases[block]
+            here = offsets[side] - ((spot[0] + HOPS[block]) & 7) * width
             now = largest
             for span in spans:
                 now = jnp.maximum(now, last[:, span])
@@ -443,21 +434,35 @@
     )(place, mask, labels)
 
 
-def call_loss(bases, rows, picks, rows_there, picks_there, blocks):
+def call_loss(spot, rows, picks, rows_there, picks_there, blocks):
     sources = [rows, picks, rows_there, picks_there, *blocks]
     return pl.pallas_call(
         loss_kernel,
         out_shape=[jax.ShapeDtypeStruct((8, TARGETS), F32)] * 2,
-        in_specs=[SMEM] + [HBM] * len(sources),
+        in_specs=[SMEM] + [VMEM] * len(sources),
         out_specs=[VMEM, VMEM],
         scratch_shapes=[
             pltpu.VMEM((2 * TARGETS, 2 * HIDDEN), BF16),
             pltpu.VMEM((2, TARGETS, blocks[0].shape[1]), F32),
-            *[pltpu.VMEM(source.shape, BF16) for source in sources],
-            pltpu.SemaphoreType.DMA((len(sources),)),
         ],
-        compiler_params=pltpu.CompilerParams(vmem_limit_bytes=MOST),
-    )(bases, *sources)
+        compiler_params=pltpu.CompilerParams(vmem_limit_bytes=16 * 2**20),
+    )(spot, *sources)
+
+
+def join_kernel(here, there, loss):
+    most = jnp.maximum(here[0:1], there[0:1])
+    total = here[1:2] * jnp.exp(here[0:1] - most) + there[1:2] * jnp.exp(there[0:1] - most)
+    loss[...] = most + jnp.log(total) - (here[2:3] + there[2:3])
+
+
+def call_join(here, there):
+    return pl.pallas_call(
+        join_kernel,
+        out_shape=jax.ShapeDtypeStruct((1, TARGETS), F32),
+        in_specs=[VMEM, VMEM],
+        out_specs=VMEM,
+        compiler_params=pltpu.CompilerParams(vmem_limit_bytes=2**20),
+    )(here, there)
 
 
 def body(
@@ -477,8 +482,8 @@
     table = features[:, 0, :]
     swap = [(device, device ^ 1) for device in range(NODE)]
     blocks = [class_weight]
-    for hops in (4, 2, 6):
-        around = [(device, (device + hops) % NODE) for device in range(NODE)]
+    for hops in HOPS[1:]:
+        around = [(device, (device - hops) % NODE) for device in range(NODE)]
         blocks.append(lax.ppermute(class_weight, "node", around))
     own, place, slots, ranks = call_prepare(
         core[None],
@@ -495,7 +500,7 @@
     send = call_gather(slots.reshape(-1), ranks, table)
     theirs = lax.ppermute(own[:, : 2 * WIDTH], "node", swap)
     means = lax.all_to_all(send, "feat", 0, 0)
-    seen = jnp.stack([block[0, 0] for block in blocks[2:]]).astype(F32)
+    means, *blocks[2:] = lax.optimization_barrier((means, *blocks[2:]))
     side = jnp.stack([core, lax.axis_index("feat").astype(jnp.int32) & 1])
     hidden, rows = pl.pallas_call(
         hidden_kernel,
@@ -503,7 +508,7 @@
             jax.ShapeDtypeStruct((OWN, HIDDEN), BF16),
             jax.ShapeDtypeStruct((FEAT * UNION, HIDDEN), BF16),
         ),
-        in_specs=[SMEM] * 2 + [VMEM] * 4,
+        in_specs=[SMEM] + [VMEM] * 4,
         out_specs=(VMEM, VMEM),
         scratch_shapes=[
             pltpu.VMEM((FEAT * 80, 256), BF16),
@@ -513,18 +518,15 @@
             pltpu.VMEM((FEAT * UNION, SLAB), F32),
         ],
         compiler_params=pltpu.CompilerParams(vmem_limit_bytes=24 * 2**20),
-    )(seen, side, own, theirs, means, first_bias[None, :])
+    )(side, own, theirs, means, first_bias[None, :])
     picks = call_pick(place, second_mask, labels)
     picks_there = lax.ppermute(picks, "node", swap)
     rows = lax.all_to_all(rows.reshape(FEAT, UNION, HIDDEN), "feat", 0, 0)
     rows = rows.reshape(FEAT * UNION, HIDDEN)
     rows_there = lax.ppermute(rows, "node", swap)
-    bases = (jnp.stack([spot, spot + 4, spot + 6, spot + 2]) & 7) * class_weight.shape[1]
-    here, there = call_loss(bases, rows, picks, rows_there, picks_there, blocks)
+    here, there = call_loss(spot[None], rows, picks, rows_there, picks_there, blocks)
     there = lax.ppermute(there, "node", swap)
-    most = jnp.maximum(here[0:1], there[0:1])
-    total = here[1:2] * jnp.exp(here[0:1] - most) + there[1:2] * jnp.exp(there[0:1] - most)
-    loss = most + jnp.log(total) - (here[2:3] + there[2:3])
+    loss = call_join(here, there)
     return (hidden[None], loss)
 
 

time: 113 us -> 110 us (0.973)
  other arithmetic: 3.43 us -> 0.07 us
  local copies, waits for them, and re-layouts: 3.29 us -> 0.92 us
  waiting for transfers between devices: 18.6 us -> 20.4 us
  starting transfers between devices: 40.6 us -> 42.1 us
    all_to_all x1, waiting for transfers between devices: 7.07 us -> 9.85 us  [body(): means = lax.all_to_all(send, 'feat', 0, 0)]
    slice x2 -> x0, local copies, waits for them, and re-layouts: 2.35 us -> none  [body(): seen = jnp.stack([block[0, 0] for block in blocks[2:]]).astype(F32)]
    convert_element_type x1 -> x0, other arithmetic: 1.37 us -> none  [body(): seen = jnp.stack([block[0, 0] for block in blocks[2:]]).astype(F32)]
    sub x1 -> x0, other arithmetic: 1.33 us -> none  [body(): loss = most + jnp.log(total) - (here[2:3] + there[2:3])]
    all_to_all x1, waiting for transfers between devices: 9.73 us -> 8.4 us  [body(): rows = lax.all_to_all(rows.reshape(FEAT, UNION, HIDDEN), 'feat', 0, 0)]
    pallas_call x1, Pallas kernels: 5.84 us -> 4.53 us  [call_loss(): pl.pallas_call(loss_kernel, out_shape=[jax.ShapeDtypeStruct((8, TARGETS),...]
  transfers between devices with their start and end apart: 10 -> 10, of which waited for: 4 -> 4; matrix products, arithmetic and copies ran while one was open for 4% -> 1% of each run, Pallas kernels for 31% -> 32%
where the time goes in v7:
time: 110 us
  Pallas kernels  45.3 us (41%)
  starting transfers between devices  42.1 us (38%)
  waiting for transfers between devices  20.4 us (19%)
    pallas_call x1, Pallas kernels, call_gather(): pl.pallas_call(gather_kernel, out_shape=jax.ShapeDtypeStruct((FEAT, 64, 1...  31.4 us
    all_to_all x1, starting transfers between devices, body(): own = lax.all_to_all(own, 'feat', 0, 0)  12.2 us
    all_to_all x1, waiting for transfers between devices, body(): means = lax.all_to_all(send, 'feat', 0, 0)  9.85 us
    all_to_all x1, starting transfers between devices, body(): means = lax.all_to_all(send, 'feat', 0, 0)  9.23 us
    all_to_all x1, waiting for transfers between devices, body(): rows = lax.all_to_all(rows.reshape(FEAT, UNION, HIDDEN), 'feat', 0, 0)  8.4 us
    all_to_all x1, starting transfers between devices, body(): rows = lax.all_to_all(rows.reshape(FEAT, UNION, HIDDEN), 'feat', 0, 0)  6.32 us
    pallas_call x1, Pallas kernels, call_prepare(): pl.pallas_call(prepare_kernel, out_shape=(jax.ShapeDtypeStruct((FEAT, 144...  5.06 us
    ppermute x1, starting transfers between devices, body(): rows_there = lax.ppermute(rows, 'node', swap)  4.68 us
  transfers between devices with their start and end apart: 10, of which 4 were waited for; matrix products, arithmetic and copies ran while one was open for 1% of the time, Pallas kernels for 32%

profile of v7, /device:TPU:1, one launch (start us, length us, event | category | flops | bytes accessed | tf_op | source)
XLA Modules:
  0.0 109.6 jit_solution(514088037447542507)
XLA Ops:
  0.6 5.1 %shard_map.113 = (bf16[32,144,128]{2,1,0:T(8,128)(2,1)}, s32[16,128]{1,0:T(8,128)}, s32[528,128]{1,0:T(8,128)}, s32[48,128]{1,0:T(8,128)}) custom-call(s32[1]{0:T(128)} %bitcast.core, s32[10,1,128]{2,1,0:T(1,128)} %refs_0_.1, s32[1,128]{1,0:T(1,128)} %refs_1_.1, bf16[2,40,256]{2,1,0:T(8,128)(2,1)} %refs_2_.1, bf16[40,24576]{1,0:T(8,128)(2,1)} %bitcast.14, ...), custom_call_target="tpu_custom_call" | custom-call | flops 100000000 | bytes 10000000 | tf_op jit(solution)/shard_map/pallas_call | solution.py:383
  5.7 0.0 copy-start
  5.7 12.2 %all-to-all-start = ((bf16[32,144,128]{2,1,0:T(8,128)(2,1)}), bf16[32,144,128]{2,1,0:T(8,128)(2,1)S(1)}, u32[]{:S(2)}, u32[]{:S(2)}) async-start(bf16[32,144,128]{2,1,0:T(8,128)(2,1)} %get-tuple-element.13), calls=%async_computation | async-start | bytes 2359296 | tf_op jit(solution)/shard_map/all_to_all | solution.py:499
  17.9 1.3 %collective-permute-start.1 = (bf16[512,1280]{1,0:T(8,128)(2,1)S(1)}, bf16[512,1280]{1,0:T(8,128)(2,1)}, u32[]{:S(2)}, u32[]{:S(2)}) collective-permute-start(bf16[512,1280]{1,0:T(8,128)(2,1)S(1)} %copy-done), channel_id=1, source_target_pairs={{0,2},{1,3},{2,4},{3,5},{4,6},{5,7},{6,0},{7,1},{8,10},{9,11},{10,... | collective-permute-start | bytes 3932168 | tf_op jit(solution)/shard_map/ppermute | solution.py:487
  19.2 1.5 %collective-permute-start.2 = (bf16[512,1280]{1,0:T(8,128)(2,1)S(1)}, bf16[512,1280]{1,0:T(8,128)(2,1)}, u32[]{:S(2)}, u32[]{:S(2)}) collective-permute-start(bf16[512,1280]{1,0:T(8,128)(2,1)S(1)} %copy-done), channel_id=1, source_target_pairs={{0,6},{1,7},{2,0},{3,1},{4,2},{5,3},{6,4},{7,5},{8,14},{9,15},{10,... | collective-permute-start | bytes 3932168 | tf_op jit(solution)/shard_map/ppermute | solution.py:487
  20.7 31.4 %shard_map.114 = bf16[32,64,128]{2,1,0:T(8,128)(2,1)} custom-call(s32[67584]{0:T(1024)} %bitcast.16, s32[48,128]{1,0:T(8,128)} %get-tuple-element.15.ranks, bf16[40,24576]{1,0:T(8,128)(2,1)} %bitcast.15), custom_call_target="tpu_custom_call" | custom-call | tf_op jit(solution)/shard_map/pallas_call | solution.py:406
  52.0 0.0 copy-start.3
  52.1 0.0 all-to-all-done.mine
  52.1 9.2 %all-to-all-start.1 = ((bf16[32,64,128]{2,1,0:T(8,128)(2,1)}), bf16[32,64,128]{2,1,0:T(8,128)(2,1)S(1)}, u32[]{:S(2)}, u32[]{:S(2)}) async-start(bf16[32,64,128]{2,1,0:T(8,128)(2,1)} %shard_map.114), calls=%async_computation.1 | async-start | bytes 1048576 | tf_op jit(solution)/shard_map/all_to_all | solution.py:502
  61.3 0.9 slice.4
  62.2 2.4 %collective-permute-start = (bf16[32,80,128]{2,1,0:T(8,128)(2,1)}, bf16[32,80,128]{2,1,0:T(8,128)(2,1)}, u32[]{:S(2)}, u32[]{:S(2)}) collective-permute-start(bf16[32,80,128]{2,1,0:T(8,128)(2,1)} %slice.4), channel_id=1, source_target_pairs={{0,1},{1,0},{2,3},{3,2},{4,5},{5,4},{6,7},{7,6},{8,9},{9,8},{10,11... | collective-permute-start | bytes 1966088 | tf_op jit(solution)/shard_map/ppermute | solution.py:501
  64.5 1.4 %collective-permute-start.5 = (bf16[512,1280]{1,0:T(8,128)(2,1)S(1)}, bf16[512,1280]{1,0:T(8,128)(2,1)}, u32[]{:S(2)}, u32[]{:S(2)}) collective-permute-start(bf16[512,1280]{1,0:T(8,128)(2,1)S(1)} %copy-done), channel_id=1, source_target_pairs={{0,4},{1,5},{2,6},{3,7},{4,0},{5,1},{6,2},{7,3},{8,12},{9,13},{10,... | collective-permute-start | bytes 3932168 | tf_op jit(solution)/shard_map/ppermute | solution.py:487
  65.9 0.1 pad_add_fusion.spot
  66.0 9.8 %all-to-all-done.1.means = bf16[32,64,128]{2,1,0:T(8,128)(2,1)S(1)} async-done(((bf16[32,64,128]{2,1,0:T(8,128)(2,1)}), bf16[32,64,128]{2,1,0:T(8,128)(2,1)S(1)}, u32[]{:S(2)}, u32[]{:S(2)}) %all-to-all-start.1) | async-done | bytes 524320 | tf_op jit(solution)/shard_map/all_to_all | solution.py:502
  75.9 0.0 collective-permute-done.1.refs_6_
  75.9 0.0 collective-permute-done.2.refs_7_
  75.9 0.0 collective-permute-done.theirs
  75.9 0.0 copy-start.2
  75.9 0.0 copy-start.4
  75.9 3.4 %shard_map.115 = (bf16[192,256]{1,0:T(8,128)(2,1)}, bf16[768,256]{1,0:T(8,128)(2,1)}) custom-call(s32[2]{0:T(128)S(1)} %pad_add_fusion.spot, bf16[32,144,128]{2,1,0:T(8,128)(2,1)S(1)} %all-to-all-done.mine, bf16[32,80,128]{2,1,0:T(8,128)(2,1)} %collective-permute-done.theirs, bf16[32,64,128]{2,1,0:T(8,128)(2,1)S(1)} %all-to-all-done.1.means, ...), custom_call_target="tpu_custom_call" | custom-call | tf_op jit(solution)/shard_map/pallas_call | solution.py:505
  79.3 6.3 %all-to-all-start.2 = ((bf16[32,24,256]{2,1,0:T(8,128)(2,1)}), bf16[32,24,256]{2,1,0:T(8,128)(2,1)S(1)}, u32[]{:S(2)}, u32[]{:S(2)}) async-start(bf16[32,24,256]{2,1,0:T(8,128)(2,1)} %bitcast.9), calls=%async_computation.2 | async-start | bytes 786432 | tf_op jit(solution)/shard_map/all_to_all | solution.py:524
  85.7 0.4 shard_map.116.refs_1_
  86.1 2.7 %collective-permute-start.4 = (bf16[2,784,128]{2,1,0:T(8,128)(2,1)S(1)}, bf16[2,784,128]{2,1,0:T(8,128)(2,1)S(1)}, u32[]{:S(2)}, u32[]{:S(2)}) collective-permute-start(bf16[2,784,128]{2,1,0:T(8,128)(2,1)S(1)} %shard_map.116.refs_1_), channel_id=1, source_target_pairs={{0,1},{1,0},{2,3},{3,2},{4,5},{5,4},{6,7},{7,6},{8,9},{9,8},{10,11... | collective-permute-start | bytes 1204232 | tf_op jit(solution)/shard_map/ppermute | solution.py:523
  88.8 8.4 %all-to-all-done.2 = bf16[32,24,256]{2,1,0:T(8,128)(2,1)S(1)} async-done(((bf16[32,24,256]{2,1,0:T(8,128)(2,1)}), bf16[32,24,256]{2,1,0:T(8,128)(2,1)S(1)}, u32[]{:S(2)}, u32[]{:S(2)}) %all-to-all-start.2) | async-done | bytes 393248 | tf_op jit(solution)/shard_map/all_to_all | solution.py:524
  97.2 4.7 %collective-permute-start.3 = (bf16[768,256]{1,0:T(8,128)(2,1)S(1)}, bf16[768,256]{1,0:T(8,128)(2,1)S(1)}, u32[]{:S(2)}, u32[]{:S(2)}) collective-permute-start(bf16[768,256]{1,0:T(8,128)(2,1)S(1)} %bitcast.11), channel_id=1, source_target_pairs={{0,1},{1,0},{2,3},{3,2},{4,5},{5,4},{6,7},{7,6},{8,9},{9,8},{10,11... | collective-permute-start | bytes 1179656 | tf_op jit(solution)/shard_map/ppermute | solution.py:526
  101.9 0.0 collective-permute-done.4.refs_3_
  101.9 0.0 collective-permute-done.5.refs_5_
  101.9 1.3 %collective-permute-done.3.refs_2_ = bf16[768,256]{1,0:T(8,128)(2,1)S(1)} collective-permute-done((bf16[768,256]{1,0:T(8,128)(2,1)S(1)}, bf16[768,256]{1,0:T(8,128)(2,1)S(1)}, u32[]{:S(2)}, u32[]{:S(2)}) %collective-permute-start.3) | collective-permute-done | bytes 393248 | tf_op jit(solution)/shard_map/ppermute | solution.py:526
  103.3 4.5 %shard_map.117 = (f32[8,128]{1,0:T(8,128)S(1)}, f32[8,128]{1,0:T(8,128)S(1)}) custom-call(s32[1]{0:T(128)} %bitcast.8.spot, bf16[768,256]{1,0:T(8,128)(2,1)S(1)} %bitcast.12, bf16[2,784,128]{2,1,0:T(8,128)(2,1)S(1)} %shard_map.116.refs_1_, bf16[768,256]{1,0:T(8,128)(2,1)S(1)} %collective-permute-done.3.refs_2_, ...), custom_call_target="tpu_custom_call" | custom-call | tf_op jit(solution)/shard_map/pallas_call | solution.py:439
  107.8 0.4 collective-permute-start.6
  108.2 0.8 collective-permute-done.6.there
  109.1 0.5 shard_map.118
  (6 shorter events, 0.0 us)
Async XLA Ops:
  5.7 12.2 %copy-start = (bf16[512,1280]{1,0:T(8,128)(2,1)S(1)}, bf16[512,1280]{1,0:T(8,128)(2,1)}, u32[]{:S(2)}) copy-start(bf16[512,1280]{1,0:T(8,128)(2,1)} %refs_4_.1) | copy-start | bytes 3932164
  5.7 46.3 %all-to-all-start = ((bf16[32,144,128]{2,1,0:T(8,128)(2,1)}), bf16[32,144,128]{2,1,0:T(8,128)(2,1)S(1)}, u32[]{:S(2)}, u32[]{:S(2)}) async-start(bf16[32,144,128]{2,1,0:T(8,128)(2,1)} %get-tuple-element.13), calls=%async_computation | async-start | bytes 2359296 | tf_op jit(solution)/shard_map/all_to_all | solution.py:499
  17.9 57.9 %collective-permute-start.1 = (bf16[512,1280]{1,0:T(8,128)(2,1)S(1)}, bf16[512,1280]{1,0:T(8,128)(2,1)}, u32[]{:S(2)}, u32[]{:S(2)}) collective-permute-start(bf16[512,1280]{1,0:T(8,128)(2,1)S(1)} %copy-done), channel_id=1, source_target_pairs={{0,2},{1,3},{2,4},{3,5},{4,6},{5,7},{6,0},{7,1},{8,10},{9,11},{10,... | collective-permute-start | bytes 3932168 | tf_op jit(solution)/shard_map/ppermute | solution.py:487
  19.2 56.7 %collective-permute-start.2 = (bf16[512,1280]{1,0:T(8,128)(2,1)S(1)}, bf16[512,1280]{1,0:T(8,128)(2,1)}, u32[]{:S(2)}, u32[]{:S(2)}) collective-permute-start(bf16[512,1280]{1,0:T(8,128)(2,1)S(1)} %copy-done), channel_id=1, source_target_pairs={{0,6},{1,7},{2,0},{3,1},{4,2},{5,3},{6,4},{7,5},{8,14},{9,15},{10,... | collective-permute-start | bytes 3932168 | tf_op jit(solution)/shard_map/ppermute | solution.py:487
  52.0 23.8 %copy-start.3 = (f32[256]{0:T(256)S(1)}, f32[256]{0:T(256)}, u32[]{:S(2)}) copy-start(f32[256]{0:T(256)} %param.18) | copy-start | bytes 3076
  52.1 23.8 %all-to-all-start.1 = ((bf16[32,64,128]{2,1,0:T(8,128)(2,1)}), bf16[32,64,128]{2,1,0:T(8,128)(2,1)S(1)}, u32[]{:S(2)}, u32[]{:S(2)}) async-start(bf16[32,64,128]{2,1,0:T(8,128)(2,1)} %shard_map.114), calls=%async_computation.1 | async-start | bytes 1048576 | tf_op jit(solution)/shard_map/all_to_all | solution.py:502
  62.2 13.7 %collective-permute-start = (bf16[32,80,128]{2,1,0:T(8,128)(2,1)}, bf16[32,80,128]{2,1,0:T(8,128)(2,1)}, u32[]{:S(2)}, u32[]{:S(2)}) collective-permute-start(bf16[32,80,128]{2,1,0:T(8,128)(2,1)} %slice.4), channel_id=1, source_target_pairs={{0,1},{1,0},{2,3},{3,2},{4,5},{5,4},{6,7},{7,6},{8,9},{9,8},{10,11... | collective-permute-start | bytes 1966088 | tf_op jit(solution)/shard_map/ppermute | solution.py:501
  64.5 37.4 %collective-permute-start.5 = (bf16[512,1280]{1,0:T(8,128)(2,1)S(1)}, bf16[512,1280]{1,0:T(8,128)(2,1)}, u32[]{:S(2)}, u32[]{:S(2)}) collective-permute-start(bf16[512,1280]{1,0:T(8,128)(2,1)S(1)} %copy-done), channel_id=1, source_target_pairs={{0,4},{1,5},{2,6},{3,7},{4,0},{5,1},{6,2},{7,3},{8,12},{9,13},{10,... | collective-permute-start | bytes 3932168 | tf_op jit(solution)/shard_map/ppermute | solution.py:487
  75.9 9.7 %copy-start.1 = (s32[16,128]{1,0:T(8,128)S(1)}, s32[16,128]{1,0:T(8,128)}, u32[]{:S(2)}) copy-start(s32[16,128]{1,0:T(8,128)} %get-tuple-element.19.place) | copy-start | bytes 24580
  75.9 9.7 %copy-start.2 = (s32[10,1,128]{2,1,0:T(1,128)S(1)}, s32[10,1,128]{2,1,0:T(1,128)}, u32[]{:S(2)}) copy-start(s32[10,1,128]{2,1,0:T(1,128)} %mask.1) | copy-start | bytes 15364
  75.9 9.7 %copy-start.4 = (s32[1,128]{1,0:T(1,128)S(1)}, s32[1,128]{1,0:T(1,128)}, u32[]{:S(2)}) copy-start(s32[1,128]{1,0:T(1,128)} %labels.1) | copy-start | bytes 1540
  79.3 18.0 %all-to-all-start.2 = ((bf16[32,24,256]{2,1,0:T(8,128)(2,1)}), bf16[32,24,256]{2,1,0:T(8,128)(2,1)S(1)}, u32[]{:S(2)}, u32[]{:S(2)}) async-start(bf16[32,24,256]{2,1,0:T(8,128)(2,1)} %bitcast.9), calls=%async_computation.2 | async-start | bytes 786432 | tf_op jit(solution)/shard_map/all_to_all | solution.py:524
  86.1 15.8 %collective-permute-start.4 = (bf16[2,784,128]{2,1,0:T(8,128)(2,1)S(1)}, bf16[2,784,128]{2,1,0:T(8,128)(2,1)S(1)}, u32[]{:S(2)}, u32[]{:S(2)}) collective-permute-start(bf16[2,784,128]{2,1,0:T(8,128)(2,1)S(1)} %shard_map.116.refs_1_), channel_id=1, source_target_pairs={{0,1},{1,0},{2,3},{3,2},{4,5},{5,4},{6,7},{7,6},{8,9},{9,8},{10,11... | collective-permute-start | bytes 1204232 | tf_op jit(solution)/shard_map/ppermute | solution.py:523
  97.2 6.0 %collective-permute-start.3 = (bf16[768,256]{1,0:T(8,128)(2,1)S(1)}, bf16[768,256]{1,0:T(8,128)(2,1)S(1)}, u32[]{:S(2)}, u32[]{:S(2)}) collective-permute-start(bf16[768,256]{1,0:T(8,128)(2,1)S(1)} %bitcast.11), channel_id=1, source_target_pairs={{0,1},{1,0},{2,3},{3,2},{4,5},{5,4},{6,7},{7,6},{8,9},{9,8},{10,11... | collective-permute-start | bytes 1179656 | tf_op jit(solution)/shard_map/ppermute | solution.py:526
  107.8 1.2 %collective-permute-start.6 = (f32[8,128]{1,0:T(8,128)S(1)}, f32[8,128]{1,0:T(8,128)S(1)}, u32[]{:S(2)}, u32[]{:S(2)}) collective-permute-start(f32[8,128]{1,0:T(8,128)S(1)} %get-tuple-element.23), channel_id=1, source_target_pairs={{0,1},{1,0},{2,3},{3,2},{4,5},{5,4},{6,7},{7,6},{8,9},{9,8},{10,11... | collective-permute-start | bytes 12296 | tf_op jit(solution)/shard_map/ppermute | solution.py:528

commit v8 on v7

--- a/solution.py
+++ b/solution.py
@@ -169,7 +169,7 @@
 
 
 def gather_kernel(
-    slots, ranks, source, send, table, sums, lists, built, features, arrived, loaded, sent
+    slots, ranks, features, send, table, sums, lists, arrived
 ):
     size = (FAN + 1) * CHUNK
 
@@ -178,24 +178,13 @@
         return pltpu.make_async_copy(slots.at[span], lists.at[span], arrived.at[chunk])
 
     third = INPUTS // 3
-    piece = 128 * TABLE_STEP
-
-    def load(step, t):
-        span = pl.ds(pl.multiple_of(t * third + step * piece, piece), piece)
-        return pltpu.make_async_copy(source.at[:, span], features.at[:, span], loaded.at[step, t])
-
     fetch(0).start()
-    for step in range(third // piece):
-        for t in range(3):
-            load(step, t).start()
     for chunk in range(1, ROWS // CHUNK):
         fetch(chunk).start()
 
     lane = iota((128, 128), 1)
 
     def fill(step, carry):
-        for t in range(3):
-            load(step, t).wait()
         for part in range(TABLE_STEP):
             at = pl.multiple_of((step * TABLE_STEP + part) * 128, 128)
             blocks = [features[:, pl.ds(t * third + at, 128)].astype(F32) for t in range(3)]
@@ -257,36 +246,40 @@
                 owner = 2 * (step * PAIRS + part + pair)
                 for half in range(2):
                     tile = folded(block, half, jnp.zeros((8, 64), F32))
-                    built[owner + half] = tile.astype(BF16)
-        copies_out(built, send, sent, step).start()
+                    send[owner + half] = tile.astype(BF16)
         return carry
 
     lax.fori_loop(0, FEAT // 2 // PAIRS, pair_step, 0)
-    for step in range(FEAT // 8):
-        copies_out(built, send, sent, step).wait()
-
-
-def hidden_kernel(
-    spot, mine, theirs, means, bias, hidden, rows, stacked, held, other, marks, chosen
-):
+
+
+def unfolded(tile):
+    rest = jnp.concatenate([tile[40:64, :64], tile[40:56, 64:]], axis=0)
+    return jnp.concatenate([tile[:40], rest, jnp.zeros((40, 64), F32)], axis=1)
+
+
+def choose_kernel(own, chosen, marks):
     for source in range(FEAT):
-        own = mine[source].astype(F32)
-        mean = means[source].astype(F32)
-        held[pl.ds(source * 80, 80), :] = own[:80].astype(BF16)
-        other[pl.ds(source * 80, 80), :] = theirs[source].astype(F32).astype(BF16)
-        last, mean_last = own[120:144], mean[40:64]
-        stacked[pl.ds(source * 80, 80), pl.ds(0, 128)] = jnp.concatenate(
-            [own[80:120], mean[:40]], axis=0
-        ).astype(BF16)
-        stacked[pl.ds(source * 80, 80), pl.ds(128, 64)] = jnp.concatenate(
-            [last[:, :64], last[:16, 64:], mean_last[:, :64], mean_last[:16, 64:]], axis=0
-        ).astype(BF16)
+        last = own[source, pl.ds(128, 16), :].astype(F32)
         marks[pl.ds(source, 1), :] = jnp.concatenate(
-            [last[16:17, 64:], last[17:18, 64:], last[18:19, 64:], jnp.zeros((1, 64), F32)], axis=1
+            [last[8 + k : 9 + k, 64:] for k in range(3)] + [jnp.zeros((1, 64), F32)], axis=1
         )
-    stacked[:, pl.ds(192, 64)] = jnp.zeros((FEAT * 80, 64), BF16)
-    first = contract(stacked[...], held[...], 0, 0)[:OWN]
-    second = contract(stacked[...], other[...], 0, 0)[:OWN]
+    rank = contract(marks[...].astype(BF16), earlier(SLAB), 1, 0)
+    for pair in range(FEAT // 2):
+        hits = []
+        for source in (2 * pair, 2 * pair + 1):
+            hit = (iota((UNION, SLAB), 0).astype(F32) == rank[source : source + 1]) & (
+                marks[pl.ds(source, 1), :] > 0.0
+            )
+            hits.append(jnp.where(hit, 1.0, 0.0))
+        chosen[pl.ds(pair * 2 * UNION, 2 * UNION), :] = jnp.concatenate(hits, axis=0).astype(BF16)
+
+
+def hidden_kernel(spot, own, means, mine, theirs, bias, chosen, hidden, rows, stacked):
+    for source in range(FEAT):
+        tiles = [unfolded(own[source].astype(F32)[80:]), unfolded(means[source].astype(F32))]
+        stacked[pl.ds(source * 80, 80), :] = jnp.concatenate(tiles, axis=0).astype(BF16)
+    first = contract(stacked[...], mine[...], 0, 0)[:OWN]
+    second = contract(stacked[...], theirs[...], 0, 0)[:OWN]
     even = spot[0] == 0
     pre = jnp.concatenate(
         [jnp.where(even, first, second), jnp.where(even, second, first)], axis=1
@@ -294,17 +287,13 @@
     pre = jnp.where(spot[1] == 0, pre, jnp.concatenate([pre[128:], pre[:128]], axis=0))
     result = jnp.maximum(pre + bias[...], 0.0).astype(BF16)
     hidden[...] = result
-    rank = contract(marks[...].astype(BF16), earlier(SLAB), 1, 0)
-    for source in range(FEAT):
-        hit = (iota((UNION, SLAB), 0).astype(F32) == rank[source : source + 1]) & (
-            marks[pl.ds(source, 1), :] > 0.0
-        )
-        chosen[pl.ds(source * UNION, UNION), :] = jnp.where(hit, 1.0, 0.0)
     padded = jnp.concatenate([result, jnp.zeros((SLAB - OWN, HIDDEN), BF16)], axis=0)
-    rows[...] = contract(chosen[...].astype(BF16), padded, 1, 0).astype(BF16)
-
-
-def pick_kernel(place, mask, labels, picks):
+    rows[...] = contract(chosen[...], padded, 1, 0).astype(BF16)
+
+
+def pick_kernel(place, mask, labels, block, picks, held, arrived):
+    copy = pltpu.make_async_copy(block, held, arrived)
+    copy.start()
     spots = iota((NAMED, TARGETS), 0)
     total = jnp.zeros((NAMED, TARGETS), F32)
     for slot in range(FAN):
@@ -318,6 +307,7 @@
     blank = jnp.zeros((16, TARGETS), F32)
     picks[0] = jnp.concatenate([total, parts.astype(F32)], axis=0).astype(BF16)
     picks[1] = jnp.concatenate([own, blank], axis=0).astype(BF16)
+    copy.wait()
 
 
 def loss_kernel(spot, *refs):
@@ -406,32 +396,32 @@
     return pl.pallas_call(
         gather_kernel,
         out_shape=jax.ShapeDtypeStruct((FEAT, 64, 128), BF16),
-        in_specs=[pl.BlockSpec(memory_space=pl.ANY), VMEM, HBM],
-        out_specs=HBM,
+        in_specs=[pl.BlockSpec(memory_space=pl.ANY), VMEM, VMEM],
+        out_specs=VMEM,
         scratch_shapes=[
             pltpu.VMEM((INPUTS + 8, 128), F32),
             pltpu.VMEM((ROWS, 128), F32),
             pltpu.SMEM(((FAN + 1) * ROWS,), jnp.int32),
-            pltpu.VMEM((FEAT, 64, 128), BF16),
-            pltpu.VMEM((WIDTH, INPUTS), BF16),
             pltpu.SemaphoreType.DMA((ROWS // CHUNK,)),
-            pltpu.SemaphoreType.DMA((INPUTS // 3 // 128 // TABLE_STEP, 3)),
-            pltpu.SemaphoreType.DMA((FEAT // 8,)),
         ],
-        compiler_params=pltpu.CompilerParams(vmem_limit_bytes=MOST),
+        compiler_params=pltpu.CompilerParams(vmem_limit_bytes=24 * 2**20),
         cost_estimate=pl.CostEstimate(flops=0, bytes_accessed=0, transcendentals=0),
     )(slots, ranks, table)
 
 
-def call_pick(place, mask, labels):
+def call_pick(place, mask, labels, block):
     return pl.pallas_call(
         pick_kernel,
-        out_shape=jax.ShapeDtypeStruct((2, NAMED + 16, TARGETS), BF16),
-        in_specs=[VMEM] * 3,
-        out_specs=VMEM,
+        out_shape=(
+            jax.ShapeDtypeStruct((2, NAMED + 16, TARGETS), BF16),
+            jax.ShapeDtypeStruct(block.shape, BF16),
+        ),
+        in_specs=[VMEM] * 3 + [HBM],
+        out_specs=(VMEM, VMEM),
+        scratch_shapes=[pltpu.SemaphoreType.DMA],
         compiler_params=pltpu.CompilerParams(vmem_limit_bytes=16 * 2**20),
-        cost_estimate=pl.CostEstimate(flops=10**7, bytes_accessed=4 * 10**6, transcendentals=0),
-    )(place, mask, labels)
+        cost_estimate=pl.CostEstimate(flops=10**7, bytes_accessed=6 * 10**6, transcendentals=0),
+    )(place, mask, labels, block)
 
 
 def call_loss(spot, rows, picks, rows_there, picks_there, blocks):
@@ -498,28 +488,33 @@
     )
     own = lax.all_to_all(own, "feat", 0, 0)
     send = call_gather(slots.reshape(-1), ranks, table)
-    theirs = lax.ppermute(own[:, : 2 * WIDTH], "node", swap)
+    send, own = lax.optimization_barrier((send, own))
+    mine = own[:, : 2 * WIDTH].reshape(FEAT * 2 * WIDTH, 128)
+    theirs = lax.ppermute(mine, "node", swap)
     means = lax.all_to_all(send, "feat", 0, 0)
     means, *blocks[2:] = lax.optimization_barrier((means, *blocks[2:]))
     side = jnp.stack([core, lax.axis_index("feat").astype(jnp.int32) & 1])
+    chosen = pl.pallas_call(
+        choose_kernel,
+        out_shape=jax.ShapeDtypeStruct((NAMED, SLAB), BF16),
+        in_specs=[VMEM],
+        out_specs=VMEM,
+        scratch_shapes=[pltpu.VMEM((FEAT, SLAB), F32)],
+        compiler_params=pltpu.CompilerParams(vmem_limit_bytes=16 * 2**20),
+        cost_estimate=pl.CostEstimate(flops=10**7, bytes_accessed=2 * 10**6, transcendentals=0),
+    )(own)
     hidden, rows = pl.pallas_call(
         hidden_kernel,
         out_shape=(
             jax.ShapeDtypeStruct((OWN, HIDDEN), BF16),
-            jax.ShapeDtypeStruct((FEAT * UNION, HIDDEN), BF16),
+            jax.ShapeDtypeStruct((NAMED, HIDDEN), BF16),
         ),
-        in_specs=[SMEM] + [VMEM] * 4,
+        in_specs=[SMEM] + [VMEM] * 6,
         out_specs=(VMEM, VMEM),
-        scratch_shapes=[
-            pltpu.VMEM((FEAT * 80, 256), BF16),
-            pltpu.VMEM((FEAT * 80, 128), BF16),
-            pltpu.VMEM((FEAT * 80, 128), BF16),
-            pltpu.VMEM((FEAT, SLAB), F32),
-            pltpu.VMEM((FEAT * UNION, SLAB), F32),
-        ],
+        scratch_shapes=[pltpu.VMEM((FEAT * 80, 256), BF16)],
         compiler_params=pltpu.CompilerParams(vmem_limit_bytes=24 * 2**20),
-    )(side, own, theirs, means, first_bias[None, :])
-    picks = call_pick(place, second_mask, labels)
+    )(side, own, means, mine, theirs, first_bias[None, :], chosen)
+    picks, blocks[0] = call_pick(place, second_mask, labels, class_weight)
     picks_there = lax.ppermute(picks, "node", swap)
     rows = lax.all_to_all(rows.reshape(FEAT, UNION, HIDDEN), "feat", 0, 0)
     rows = rows.reshape(FEAT * UNION, HIDDEN)

time: 110 us -> 108 us (0.982)
  Pallas kernels: 45.3 us -> 42 us
  local copies, waits for them, and re-layouts: 0.92 us -> 2.94 us
    unnamed x10 -> x20, local copies, waits for them, and re-layouts: 0.03 us -> 2.9 us
    pallas_call x1, Pallas kernels: 31.4 us -> 28.8 us  [call_gather(): pl.pallas_call(gather_kernel, out_shape=jax.ShapeDtypeStruct((FEAT, 64, 1...]
  transfers between devices with their start and end apart: 10 -> 10, of which waited for: 4 -> 4; matrix products, arithmetic and copies ran while one was open for 1% -> 0% of each run, Pallas kernels for 32% -> 30%
where the time goes in v8:
time: 108 us
  Pallas kernels  42 us (39%)
  starting transfers between devices  41.3 us (38%)
  waiting for transfers between devices  20.5 us (19%)
  local copies, waits for them, and re-layouts  2.94 us (3%)
    pallas_call x1, Pallas kernels, call_gather(): pl.pallas_call(gather_kernel, out_shape=jax.ShapeDtypeStruct((FEAT, 64, 1...  28.8 us
    all_to_all x1, starting transfers between devices, body(): own = lax.all_to_all(own, 'feat', 0, 0)  12.2 us
    all_to_all x1, waiting for transfers between devices, body(): means = lax.all_to_all(send, 'feat', 0, 0)  10.8 us
    all_to_all x1, starting transfers between devices, body(): means = lax.all_to_all(send, 'feat', 0, 0)  9.21 us
    all_to_all x1, waiting for transfers between devices, body(): rows = lax.all_to_all(rows.reshape(FEAT, UNION, HIDDEN), 'feat', 0, 0)  7.56 us
    all_to_all x1, starting transfers between devices, body(): rows = lax.all_to_all(rows.reshape(FEAT, UNION, HIDDEN), 'feat', 0, 0)  6.25 us
    pallas_call x1, Pallas kernels, call_prepare(): pl.pallas_call(prepare_kernel, out_shape=(jax.ShapeDtypeStruct((FEAT, 144...  5.06 us
    pallas_call x1, Pallas kernels, call_loss(): pl.pallas_call(loss_kernel, out_shape=[jax.ShapeDtypeStruct((8, TARGETS),...  4.53 us
  transfers between devices with their start and end apart: 10, of which 4 were waited for; matrix products, arithmetic and copies ran while one was open for 0% of the time, Pallas kernels for 30%

profile of v8, /device:TPU:1, one launch (start us, length us, event | category | flops | bytes accessed | tf_op | source)
XLA Modules:
  0.0 107.7 jit_solution(3415965164713046581)
XLA Ops:
  0.6 5.1 %shard_map.113 = (bf16[32,144,128]{2,1,0:T(8,128)(2,1)}, s32[16,128]{1,0:T(8,128)}, s32[528,128]{1,0:T(8,128)}, s32[48,128]{1,0:T(8,128)}) custom-call(s32[1]{0:T(128)} %bitcast.core, s32[10,1,128]{2,1,0:T(1,128)} %refs_0_.1, s32[1,128]{1,0:T(1,128)} %refs_1_.1, bf16[2,40,256]{2,1,0:T(8,128)(2,1)} %refs_2_.1, bf16[40,24576]{1,0:T(8,128)(2,1)} %bitcast.12, ...), custom_call_target="tpu_custom_call" | custom-call | flops 100000000 | bytes 10000000 | tf_op jit(solution)/shard_map/pallas_call | solution.py:373
  5.7 0.0 copy-start
  5.7 0.0 copy-start.5
  5.7 12.2 %all-to-all-start = ((bf16[32,144,128]{2,1,0:T(8,128)(2,1)}), bf16[32,144,128]{2,1,0:T(8,128)(2,1)S(1)}, u32[]{:S(2)}, u32[]{:S(2)}) async-start(bf16[32,144,128]{2,1,0:T(8,128)(2,1)} %get-tuple-element.19), calls=%async_computation | async-start | bytes 2359296 | tf_op jit(solution)/shard_map/all_to_all | solution.py:489
  17.9 1.3 %collective-permute-start = (bf16[512,1280]{1,0:T(8,128)(2,1)}, bf16[512,1280]{1,0:T(8,128)(2,1)}, u32[]{:S(2)}, u32[]{:S(2)}) collective-permute-start(bf16[512,1280]{1,0:T(8,128)(2,1)} %block.1), channel_id=1, source_target_pairs={{0,2},{1,3},{2,4},{3,5},{4,6},{5,7},{6,0},{7,1},{8,10},{9,11},{10,... | collective-permute-start | bytes 3932168 | tf_op jit(solution)/shard_map/ppermute | solution.py:477
  19.2 1.5 %collective-permute-start.1 = (bf16[512,1280]{1,0:T(8,128)(2,1)}, bf16[512,1280]{1,0:T(8,128)(2,1)}, u32[]{:S(2)}, u32[]{:S(2)}) collective-permute-start(bf16[512,1280]{1,0:T(8,128)(2,1)} %block.1), channel_id=1, source_target_pairs={{0,6},{1,7},{2,0},{3,1},{4,2},{5,3},{6,4},{7,5},{8,14},{9,15},{10,... | collective-permute-start | bytes 3932168 | tf_op jit(solution)/shard_map/ppermute | solution.py:477
  20.7 28.8 %shard_map.114 = bf16[32,64,128]{2,1,0:T(8,128)(2,1)S(1)} custom-call(s32[67584]{0:T(1024)S(1)} %bitcast.19, s32[48,128]{1,0:T(8,128)S(1)} %copy-done.5, bf16[40,24576]{1,0:T(8,128)(2,1)S(1)} %bitcast.13), custom_call_target="tpu_custom_call" | custom-call | tf_op jit(solution)/shard_map/pallas_call | solution.py:396
  49.5 0.8 copy-done.1
  50.3 9.2 %all-to-all-start.1 = ((bf16[32,64,128]{2,1,0:T(8,128)(2,1)}), bf16[32,64,128]{2,1,0:T(8,128)(2,1)S(1)}, u32[]{:S(2)}, u32[]{:S(2)}) async-start(bf16[32,64,128]{2,1,0:T(8,128)(2,1)} %copy-done.1), calls=%async_computation.1 | async-start | bytes 1048576 | tf_op jit(solution)/shard_map/all_to_all | solution.py:494
  59.5 0.0 copy-start.8
  59.6 2.1 %collective-permute-start.2 = (bf16[2560,128]{1,0:T(8,128)(2,1)S(1)}, bf16[2560,128]{1,0:T(8,128)(2,1)S(1)}, u32[]{:S(2)}, u32[]{:S(2)}) collective-permute-start(bf16[2560,128]{1,0:T(8,128)(2,1)S(1)} %bitcast.14), channel_id=1, source_target_pairs={{0,1},{1,0},{2,3},{3,2},{4,5},{5,4},{6,7},{7,6},{8,9},{9,8},{10,11... | collective-permute-start | bytes 1966088 | tf_op jit(solution)/shard_map/ppermute | solution.py:493
  61.7 1.5 %collective-permute-start.5 = (bf16[512,1280]{1,0:T(8,128)(2,1)}, bf16[512,1280]{1,0:T(8,128)(2,1)}, u32[]{:S(2)}, u32[]{:S(2)}) collective-permute-start(bf16[512,1280]{1,0:T(8,128)(2,1)} %block.1), channel_id=1, source_target_pairs={{0,4},{1,5},{2,6},{3,7},{4,0},{5,1},{6,2},{7,3},{8,12},{9,13},{10,... | collective-permute-start | bytes 3932168 | tf_op jit(solution)/shard_map/ppermute | solution.py:477
  63.3 0.1 pad_add_fusion.spot
  63.3 0.3 shard_map.115.chosen
  63.6 0.0 collective-permute-done.refs_6_
  63.7 10.8 %all-to-all-done.1.means = bf16[32,64,128]{2,1,0:T(8,128)(2,1)S(1)} async-done(((bf16[32,64,128]{2,1,0:T(8,128)(2,1)}), bf16[32,64,128]{2,1,0:T(8,128)(2,1)S(1)}, u32[]{:S(2)}, u32[]{:S(2)}) %all-to-all-start.1) | async-done | bytes 524320 | tf_op jit(solution)/shard_map/all_to_all | solution.py:494
  74.4 0.0 copy-start.7
  74.4 0.0 copy-start.9
  74.5 2.3 %shard_map.116 = (bf16[192,256]{1,0:T(8,128)(2,1)}, bf16[768,256]{1,0:T(8,128)(2,1)S(1)}) custom-call(s32[2]{0:T(128)S(1)} %pad_add_fusion.spot, bf16[32,144,128]{2,1,0:T(8,128)(2,1)S(1)} %all-to-all-done.own, bf16[32,64,128]{2,1,0:T(8,128)(2,1)S(1)} %all-to-all-done.1.means, bf16[2560,128]{1,0:T(8,128)(2,1)S(1)} %bitcast.15, ...), custom_call_target="tpu_custom_call" | custom-call | tf_op jit(solution)/shard_map/pallas_call | solution.py:506
  76.7 0.7 copy-done.3
  77.5 6.2 %all-to-all-start.2 = ((bf16[32,24,256]{2,1,0:T(8,128)(2,1)}), bf16[32,24,256]{2,1,0:T(8,128)(2,1)S(1)}, u32[]{:S(2)}, u32[]{:S(2)}) async-start(bf16[32,24,256]{2,1,0:T(8,128)(2,1)} %bitcast.18), calls=%async_computation.2 | async-start | bytes 786432 | tf_op jit(solution)/shard_map/all_to_all | solution.py:519
  83.8 0.0 copy-start.2
  83.8 1.3 %copy-done.2 = bf16[512,1280]{1,0:T(8,128)(2,1)S(1)} copy-done((bf16[512,1280]{1,0:T(8,128)(2,1)S(1)}, bf16[512,1280]{1,0:T(8,128)(2,1)}, u32[]{:S(2)}) %copy-start.2) | copy-done | bytes 1310744
  85.1 0.5 shard_map.117
  85.6 2.5 %collective-permute-start.4 = (bf16[2,784,128]{2,1,0:T(8,128)(2,1)S(1)}, bf16[2,784,128]{2,1,0:T(8,128)(2,1)S(1)}, u32[]{:S(2)}, u32[]{:S(2)}) collective-permute-start(bf16[2,784,128]{2,1,0:T(8,128)(2,1)S(1)} %get-tuple-element.26.refs_1_), channel_id=1, source_target_pairs={{0,1},{1,0},{2,3},{3,2},{4,5},{5,4},{6,7},{7,6},{8,9},{9,8},{10,11... | collective-permute-start | bytes 1204232 | tf_op jit(solution)/shard_map/ppermute | solution.py:518
  88.1 7.6 %all-to-all-done.2 = bf16[32,24,256]{2,1,0:T(8,128)(2,1)S(1)} async-done(((bf16[32,24,256]{2,1,0:T(8,128)(2,1)}), bf16[32,24,256]{2,1,0:T(8,128)(2,1)S(1)}, u32[]{:S(2)}, u32[]{:S(2)}) %all-to-all-start.2) | async-done | bytes 393248 | tf_op jit(solution)/shard_map/all_to_all | solution.py:519
  95.7 4.3 %collective-permute-start.3 = (bf16[768,256]{1,0:T(8,128)(2,1)S(1)}, bf16[768,256]{1,0:T(8,128)(2,1)S(1)}, u32[]{:S(2)}, u32[]{:S(2)}) collective-permute-start(bf16[768,256]{1,0:T(8,128)(2,1)S(1)} %bitcast.16), channel_id=1, source_target_pairs={{0,1},{1,0},{2,3},{3,2},{4,5},{5,4},{6,7},{7,6},{8,9},{9,8},{10,11... | collective-permute-start | bytes 1179656 | tf_op jit(solution)/shard_map/ppermute | solution.py:521
  100.0 1.3 %collective-permute-done.3.refs_2_ = bf16[768,256]{1,0:T(8,128)(2,1)S(1)} collective-permute-done((bf16[768,256]{1,0:T(8,128)(2,1)S(1)}, bf16[768,256]{1,0:T(8,128)(2,1)S(1)}, u32[]{:S(2)}, u32[]{:S(2)}) %collective-permute-start.3) | collective-permute-done | bytes 393248 | tf_op jit(solution)/shard_map/ppermute | solution.py:521
  101.3 4.5 %shard_map.118 = (f32[8,128]{1,0:T(8,128)S(1)}, f32[8,128]{1,0:T(8,128)S(1)}) custom-call(s32[1]{0:T(128)} %bitcast.9.spot, bf16[768,256]{1,0:T(8,128)(2,1)S(1)} %bitcast.17, bf16[2,784,128]{2,1,0:T(8,128)(2,1)S(1)} %get-tuple-element.26.refs_1_, bf16[768,256]{1,0:T(8,128)(2,1)S(1)} %collective-permute-done.3.refs_2_, ...), custom_call_target="tpu_custom_call" | custom-call | tf_op jit(solution)/shard_map/pallas_call | solution.py:429
  105.9 0.4 collective-permute-start.6
  106.3 0.8 collective-permute-done.6.there
  107.1 0.5 shard_map.119
  (17 shorter events, 0.1 us)
Async XLA Ops:
  5.7 15.0 %copy-start = (bf16[40,1,24576]{2,0,1:T(8,128)(2,1)S(1)}, bf16[40,1,24576]{2,0,1:T(8,128)(2,1)}, u32[]{:S(2)}) copy-start(bf16[40,1,24576]{2,0,1:T(8,128)(2,1)} %param.10) | copy-start | bytes 5898244
  5.7 15.0 %copy-start.4 = (s32[528,128]{1,0:T(8,128)S(1)}, s32[528,128]{1,0:T(8,128)}, u32[]{:S(2)}) copy-start(s32[528,128]{1,0:T(8,128)} %get-tuple-element.17) | copy-start | bytes 811012
  5.7 15.0 %copy-start.5 = (s32[48,128]{1,0:T(8,128)S(1)}, s32[48,128]{1,0:T(8,128)}, u32[]{:S(2)}) copy-start(s32[48,128]{1,0:T(8,128)} %get-tuple-element.18.ranks) | copy-start | bytes 73732
  5.7 44.5 %all-to-all-start = ((bf16[32,144,128]{2,1,0:T(8,128)(2,1)}), bf16[32,144,128]{2,1,0:T(8,128)(2,1)S(1)}, u32[]{:S(2)}, u32[]{:S(2)}) async-start(bf16[32,144,128]{2,1,0:T(8,128)(2,1)} %get-tuple-element.19), calls=%async_computation | async-start | bytes 2359296 | tf_op jit(solution)/shard_map/all_to_all | solution.py:489
  17.9 45.7 %collective-permute-start = (bf16[512,1280]{1,0:T(8,128)(2,1)}, bf16[512,1280]{1,0:T(8,128)(2,1)}, u32[]{:S(2)}, u32[]{:S(2)}) collective-permute-start(bf16[512,1280]{1,0:T(8,128)(2,1)} %block.1), channel_id=1, source_target_pairs={{0,2},{1,3},{2,4},{3,5},{4,6},{5,7},{6,0},{7,1},{8,10},{9,11},{10,... | collective-permute-start | bytes 3932168 | tf_op jit(solution)/shard_map/ppermute | solution.py:477
  19.2 44.4 %collective-permute-start.1 = (bf16[512,1280]{1,0:T(8,128)(2,1)}, bf16[512,1280]{1,0:T(8,128)(2,1)}, u32[]{:S(2)}, u32[]{:S(2)}) collective-permute-start(bf16[512,1280]{1,0:T(8,128)(2,1)} %block.1), channel_id=1, source_target_pairs={{0,6},{1,7},{2,0},{3,1},{4,2},{5,3},{6,4},{7,5},{8,14},{9,15},{10,... | collective-permute-start | bytes 3932168 | tf_op jit(solution)/shard_map/ppermute | solution.py:477
  49.5 0.8 copy-start.1
  50.3 24.1 %all-to-all-start.1 = ((bf16[32,64,128]{2,1,0:T(8,128)(2,1)}), bf16[32,64,128]{2,1,0:T(8,128)(2,1)S(1)}, u32[]{:S(2)}, u32[]{:S(2)}) async-start(bf16[32,64,128]{2,1,0:T(8,128)(2,1)} %copy-done.1), calls=%async_computation.1 | async-start | bytes 1048576 | tf_op jit(solution)/shard_map/all_to_all | solution.py:494
  59.5 14.9 %copy-start.8 = (f32[256]{0:T(256)S(1)}, f32[256]{0:T(256)}, u32[]{:S(2)}) copy-start(f32[256]{0:T(256)} %param.18) | copy-start | bytes 3076
  59.6 14.9 %collective-permute-start.2 = (bf16[2560,128]{1,0:T(8,128)(2,1)S(1)}, bf16[2560,128]{1,0:T(8,128)(2,1)S(1)}, u32[]{:S(2)}, u32[]{:S(2)}) collective-permute-start(bf16[2560,128]{1,0:T(8,128)(2,1)S(1)} %bitcast.14), channel_id=1, source_target_pairs={{0,1},{1,0},{2,3},{3,2},{4,5},{5,4},{6,7},{7,6},{8,9},{9,8},{10,11... | collective-permute-start | bytes 1966088 | tf_op jit(solution)/shard_map/ppermute | solution.py:493
  61.7 38.3 %collective-permute-start.5 = (bf16[512,1280]{1,0:T(8,128)(2,1)}, bf16[512,1280]{1,0:T(8,128)(2,1)}, u32[]{:S(2)}, u32[]{:S(2)}) collective-permute-start(bf16[512,1280]{1,0:T(8,128)(2,1)} %block.1), channel_id=1, source_target_pairs={{0,4},{1,5},{2,6},{3,7},{4,0},{5,1},{6,2},{7,3},{8,12},{9,13},{10,... | collective-permute-start | bytes 3932168 | tf_op jit(solution)/shard_map/ppermute | solution.py:477
  74.4 9.3 %copy-start.6 = (s32[16,128]{1,0:T(8,128)S(1)}, s32[16,128]{1,0:T(8,128)}, u32[]{:S(2)}) copy-start(s32[16,128]{1,0:T(8,128)} %get-tuple-element.25.place) | copy-start | bytes 24580
  74.4 9.3 %copy-start.7 = (s32[10,1,128]{2,1,0:T(1,128)S(1)}, s32[10,1,128]{2,1,0:T(1,128)}, u32[]{:S(2)}) copy-start(s32[10,1,128]{2,1,0:T(1,128)} %mask.1) | copy-start | bytes 15364
  74.4 9.3 %copy-start.9 = (s32[1,128]{1,0:T(1,128)S(1)}, s32[1,128]{1,0:T(1,128)}, u32[]{:S(2)}) copy-start(s32[1,128]{1,0:T(1,128)} %labels.1) | copy-start | bytes 1540
  76.7 0.7 copy-start.3
  77.5 18.2 %all-to-all-start.2 = ((bf16[32,24,256]{2,1,0:T(8,128)(2,1)}), bf16[32,24,256]{2,1,0:T(8,128)(2,1)S(1)}, u32[]{:S(2)}, u32[]{:S(2)}) async-start(bf16[32,24,256]{2,1,0:T(8,128)(2,1)} %bitcast.18), calls=%async_computation.2 | async-start | bytes 786432 | tf_op jit(solution)/shard_map/all_to_all | solution.py:519
  83.8 1.3 %copy-start.2 = (bf16[512,1280]{1,0:T(8,128)(2,1)S(1)}, bf16[512,1280]{1,0:T(8,128)(2,1)}, u32[]{:S(2)}) copy-start(bf16[512,1280]{1,0:T(8,128)(2,1)} %block.1) | copy-start | bytes 3932164
  85.6 14.4 %collective-permute-start.4 = (bf16[2,784,128]{2,1,0:T(8,128)(2,1)S(1)}, bf16[2,784,128]{2,1,0:T(8,128)(2,1)S(1)}, u32[]{:S(2)}, u32[]{:S(2)}) collective-permute-start(bf16[2,784,128]{2,1,0:T(8,128)(2,1)S(1)} %get-tuple-element.26.refs_1_), channel_id=1, source_target_pairs={{0,1},{1,0},{2,3},{3,2},{4,5},{5,4},{6,7},{7,6},{8,9},{9,8},{10,11... | collective-permute-start | bytes 1204232 | tf_op jit(solution)/shard_map/ppermute | solution.py:518
  95.7 5.7 %collective-permute-start.3 = (bf16[768,256]{1,0:T(8,128)(2,1)S(1)}, bf16[768,256]{1,0:T(8,128)(2,1)S(1)}, u32[]{:S(2)}, u32[]{:S(2)}) collective-permute-start(bf16[768,256]{1,0:T(8,128)(2,1)S(1)} %bitcast.16), channel_id=1, source_target_pairs={{0,1},{1,0},{2,3},{3,2},{4,5},{5,4},{6,7},{7,6},{8,9},{9,8},{10,11... | collective-permute-start | bytes 1179656 | tf_op jit(solution)/shard_map/ppermute | solution.py:521
  105.9 1.3 %collective-permute-start.6 = (f32[8,128]{1,0:T(8,128)S(1)}, f32[8,128]{1,0:T(8,128)S(1)}, u32[]{:S(2)}, u32[]{:S(2)}) collective-permute-start(f32[8,128]{1,0:T(8,128)S(1)} %get-tuple-element.31), channel_id=1, source_target_pairs={{0,1},{1,0},{2,3},{3,2},{4,5},{5,4},{6,7},{7,6},{8,9},{9,8},{10,11... | collective-permute-start | bytes 12296 | tf_op jit(solution)/shard_map/ppermute | solution.py:523

commit v9 on v8

--- a/solution.py
+++ b/solution.py
@@ -291,9 +291,13 @@
     rows[...] = contract(chosen[...], padded, 1, 0).astype(BF16)
 
 
-def pick_kernel(place, mask, labels, block, picks, held, arrived):
-    copy = pltpu.make_async_copy(block, held, arrived)
-    copy.start()
+def pick_kernel(place, mask, labels, near, far, picks, held, held_far, arrived):
+    copies = [
+        pltpu.make_async_copy(near, held, arrived.at[0]),
+        pltpu.make_async_copy(far, held_far, arrived.at[1]),
+    ]
+    for copy in copies:
+        copy.start()
     spots = iota((NAMED, TARGETS), 0)
     total = jnp.zeros((NAMED, TARGETS), F32)
     for slot in range(FAN):
@@ -307,7 +311,8 @@
     blank = jnp.zeros((16, TARGETS), F32)
     picks[0] = jnp.concatenate([total, parts.astype(F32)], axis=0).astype(BF16)
     picks[1] = jnp.concatenate([own, blank], axis=0).astype(BF16)
-    copy.wait()
+    for copy in copies:
+        copy.wait()
 
 
 def loss_kernel(spot, *refs):
@@ -409,19 +414,20 @@
     )(slots, ranks, table)
 
 
-def call_pick(place, mask, labels, block):
+def call_pick(place, mask, labels, near, far):
     return pl.pallas_call(
         pick_kernel,
         out_shape=(
             jax.ShapeDtypeStruct((2, NAMED + 16, TARGETS), BF16),
-            jax.ShapeDtypeStruct(block.shape, BF16),
+            jax.ShapeDtypeStruct(near.shape, BF16),
+            jax.ShapeDtypeStruct(far.shape, BF16),
         ),
-        in_specs=[VMEM] * 3 + [HBM],
-        out_specs=(VMEM, VMEM),
-        scratch_shapes=[pltpu.SemaphoreType.DMA],
+        in_specs=[VMEM] * 3 + [HBM] * 2,
+        out_specs=(VMEM,) * 3,
+        scratch_shapes=[pltpu.SemaphoreType.DMA((2,))],
         compiler_params=pltpu.CompilerParams(vmem_limit_bytes=16 * 2**20),
         cost_estimate=pl.CostEstimate(flops=10**7, bytes_accessed=6 * 10**6, transcendentals=0),
-    )(place, mask, labels, block)
+    )(place, mask, labels, near, far)
 
 
 def call_loss(spot, rows, picks, rows_there, picks_there, blocks):
@@ -492,7 +498,7 @@
     mine = own[:, : 2 * WIDTH].reshape(FEAT * 2 * WIDTH, 128)
     theirs = lax.ppermute(mine, "node", swap)
     means = lax.all_to_all(send, "feat", 0, 0)
-    means, *blocks[2:] = lax.optimization_barrier((means, *blocks[2:]))
+    means, blocks[1] = lax.optimization_barrier((means, blocks[1]))
     side = jnp.stack([core, lax.axis_index("feat").astype(jnp.int32) & 1])
     chosen = pl.pallas_call(
         choose_kernel,
@@ -514,7 +520,7 @@
         scratch_shapes=[pltpu.VMEM((FEAT * 80, 256), BF16)],
         compiler_params=pltpu.CompilerParams(vmem_limit_bytes=24 * 2**20),
     )(side, own, means, mine, theirs, first_bias[None, :], chosen)
-    picks, blocks[0] = call_pick(place, second_mask, labels, class_weight)
+    picks, *blocks[:2] = call_pick(place, second_mask, labels, *blocks[:2])
     picks_there = lax.ppermute(picks, "node", swap)
     rows = lax.all_to_all(rows.reshape(FEAT, UNION, HIDDEN), "feat", 0, 0)
     rows = rows.reshape(FEAT * UNION, HIDDEN)

time: 108 us -> 108 us (level)
    ppermute x3, starting transfers between devices: 4.3 us -> 5.52 us  [body(): blocks.append(lax.ppermute(class_weight, 'node', around))]
where the time goes in v9:
time: 108 us
  Pallas kernels  42.7 us (40%)
  starting transfers between devices  41.1 us (38%)
  waiting for transfers between devices  20.1 us (19%)
  local copies, waits for them, and re-layouts  2.94 us (3%)
    pallas_call x1, Pallas kernels, call_gather(): pl.pallas_call(gather_kernel, out_shape=jax.ShapeDtypeStruct((FEAT, 64, 1...  28.8 us
    all_to_all x1, starting transfers between devices, body(): own = lax.all_to_all(own, 'feat', 0, 0)  12.2 us
    all_to_all x1, waiting for transfers between devices, body(): means = lax.all_to_all(send, 'feat', 0, 0)  10 us
    all_to_all x1, starting transfers between devices, body(): means = lax.all_to_all(send, 'feat', 0, 0)  9.22 us
    all_to_all x1, waiting for transfers between devices, body(): rows = lax.all_to_all(rows.reshape(FEAT, UNION, HIDDEN), 'feat', 0, 0)  7.94 us
    all_to_all x1, starting transfers between devices, body(): rows = lax.all_to_all(rows.reshape(FEAT, UNION, HIDDEN), 'feat', 0, 0)  6.35 us
    ppermute x3, starting transfers between devices, body(): blocks.append(lax.ppermute(class_weight, 'node', around))  5.52 us
    pallas_call x1, Pallas kernels, call_prepare(): pl.pallas_call(prepare_kernel, out_shape=(jax.ShapeDtypeStruct((FEAT, 144...  5.1 us
  transfers between devices with their start and end apart: 10, of which 4 were waited for; matrix products, arithmetic and copies ran while one was open for 0% of the time, Pallas kernels for 30%

profile of v9, /device:TPU:1, one launch (start us, length us, event | category | flops | bytes accessed | tf_op | source)
XLA Modules:
  0.0 107.8 jit_solution(7507321751805258037)
XLA Ops:
  0.6 5.1 %shard_map.113 = (bf16[32,144,128]{2,1,0:T(8,128)(2,1)}, s32[16,128]{1,0:T(8,128)}, s32[528,128]{1,0:T(8,128)}, s32[48,128]{1,0:T(8,128)}) custom-call(s32[1]{0:T(128)} %bitcast.core, s32[10,1,128]{2,1,0:T(1,128)} %refs_0_.1, s32[1,128]{1,0:T(1,128)} %refs_1_.1, bf16[2,40,256]{2,1,0:T(8,128)(2,1)} %refs_2_.1, bf16[40,24576]{1,0:T(8,128)(2,1)} %bitcast.12, ...), custom_call_target="tpu_custom_call" | custom-call | flops 100000000 | bytes 10000000 | tf_op jit(solution)/shard_map/pallas_call | solution.py:378
  5.7 0.0 copy-start
  5.8 0.0 copy-start.5
  5.8 12.2 %all-to-all-start = ((bf16[32,144,128]{2,1,0:T(8,128)(2,1)}), bf16[32,144,128]{2,1,0:T(8,128)(2,1)S(1)}, u32[]{:S(2)}, u32[]{:S(2)}) async-start(bf16[32,144,128]{2,1,0:T(8,128)(2,1)} %get-tuple-element.19), calls=%async_computation | async-start | bytes 2359296 | tf_op jit(solution)/shard_map/all_to_all | solution.py:495
  18.0 2.8 %collective-permute-start = (bf16[512,1280]{1,0:T(8,128)(2,1)}, bf16[512,1280]{1,0:T(8,128)(2,1)}, u32[]{:S(2)}, u32[]{:S(2)}) collective-permute-start(bf16[512,1280]{1,0:T(8,128)(2,1)} %near.1), channel_id=1, source_target_pairs={{0,4},{1,5},{2,6},{3,7},{4,0},{5,1},{6,2},{7,3},{8,12},{9,13},{10,... | collective-permute-start | bytes 3932168 | tf_op jit(solution)/shard_map/ppermute | solution.py:483
  20.8 28.8 %shard_map.114 = bf16[32,64,128]{2,1,0:T(8,128)(2,1)S(1)} custom-call(s32[67584]{0:T(1024)S(1)} %bitcast.19, s32[48,128]{1,0:T(8,128)S(1)} %copy-done.5, bf16[40,24576]{1,0:T(8,128)(2,1)S(1)} %bitcast.13), custom_call_target="tpu_custom_call" | custom-call | tf_op jit(solution)/shard_map/pallas_call | solution.py:401
  49.6 0.8 copy-done.1
  50.4 0.0 all-to-all-done.own
  50.4 9.2 %all-to-all-start.1 = ((bf16[32,64,128]{2,1,0:T(8,128)(2,1)}), bf16[32,64,128]{2,1,0:T(8,128)(2,1)S(1)}, u32[]{:S(2)}, u32[]{:S(2)}) async-start(bf16[32,64,128]{2,1,0:T(8,128)(2,1)} %copy-done.1), calls=%async_computation.1 | async-start | bytes 1048576 | tf_op jit(solution)/shard_map/all_to_all | solution.py:500
  59.7 0.0 copy-start.8
  59.7 1.9 %collective-permute-start.1 = (bf16[2560,128]{1,0:T(8,128)(2,1)S(1)}, bf16[2560,128]{1,0:T(8,128)(2,1)S(1)}, u32[]{:S(2)}, u32[]{:S(2)}) collective-permute-start(bf16[2560,128]{1,0:T(8,128)(2,1)S(1)} %bitcast.14), channel_id=1, source_target_pairs={{0,1},{1,0},{2,3},{3,2},{4,5},{5,4},{6,7},{7,6},{8,9},{9,8},{10,11... | collective-permute-start | bytes 1966088 | tf_op jit(solution)/shard_map/ppermute | solution.py:499
  61.6 0.4 collective-permute-start.4
  62.0 2.3 %collective-permute-start.5 = (bf16[512,1280]{1,0:T(8,128)(2,1)}, bf16[512,1280]{1,0:T(8,128)(2,1)}, u32[]{:S(2)}, u32[]{:S(2)}) collective-permute-start(bf16[512,1280]{1,0:T(8,128)(2,1)} %near.1), channel_id=1, source_target_pairs={{0,6},{1,7},{2,0},{3,1},{4,2},{5,3},{6,4},{7,5},{8,14},{9,15},{10,... | collective-permute-start | bytes 3932168 | tf_op jit(solution)/shard_map/ppermute | solution.py:483
  64.3 0.1 pad_add_fusion.spot
  64.4 0.3 shard_map.115.chosen
  64.7 10.0 %all-to-all-done.1.means = bf16[32,64,128]{2,1,0:T(8,128)(2,1)S(1)} async-done(((bf16[32,64,128]{2,1,0:T(8,128)(2,1)}), bf16[32,64,128]{2,1,0:T(8,128)(2,1)S(1)}, u32[]{:S(2)}, u32[]{:S(2)}) %all-to-all-start.1) | async-done | bytes 524320 | tf_op jit(solution)/shard_map/all_to_all | solution.py:500
  74.8 0.0 copy-start.7
  74.8 0.0 copy-start.9
  74.8 2.3 %shard_map.116 = (bf16[192,256]{1,0:T(8,128)(2,1)}, bf16[768,256]{1,0:T(8,128)(2,1)S(1)}) custom-call(s32[2]{0:T(128)S(1)} %pad_add_fusion.spot, bf16[32,144,128]{2,1,0:T(8,128)(2,1)S(1)} %all-to-all-done.own, bf16[32,64,128]{2,1,0:T(8,128)(2,1)S(1)} %all-to-all-done.1.means, bf16[2560,128]{1,0:T(8,128)(2,1)S(1)} %bitcast.15, ...), custom_call_target="tpu_custom_call" | custom-call | tf_op jit(solution)/shard_map/pallas_call | solution.py:512
  77.1 0.7 copy-done.3
  77.8 6.4 %all-to-all-start.2 = ((bf16[32,24,256]{2,1,0:T(8,128)(2,1)}), bf16[32,24,256]{2,1,0:T(8,128)(2,1)S(1)}, u32[]{:S(2)}, u32[]{:S(2)}) async-start(bf16[32,24,256]{2,1,0:T(8,128)(2,1)} %bitcast.18), calls=%async_computation.2 | async-start | bytes 786432 | tf_op jit(solution)/shard_map/all_to_all | solution.py:525
  84.2 0.0 copy-start.2
  84.2 1.3 %copy-done.2 = bf16[512,1280]{1,0:T(8,128)(2,1)S(1)} copy-done((bf16[512,1280]{1,0:T(8,128)(2,1)S(1)}, bf16[512,1280]{1,0:T(8,128)(2,1)}, u32[]{:S(2)}) %copy-start.2) | copy-done | bytes 1310744
  85.5 1.4 %shard_map.117 = (bf16[2,784,128]{2,1,0:T(8,128)(2,1)S(1)}, bf16[512,1280]{1,0:T(8,128)(2,1)S(1)}, bf16[512,1280]{1,0:T(8,128)(2,1)S(1)}) custom-call(s32[16,128]{1,0:T(8,128)S(1)} %copy-done.6, s32[10,1,128]{2,1,0:T(1,128)S(1)} %copy-done.7, s32[1,128]{1,0:T(1,128)S(1)} %copy-done.9, bf16[512,1280]{1,0:T(8,128)(2,1)S(1)} %copy-done.2, ...), custom_call_target="tpu_custom_call" | custom-call | flops 10000000 | bytes 6000000 | tf_op jit(solution)/shard_map/pallas_call | solution.py:418
  87.0 2.2 %collective-permute-start.3 = (bf16[2,784,128]{2,1,0:T(8,128)(2,1)S(1)}, bf16[2,784,128]{2,1,0:T(8,128)(2,1)}, u32[]{:S(2)}, u32[]{:S(2)}) collective-permute-start(bf16[2,784,128]{2,1,0:T(8,128)(2,1)S(1)} %get-tuple-element.27.refs_1_), channel_id=1, source_target_pairs={{0,1},{1,0},{2,3},{3,2},{4,5},{5,4},{6,7},{7,6},{8,9},{9,8},{10,11... | collective-permute-start | bytes 1204232 | tf_op jit(solution)/shard_map/ppermute | solution.py:524
  89.1 7.9 %all-to-all-done.2 = bf16[32,24,256]{2,1,0:T(8,128)(2,1)S(1)} async-done(((bf16[32,24,256]{2,1,0:T(8,128)(2,1)}), bf16[32,24,256]{2,1,0:T(8,128)(2,1)S(1)}, u32[]{:S(2)}, u32[]{:S(2)}) %all-to-all-start.2) | async-done | bytes 393248 | tf_op jit(solution)/shard_map/all_to_all | solution.py:525
  97.1 3.3 %collective-permute-start.2 = (bf16[768,256]{1,0:T(8,128)(2,1)S(1)}, bf16[768,256]{1,0:T(8,128)(2,1)S(1)}, u32[]{:S(2)}, u32[]{:S(2)}) collective-permute-start(bf16[768,256]{1,0:T(8,128)(2,1)S(1)} %bitcast.16), channel_id=1, source_target_pairs={{0,1},{1,0},{2,3},{3,2},{4,5},{5,4},{6,7},{7,6},{8,9},{9,8},{10,11... | collective-permute-start | bytes 1179656 | tf_op jit(solution)/shard_map/ppermute | solution.py:527
  100.4 1.3 %collective-permute-done.2.refs_2_ = bf16[768,256]{1,0:T(8,128)(2,1)S(1)} collective-permute-done((bf16[768,256]{1,0:T(8,128)(2,1)S(1)}, bf16[768,256]{1,0:T(8,128)(2,1)S(1)}, u32[]{:S(2)}, u32[]{:S(2)}) %collective-permute-start.2) | collective-permute-done | bytes 393248 | tf_op jit(solution)/shard_map/ppermute | solution.py:527
  101.7 4.2 %shard_map.118 = (f32[8,128]{1,0:T(8,128)S(1)}, f32[8,128]{1,0:T(8,128)S(1)}) custom-call(s32[1]{0:T(128)} %bitcast.9.spot, bf16[768,256]{1,0:T(8,128)(2,1)S(1)} %bitcast.17, bf16[2,784,128]{2,1,0:T(8,128)(2,1)S(1)} %get-tuple-element.27.refs_1_, bf16[768,256]{1,0:T(8,128)(2,1)S(1)} %collective-permute-done.2.refs_2_, ...), custom_call_target="tpu_custom_call" | custom-call | tf_op jit(solution)/shard_map/pallas_call | solution.py:435
  106.0 0.4 collective-permute-start.6
  106.4 0.8 collective-permute-done.6.there
  107.3 0.5 shard_map.119
  (17 shorter events, 0.1 us)
Async XLA Ops:
  5.7 15.1 %copy-start = (bf16[40,1,24576]{2,0,1:T(8,128)(2,1)S(1)}, bf16[40,1,24576]{2,0,1:T(8,128)(2,1)}, u32[]{:S(2)}) copy-start(bf16[40,1,24576]{2,0,1:T(8,128)(2,1)} %param.10) | copy-start | bytes 5898244
  5.8 15.0 %copy-start.4 = (s32[528,128]{1,0:T(8,128)S(1)}, s32[528,128]{1,0:T(8,128)}, u32[]{:S(2)}) copy-start(s32[528,128]{1,0:T(8,128)} %get-tuple-element.17) | copy-start | bytes 811012
  5.8 15.0 %copy-start.5 = (s32[48,128]{1,0:T(8,128)S(1)}, s32[48,128]{1,0:T(8,128)}, u32[]{:S(2)}) copy-start(s32[48,128]{1,0:T(8,128)} %get-tuple-element.18.ranks) | copy-start | bytes 73732
  5.8 44.6 %all-to-all-start = ((bf16[32,144,128]{2,1,0:T(8,128)(2,1)}), bf16[32,144,128]{2,1,0:T(8,128)(2,1)S(1)}, u32[]{:S(2)}, u32[]{:S(2)}) async-start(bf16[32,144,128]{2,1,0:T(8,128)(2,1)} %get-tuple-element.19), calls=%async_computation | async-start | bytes 2359296 | tf_op jit(solution)/shard_map/all_to_all | solution.py:495
  18.0 46.7 %collective-permute-start = (bf16[512,1280]{1,0:T(8,128)(2,1)}, bf16[512,1280]{1,0:T(8,128)(2,1)}, u32[]{:S(2)}, u32[]{:S(2)}) collective-permute-start(bf16[512,1280]{1,0:T(8,128)(2,1)} %near.1), channel_id=1, source_target_pairs={{0,4},{1,5},{2,6},{3,7},{4,0},{5,1},{6,2},{7,3},{8,12},{9,13},{10,... | collective-permute-start | bytes 3932168 | tf_op jit(solution)/shard_map/ppermute | solution.py:483
  49.6 0.8 copy-start.1
  50.4 24.3 %all-to-all-start.1 = ((bf16[32,64,128]{2,1,0:T(8,128)(2,1)}), bf16[32,64,128]{2,1,0:T(8,128)(2,1)S(1)}, u32[]{:S(2)}, u32[]{:S(2)}) async-start(bf16[32,64,128]{2,1,0:T(8,128)(2,1)} %copy-done.1), calls=%async_computation.1 | async-start | bytes 1048576 | tf_op jit(solution)/shard_map/all_to_all | solution.py:500
  59.7 15.1 %copy-start.8 = (f32[256]{0:T(256)S(1)}, f32[256]{0:T(256)}, u32[]{:S(2)}) copy-start(f32[256]{0:T(256)} %param.18) | copy-start | bytes 3076
  59.7 15.0 %collective-permute-start.1 = (bf16[2560,128]{1,0:T(8,128)(2,1)S(1)}, bf16[2560,128]{1,0:T(8,128)(2,1)S(1)}, u32[]{:S(2)}, u32[]{:S(2)}) collective-permute-start(bf16[2560,128]{1,0:T(8,128)(2,1)S(1)} %bitcast.14), channel_id=1, source_target_pairs={{0,1},{1,0},{2,3},{3,2},{4,5},{5,4},{6,7},{7,6},{8,9},{9,8},{10,11... | collective-permute-start | bytes 1966088 | tf_op jit(solution)/shard_map/ppermute | solution.py:499
  61.6 38.8 %collective-permute-start.4 = (bf16[512,1280]{1,0:T(8,128)(2,1)}, bf16[512,1280]{1,0:T(8,128)(2,1)}, u32[]{:S(2)}, u32[]{:S(2)}) collective-permute-start(bf16[512,1280]{1,0:T(8,128)(2,1)} %near.1), channel_id=1, source_target_pairs={{0,2},{1,3},{2,4},{3,5},{4,6},{5,7},{6,0},{7,1},{8,10},{9,11},{10,... | collective-permute-start | bytes 3932168 | tf_op jit(solution)/shard_map/ppermute | solution.py:483
  62.0 38.4 %collective-permute-start.5 = (bf16[512,1280]{1,0:T(8,128)(2,1)}, bf16[512,1280]{1,0:T(8,128)(2,1)}, u32[]{:S(2)}, u32[]{:S(2)}) collective-permute-start(bf16[512,1280]{1,0:T(8,128)(2,1)} %near.1), channel_id=1, source_target_pairs={{0,6},{1,7},{2,0},{3,1},{4,2},{5,3},{6,4},{7,5},{8,14},{9,15},{10,... | collective-permute-start | bytes 3932168 | tf_op jit(solution)/shard_map/ppermute | solution.py:483
  74.8 9.4 %copy-start.6 = (s32[16,128]{1,0:T(8,128)S(1)}, s32[16,128]{1,0:T(8,128)}, u32[]{:S(2)}) copy-start(s32[16,128]{1,0:T(8,128)} %get-tuple-element.25.place) | copy-start | bytes 24580
  74.8 9.4 %copy-start.7 = (s32[10,1,128]{2,1,0:T(1,128)S(1)}, s32[10,1,128]{2,1,0:T(1,128)}, u32[]{:S(2)}) copy-start(s32[10,1,128]{2,1,0:T(1,128)} %mask.1) | copy-start | bytes 15364
  74.8 9.4 %copy-start.9 = (s32[1,128]{1,0:T(1,128)S(1)}, s32[1,128]{1,0:T(1,128)}, u32[]{:S(2)}) copy-start(s32[1,128]{1,0:T(1,128)} %labels.1) | copy-start | bytes 1540
  77.1 0.7 copy-start.3
  77.8 19.3 %all-to-all-start.2 = ((bf16[32,24,256]{2,1,0:T(8,128)(2,1)}), bf16[32,24,256]{2,1,0:T(8,128)(2,1)S(1)}, u32[]{:S(2)}, u32[]{:S(2)}) async-start(bf16[32,24,256]{2,1,0:T(8,128)(2,1)} %bitcast.18), calls=%async_computation.2 | async-start | bytes 786432 | tf_op jit(solution)/shard_map/all_to_all | solution.py:525
  84.2 1.3 %copy-start.2 = (bf16[512,1280]{1,0:T(8,128)(2,1)S(1)}, bf16[512,1280]{1,0:T(8,128)(2,1)}, u32[]{:S(2)}) copy-start(bf16[512,1280]{1,0:T(8,128)(2,1)} %near.1) | copy-start | bytes 3932164
  87.0 13.5 %collective-permute-start.3 = (bf16[2,784,128]{2,1,0:T(8,128)(2,1)S(1)}, bf16[2,784,128]{2,1,0:T(8,128)(2,1)}, u32[]{:S(2)}, u32[]{:S(2)}) collective-permute-start(bf16[2,784,128]{2,1,0:T(8,128)(2,1)S(1)} %get-tuple-element.27.refs_1_), channel_id=1, source_target_pairs={{0,1},{1,0},{2,3},{3,2},{4,5},{5,4},{6,7},{7,6},{8,9},{9,8},{10,11... | collective-permute-start | bytes 1204232 | tf_op jit(solution)/shard_map/ppermute | solution.py:524
  97.1 4.7 %collective-permute-start.2 = (bf16[768,256]{1,0:T(8,128)(2,1)S(1)}, bf16[768,256]{1,0:T(8,128)(2,1)S(1)}, u32[]{:S(2)}, u32[]{:S(2)}) collective-permute-start(bf16[768,256]{1,0:T(8,128)(2,1)S(1)} %bitcast.16), channel_id=1, source_target_pairs={{0,1},{1,0},{2,3},{3,2},{4,5},{5,4},{6,7},{7,6},{8,9},{9,8},{10,11... | collective-permute-start | bytes 1179656 | tf_op jit(solution)/shard_map/ppermute | solution.py:527
  106.0 1.3 %collective-permute-start.6 = (f32[8,128]{1,0:T(8,128)S(1)}, f32[8,128]{1,0:T(8,128)S(1)}, u32[]{:S(2)}, u32[]{:S(2)}) collective-permute-start(f32[8,128]{1,0:T(8,128)S(1)} %get-tuple-element.31), channel_id=1, source_target_pairs={{0,1},{1,0},{2,3},{3,2},{4,5},{5,4},{6,7},{7,6},{8,9},{9,8},{10,11... | collective-permute-start | bytes 12296 | tf_op jit(solution)/shard_map/ppermute | solution.py:529

commit v10 on v8

--- a/solution.py
+++ b/solution.py
@@ -512,7 +512,7 @@
         in_specs=[SMEM] + [VMEM] * 6,
         out_specs=(VMEM, VMEM),
         scratch_shapes=[pltpu.VMEM((FEAT * 80, 256), BF16)],
-        compiler_params=pltpu.CompilerParams(vmem_limit_bytes=24 * 2**20),
+        compiler_params=pltpu.CompilerParams(vmem_limit_bytes=51 * 2**20),
     )(side, own, means, mine, theirs, first_bias[None, :], chosen)
     picks, blocks[0] = call_pick(place, second_mask, labels, class_weight)
     picks_there = lax.ppermute(picks, "node", swap)

time: 108 us -> 109 us (level)
  Pallas kernels: 42 us -> 43.2 us
    pallas_call x1, Pallas kernels: 2.28 us -> 3.44 us  [body(): pl.pallas_call(hidden_kernel, out_shape=(jax.ShapeDtypeStruct((OWN, HIDDE...]
  transfers between devices with their start and end apart: 10 -> 10, of which waited for: 4 -> 4; matrix products, arithmetic and copies ran while one was open for 0% -> 0% of each run, Pallas kernels for 30% -> 31%
where the time goes in v10:
time: 109 us; the launch traced here: 108 us
  Pallas kernels  43.2 us (40%)
  starting transfers between devices  41.3 us (38%)
  waiting for transfers between devices  20.5 us (19%)
  local copies, waits for them, and re-layouts  2.22 us (2%)
    pallas_call x1, Pallas kernels, call_gather(): pl.pallas_call(gather_kernel, out_shape=jax.ShapeDtypeStruct((FEAT, 64, 1...  28.8 us
    all_to_all x1, starting transfers between devices, body(): own = lax.all_to_all(own, 'feat', 0, 0)  12.2 us
    all_to_all x1, waiting for transfers between devices, body(): means = lax.all_to_all(send, 'feat', 0, 0)  10.7 us
    all_to_all x1, starting transfers between devices, body(): means = lax.all_to_all(send, 'feat', 0, 0)  9.21 us
    all_to_all x1, waiting for transfers between devices, body(): rows = lax.all_to_all(rows.reshape(FEAT, UNION, HIDDEN), 'feat', 0, 0)  7.6 us
    all_to_all x1, starting transfers between devices, body(): rows = lax.all_to_all(rows.reshape(FEAT, UNION, HIDDEN), 'feat', 0, 0)  6.24 us
    pallas_call x1, Pallas kernels, call_prepare(): pl.pallas_call(prepare_kernel, out_shape=(jax.ShapeDtypeStruct((FEAT, 144...  5.06 us
    pallas_call x1, Pallas kernels, call_loss(): pl.pallas_call(loss_kernel, out_shape=[jax.ShapeDtypeStruct((8, TARGETS),...  4.53 us
  transfers between devices with their start and end apart: 10, of which 4 were waited for; matrix products, arithmetic and copies ran while one was open for 0% of the time, Pallas kernels for 31%

profile of v10, /device:TPU:1, one launch (start us, length us, event | category | flops | bytes accessed | tf_op | source)
XLA Modules:
  0.0 108.1 jit_solution(10272052424738999130)
XLA Ops:
  0.6 5.1 %shard_map.113 = (bf16[32,144,128]{2,1,0:T(8,128)(2,1)}, s32[16,128]{1,0:T(8,128)}, s32[528,128]{1,0:T(8,128)}, s32[48,128]{1,0:T(8,128)}) custom-call(s32[1]{0:T(128)} %bitcast.core, s32[10,1,128]{2,1,0:T(1,128)} %refs_0_.1, s32[1,128]{1,0:T(1,128)} %refs_1_.1, bf16[2,40,256]{2,1,0:T(8,128)(2,1)} %refs_2_.1, bf16[40,24576]{1,0:T(8,128)(2,1)} %bitcast.12, ...), custom_call_target="tpu_custom_call" | custom-call | flops 100000000 | bytes 10000000 | tf_op jit(solution)/shard_map/pallas_call | solution.py:373
  5.7 0.0 copy-start.1
  5.7 0.0 copy-start.5
  5.7 12.2 %all-to-all-start = ((bf16[32,144,128]{2,1,0:T(8,128)(2,1)}), bf16[32,144,128]{2,1,0:T(8,128)(2,1)S(1)}, u32[]{:S(2)}, u32[]{:S(2)}) async-start(bf16[32,144,128]{2,1,0:T(8,128)(2,1)} %get-tuple-element.19), calls=%async_computation | async-start | bytes 2359296 | tf_op jit(solution)/shard_map/all_to_all | solution.py:489
  17.9 1.3 %collective-permute-start = (bf16[512,1280]{1,0:T(8,128)(2,1)}, bf16[512,1280]{1,0:T(8,128)(2,1)}, u32[]{:S(2)}, u32[]{:S(2)}) collective-permute-start(bf16[512,1280]{1,0:T(8,128)(2,1)} %block.1), channel_id=1, source_target_pairs={{0,2},{1,3},{2,4},{3,5},{4,6},{5,7},{6,0},{7,1},{8,10},{9,11},{10,... | collective-permute-start | bytes 3932168 | tf_op jit(solution)/shard_map/ppermute | solution.py:477
  19.2 1.5 %collective-permute-start.1 = (bf16[512,1280]{1,0:T(8,128)(2,1)}, bf16[512,1280]{1,0:T(8,128)(2,1)}, u32[]{:S(2)}, u32[]{:S(2)}) collective-permute-start(bf16[512,1280]{1,0:T(8,128)(2,1)} %block.1), channel_id=1, source_target_pairs={{0,6},{1,7},{2,0},{3,1},{4,2},{5,3},{6,4},{7,5},{8,14},{9,15},{10,... | collective-permute-start | bytes 3932168 | tf_op jit(solution)/shard_map/ppermute | solution.py:477
  20.7 28.8 %shard_map.114 = bf16[32,64,128]{2,1,0:T(8,128)(2,1)S(1)} custom-call(s32[67584]{0:T(1024)S(1)} %bitcast.18, s32[48,128]{1,0:T(8,128)S(1)} %copy-done.5, bf16[40,24576]{1,0:T(8,128)(2,1)S(1)} %bitcast.13), custom_call_target="tpu_custom_call" | custom-call | tf_op jit(solution)/shard_map/pallas_call | solution.py:396
  49.6 0.8 copy-done.2
  50.4 0.0 all-to-all-done.own
  50.4 9.2 %all-to-all-start.1 = ((bf16[32,64,128]{2,1,0:T(8,128)(2,1)}), bf16[32,64,128]{2,1,0:T(8,128)(2,1)S(1)}, u32[]{:S(2)}, u32[]{:S(2)}) async-start(bf16[32,64,128]{2,1,0:T(8,128)(2,1)} %copy-done.2), calls=%async_computation.1 | async-start | bytes 1048576 | tf_op jit(solution)/shard_map/all_to_all | solution.py:494
  59.6 0.0 copy-start.8
  59.7 2.1 %collective-permute-start.2 = (bf16[2560,128]{1,0:T(8,128)(2,1)S(1)}, bf16[2560,128]{1,0:T(8,128)(2,1)S(1)}, u32[]{:S(2)}, u32[]{:S(2)}) collective-permute-start(bf16[2560,128]{1,0:T(8,128)(2,1)S(1)} %bitcast.14), channel_id=1, source_target_pairs={{0,1},{1,0},{2,3},{3,2},{4,5},{5,4},{6,7},{7,6},{8,9},{9,8},{10,11... | collective-permute-start | bytes 1966088 | tf_op jit(solution)/shard_map/ppermute | solution.py:493
  61.8 1.6 %collective-permute-start.5 = (bf16[512,1280]{1,0:T(8,128)(2,1)}, bf16[512,1280]{1,0:T(8,128)(2,1)}, u32[]{:S(2)}, u32[]{:S(2)}) collective-permute-start(bf16[512,1280]{1,0:T(8,128)(2,1)} %block.1), channel_id=1, source_target_pairs={{0,4},{1,5},{2,6},{3,7},{4,0},{5,1},{6,2},{7,3},{8,12},{9,13},{10,... | collective-permute-start | bytes 3932168 | tf_op jit(solution)/shard_map/ppermute | solution.py:477
  63.4 0.1 pad_add_fusion.spot
  63.5 0.3 shard_map.115.chosen
  63.8 0.0 collective-permute-done.refs_6_
  63.8 10.7 %all-to-all-done.1.means = bf16[32,64,128]{2,1,0:T(8,128)(2,1)S(1)} async-done(((bf16[32,64,128]{2,1,0:T(8,128)(2,1)}), bf16[32,64,128]{2,1,0:T(8,128)(2,1)S(1)}, u32[]{:S(2)}, u32[]{:S(2)}) %all-to-all-start.1) | async-done | bytes 524320 | tf_op jit(solution)/shard_map/all_to_all | solution.py:494
  74.5 0.0 copy-start.7
  74.5 0.0 copy-start.9
  74.6 3.4 %shard_map.116 = (bf16[192,256]{1,0:T(8,128)(2,1)}, bf16[768,256]{1,0:T(8,128)(2,1)}) custom-call(s32[2]{0:T(128)S(1)} %pad_add_fusion.spot, bf16[32,144,128]{2,1,0:T(8,128)(2,1)} %copy-done, bf16[32,64,128]{2,1,0:T(8,128)(2,1)S(1)} %all-to-all-done.1.means, bf16[2560,128]{1,0:T(8,128)(2,1)S(1)} %bitcast.15, ...), custom_call_target="tpu_custom_call" | custom-call | tf_op jit(solution)/shard_map/pallas_call | solution.py:506
  78.0 6.2 %all-to-all-start.2 = ((bf16[32,24,256]{2,1,0:T(8,128)(2,1)}), bf16[32,24,256]{2,1,0:T(8,128)(2,1)S(1)}, u32[]{:S(2)}, u32[]{:S(2)}) async-start(bf16[32,24,256]{2,1,0:T(8,128)(2,1)} %bitcast.10), calls=%async_computation.2 | async-start | bytes 786432 | tf_op jit(solution)/shard_map/all_to_all | solution.py:519
  84.3 0.0 copy-start.3
  84.3 1.3 %copy-done.3 = bf16[512,1280]{1,0:T(8,128)(2,1)S(1)} copy-done((bf16[512,1280]{1,0:T(8,128)(2,1)S(1)}, bf16[512,1280]{1,0:T(8,128)(2,1)}, u32[]{:S(2)}) %copy-start.3) | copy-done | bytes 1310744
  85.6 0.5 shard_map.117
  86.1 2.4 %collective-permute-start.4 = (bf16[2,784,128]{2,1,0:T(8,128)(2,1)S(1)}, bf16[2,784,128]{2,1,0:T(8,128)(2,1)S(1)}, u32[]{:S(2)}, u32[]{:S(2)}) collective-permute-start(bf16[2,784,128]{2,1,0:T(8,128)(2,1)S(1)} %get-tuple-element.26.refs_1_), channel_id=1, source_target_pairs={{0,1},{1,0},{2,3},{3,2},{4,5},{5,4},{6,7},{7,6},{8,9},{9,8},{10,11... | collective-permute-start | bytes 1204232 | tf_op jit(solution)/shard_map/ppermute | solution.py:518
  88.6 7.6 %all-to-all-done.2 = bf16[32,24,256]{2,1,0:T(8,128)(2,1)S(1)} async-done(((bf16[32,24,256]{2,1,0:T(8,128)(2,1)}), bf16[32,24,256]{2,1,0:T(8,128)(2,1)S(1)}, u32[]{:S(2)}, u32[]{:S(2)}) %all-to-all-start.2) | async-done | bytes 393248 | tf_op jit(solution)/shard_map/all_to_all | solution.py:519
  96.2 4.3 %collective-permute-start.3 = (bf16[768,256]{1,0:T(8,128)(2,1)S(1)}, bf16[768,256]{1,0:T(8,128)(2,1)S(1)}, u32[]{:S(2)}, u32[]{:S(2)}) collective-permute-start(bf16[768,256]{1,0:T(8,128)(2,1)S(1)} %bitcast.16), channel_id=1, source_target_pairs={{0,1},{1,0},{2,3},{3,2},{4,5},{5,4},{6,7},{7,6},{8,9},{9,8},{10,11... | collective-permute-start | bytes 1179656 | tf_op jit(solution)/shard_map/ppermute | solution.py:521
  100.5 1.3 %collective-permute-done.3.refs_2_ = bf16[768,256]{1,0:T(8,128)(2,1)S(1)} collective-permute-done((bf16[768,256]{1,0:T(8,128)(2,1)S(1)}, bf16[768,256]{1,0:T(8,128)(2,1)S(1)}, u32[]{:S(2)}, u32[]{:S(2)}) %collective-permute-start.3) | collective-permute-done | bytes 393248 | tf_op jit(solution)/shard_map/ppermute | solution.py:521
  101.8 4.5 %shard_map.118 = (f32[8,128]{1,0:T(8,128)S(1)}, f32[8,128]{1,0:T(8,128)S(1)}) custom-call(s32[1]{0:T(128)} %bitcast.9.spot, bf16[768,256]{1,0:T(8,128)(2,1)S(1)} %bitcast.17, bf16[2,784,128]{2,1,0:T(8,128)(2,1)S(1)} %get-tuple-element.26.refs_1_, bf16[768,256]{1,0:T(8,128)(2,1)S(1)} %collective-permute-done.3.refs_2_, ...), custom_call_target="tpu_custom_call" | custom-call | tf_op jit(solution)/shard_map/pallas_call | solution.py:429
  106.4 0.4 collective-permute-start.6
  106.8 0.8 collective-permute-done.6.there
  107.6 0.5 shard_map.119
  (17 shorter events, 0.1 us)
Async XLA Ops:
  5.7 15.0 %copy-start.1 = (bf16[40,1,24576]{2,0,1:T(8,128)(2,1)S(1)}, bf16[40,1,24576]{2,0,1:T(8,128)(2,1)}, u32[]{:S(2)}) copy-start(bf16[40,1,24576]{2,0,1:T(8,128)(2,1)} %param.10) | copy-start | bytes 5898244
  5.7 15.0 %copy-start.4 = (s32[528,128]{1,0:T(8,128)S(1)}, s32[528,128]{1,0:T(8,128)}, u32[]{:S(2)}) copy-start(s32[528,128]{1,0:T(8,128)} %get-tuple-element.17) | copy-start | bytes 811012
  5.7 15.0 %copy-start.5 = (s32[48,128]{1,0:T(8,128)S(1)}, s32[48,128]{1,0:T(8,128)}, u32[]{:S(2)}) copy-start(s32[48,128]{1,0:T(8,128)} %get-tuple-element.18.ranks) | copy-start | bytes 73732
  5.7 44.6 %all-to-all-start = ((bf16[32,144,128]{2,1,0:T(8,128)(2,1)}), bf16[32,144,128]{2,1,0:T(8,128)(2,1)S(1)}, u32[]{:S(2)}, u32[]{:S(2)}) async-start(bf16[32,144,128]{2,1,0:T(8,128)(2,1)} %get-tuple-element.19), calls=%async_computation | async-start | bytes 2359296 | tf_op jit(solution)/shard_map/all_to_all | solution.py:489
  17.9 45.9 %collective-permute-start = (bf16[512,1280]{1,0:T(8,128)(2,1)}, bf16[512,1280]{1,0:T(8,128)(2,1)}, u32[]{:S(2)}, u32[]{:S(2)}) collective-permute-start(bf16[512,1280]{1,0:T(8,128)(2,1)} %block.1), channel_id=1, source_target_pairs={{0,2},{1,3},{2,4},{3,5},{4,6},{5,7},{6,0},{7,1},{8,10},{9,11},{10,... | collective-permute-start | bytes 3932168 | tf_op jit(solution)/shard_map/ppermute | solution.py:477
  19.2 44.6 %collective-permute-start.1 = (bf16[512,1280]{1,0:T(8,128)(2,1)}, bf16[512,1280]{1,0:T(8,128)(2,1)}, u32[]{:S(2)}, u32[]{:S(2)}) collective-permute-start(bf16[512,1280]{1,0:T(8,128)(2,1)} %block.1), channel_id=1, source_target_pairs={{0,6},{1,7},{2,0},{3,1},{4,2},{5,3},{6,4},{7,5},{8,14},{9,15},{10,... | collective-permute-start | bytes 3932168 | tf_op jit(solution)/shard_map/ppermute | solution.py:477
  49.5 0.8 copy-start.2
  50.4 13.4 %copy-start = (bf16[32,144,128]{2,1,0:T(8,128)(2,1)}, bf16[32,144,128]{2,1,0:T(8,128)(2,1)S(1)}, u32[]{:S(2)}) copy-start(bf16[32,144,128]{2,1,0:T(8,128)(2,1)S(1)} %all-to-all-done.own) | copy-start | bytes 3538948
  50.4 24.1 %all-to-all-start.1 = ((bf16[32,64,128]{2,1,0:T(8,128)(2,1)}), bf16[32,64,128]{2,1,0:T(8,128)(2,1)S(1)}, u32[]{:S(2)}, u32[]{:S(2)}) async-start(bf16[32,64,128]{2,1,0:T(8,128)(2,1)} %copy-done.2), calls=%async_computation.1 | async-start | bytes 1048576 | tf_op jit(solution)/shard_map/all_to_all | solution.py:494
  59.6 14.9 %copy-start.8 = (f32[256]{0:T(256)S(1)}, f32[256]{0:T(256)}, u32[]{:S(2)}) copy-start(f32[256]{0:T(256)} %param.18) | copy-start | bytes 3076
  59.7 14.9 %collective-permute-start.2 = (bf16[2560,128]{1,0:T(8,128)(2,1)S(1)}, bf16[2560,128]{1,0:T(8,128)(2,1)S(1)}, u32[]{:S(2)}, u32[]{:S(2)}) collective-permute-start(bf16[2560,128]{1,0:T(8,128)(2,1)S(1)} %bitcast.14), channel_id=1, source_target_pairs={{0,1},{1,0},{2,3},{3,2},{4,5},{5,4},{6,7},{7,6},{8,9},{9,8},{10,11... | collective-permute-start | bytes 1966088 | tf_op jit(solution)/shard_map/ppermute | solution.py:493
  61.8 38.7 %collective-permute-start.5 = (bf16[512,1280]{1,0:T(8,128)(2,1)}, bf16[512,1280]{1,0:T(8,128)(2,1)}, u32[]{:S(2)}, u32[]{:S(2)}) collective-permute-start(bf16[512,1280]{1,0:T(8,128)(2,1)} %block.1), channel_id=1, source_target_pairs={{0,4},{1,5},{2,6},{3,7},{4,0},{5,1},{6,2},{7,3},{8,12},{9,13},{10,... | collective-permute-start | bytes 3932168 | tf_op jit(solution)/shard_map/ppermute | solution.py:477
  74.5 9.7 %copy-start.6 = (s32[16,128]{1,0:T(8,128)S(1)}, s32[16,128]{1,0:T(8,128)}, u32[]{:S(2)}) copy-start(s32[16,128]{1,0:T(8,128)} %get-tuple-element.25.place) | copy-start | bytes 24580
  74.5 9.7 %copy-start.7 = (s32[10,1,128]{2,1,0:T(1,128)S(1)}, s32[10,1,128]{2,1,0:T(1,128)}, u32[]{:S(2)}) copy-start(s32[10,1,128]{2,1,0:T(1,128)} %mask.1) | copy-start | bytes 15364
  74.5 9.7 %copy-start.9 = (s32[1,128]{1,0:T(1,128)S(1)}, s32[1,128]{1,0:T(1,128)}, u32[]{:S(2)}) copy-start(s32[1,128]{1,0:T(1,128)} %labels.1) | copy-start | bytes 1540
  78.0 18.2 %all-to-all-start.2 = ((bf16[32,24,256]{2,1,0:T(8,128)(2,1)}), bf16[32,24,256]{2,1,0:T(8,128)(2,1)S(1)}, u32[]{:S(2)}, u32[]{:S(2)}) async-start(bf16[32,24,256]{2,1,0:T(8,128)(2,1)} %bitcast.10), calls=%async_computation.2 | async-start | bytes 786432 | tf_op jit(solution)/shard_map/all_to_all | solution.py:519
  84.3 1.3 %copy-start.3 = (bf16[512,1280]{1,0:T(8,128)(2,1)S(1)}, bf16[512,1280]{1,0:T(8,128)(2,1)}, u32[]{:S(2)}) copy-start(bf16[512,1280]{1,0:T(8,128)(2,1)} %block.1) | copy-start | bytes 3932164
  86.1 14.3 %collective-permute-start.4 = (bf16[2,784,128]{2,1,0:T(8,128)(2,1)S(1)}, bf16[2,784,128]{2,1,0:T(8,128)(2,1)S(1)}, u32[]{:S(2)}, u32[]{:S(2)}) collective-permute-start(bf16[2,784,128]{2,1,0:T(8,128)(2,1)S(1)} %get-tuple-element.26.refs_1_), channel_id=1, source_target_pairs={{0,1},{1,0},{2,3},{3,2},{4,5},{5,4},{6,7},{7,6},{8,9},{9,8},{10,11... | collective-permute-start | bytes 1204232 | tf_op jit(solution)/shard_map/ppermute | solution.py:518
  96.2 5.6 %collective-permute-start.3 = (bf16[768,256]{1,0:T(8,128)(2,1)S(1)}, bf16[768,256]{1,0:T(8,128)(2,1)S(1)}, u32[]{:S(2)}, u32[]{:S(2)}) collective-permute-start(bf16[768,256]{1,0:T(8,128)(2,1)S(1)} %bitcast.16), channel_id=1, source_target_pairs={{0,1},{1,0},{2,3},{3,2},{4,5},{5,4},{6,7},{7,6},{8,9},{9,8},{10,11... | collective-permute-start | bytes 1179656 | tf_op jit(solution)/shard_map/ppermute | solution.py:521
  106.4 1.3 %collective-permute-start.6 = (f32[8,128]{1,0:T(8,128)S(1)}, f32[8,128]{1,0:T(8,128)S(1)}, u32[]{:S(2)}, u32[]{:S(2)}) collective-permute-start(f32[8,128]{1,0:T(8,128)S(1)} %get-tuple-element.31), channel_id=1, source_target_pairs={{0,1},{1,0},{2,3},{3,2},{4,5},{5,4},{6,7},{7,6},{8,9},{9,8},{10,11... | collective-permute-start | bytes 12296 | tf_op jit(solution)/shard_map/ppermute | solution.py:523
